TPU v7x, 32 devices: a whole 2x2x4 slice. The times are simulated.
32 devices in a mesh: mem: 4 (over z), grid: 8 (over y, x, core).
Axes of the slice: x: 2, y: 2, z: 4, core: 2. Of those that a mesh axis runs over, the one named last changes fastest.
Arguments:
- state: float32 [80, 131072], P('mem', 'grid'), may hold values from -6 to 6
- obs_tile: int32 [4], replicated, may hold values from 0 to 1023
- obs_offset: int32 [4, 256], replicated, may hold values from 0 to 127
- obs_value: float32 [4, 256], replicated, may hold values from -8 to 8
- obs_error: float32 [4, 256], replicated, may hold values from 0.5 to 4
- loc_mask: int32 [4, 1024], replicated, may hold values 0 or 1
- block_order: int32 [4], replicated, may hold values from 0 to 3, each once
Outputs:
- posterior: float32 [80, 131072], P('mem', 'grid')
Inputs may be any that keep to these rules, and one draw needn't show every extreme that they name: `block_order`: a permutation of 0 to 3.
All inputs are finite; a program needn't handle non-finite values.
Results may differ from a plain program's by a relative error of at most 0.00024.
Values sent between devices are 32-bit elements; how exact they have to be, the bound alone decides.
No kernel may reach another device: no remote copies, remote signals or barrier semaphores. Data moves between devices by JAX's collectives and lax.ppermute only.
A program may use at most 64 MiB of HBM per device.

v0:
```python
import jax
import jax.numpy as jnp
from jax import lax
from jax.sharding import PartitionSpec as P

BLOCKS = 4
TILE = 128


def from_root(value, axis, root):
    mine = lax.axis_index(axis) == root
    return lax.psum(jnp.where(mine, value, jnp.zeros_like(value)), axis)


def on_device(state, obs_tile, obs_offset, obs_value, obs_error, loc_mask, block_order):
    highest = lax.Precision.HIGHEST
    n_mem = lax.axis_size("mem")
    n_grid = lax.axis_size("grid")
    mem_idx = lax.axis_index("mem")
    grid_idx = lax.axis_index("grid")
    my_rank = mem_idx * n_grid + grid_idx
    mem_loc = state.shape[0]
    grid_width = state.shape[1]
    members = mem_loc * n_mem
    piece = grid_width // (n_mem * n_grid)
    moved = lax.all_to_all(state, ("mem", "grid"), split_axis=1, concat_axis=0, tiled=True)
    field = moved.reshape(n_mem, n_grid, mem_loc, piece)
    n_part = field.shape[1]
    for k in range(BLOCKS):
        b = block_order[k]
        base = obs_tile[b] * TILE
        owner_grid = base // grid_width
        rest = base % grid_width
        root = rest // piece
        masks = loc_mask[b].reshape(n_grid, n_mem * n_grid, piece // TILE)
        local_mask = lax.dynamic_slice_in_dim(masks, my_rank, 1, 1)[:, 0, :]
        col = rest % piece
        zero = jnp.zeros((), jnp.int32)
        slab = lax.dynamic_slice(field, (zero, owner_grid, zero, col), (n_mem, 1, mem_loc, TILE))
        slab = slab.reshape(members, TILE)
        local_prior = jnp.take(slab, obs_offset[b], axis=1)
        prior = from_root(local_prior, ("mem", "grid"), root)
        ybar = jnp.mean(prior, axis=0)
        dev = prior - ybar
        var = jnp.sum(dev * dev, axis=0) / (members - 1.0)
        error = obs_error[b]
        dy_inc = (
            var / (var + error) * (obs_value[b] - ybar)
            + (jnp.sqrt(error / (var + error)) - 1.0) * dev
        )
        weighted = dev / ((members - 1.0) * (var + 1e-05))
        weighted = weighted.reshape(n_mem, mem_loc, -1)
        dy_inc = dy_inc.reshape(n_mem, mem_loc, -1)
        anom = field - jnp.mean(field, axis=(0, 2), keepdims=True)
        coef = jnp.einsum("agmp,amo->gpo", anom, weighted, precision=highest)
        incr = jnp.einsum("gpo,amo->agmp", coef, dy_inc, precision=highest)
        spread = jnp.broadcast_to(
            local_mask.astype(jnp.float32)[:, :, None], (n_part, piece // TILE, TILE)
        ).reshape(n_part, piece)
        field = field + incr * spread[None, :, None, :]
    flat = field.reshape(n_mem * n_grid * mem_loc, piece)
    return lax.all_to_all(flat, ("mem", "grid"), split_axis=0, concat_axis=1, tiled=True)


def solution(mesh):
    placed = (P("mem", "grid"), P(), P(), P(), P(), P(), P())
    return jax.shard_map(
        on_device, mesh=mesh, in_specs=placed, out_specs=P("mem", "grid"), check_vma=False
    )
```

profile of v0, /device:TPU:0, one launch (start us, length us, event | category | flops | bytes accessed | tf_op | source)
XLA Modules:
  0.0 644.2 jit_solution(10575613686614636627)
XLA Ops:
  6.5 2.3 copy.76
  9.0 1.9 copy.50
  10.9 7.3 %all-to-all-start = ((f32[20,32,512]{2,0,1:T(8,128)}), f32[20,32,512]{2,0,1:T(8,128)S(1)}, u32[]{:S(2)}, u32[]{:S(2)}) async-start(f32[20,32,512]{2,0,1:T(8,128)} %copy.50), calls=%async_computation | async-start | bytes 3145728 | tf_op jit(solution)/shard_map/all_to_all | solution.py:26
  31.4 24.5 %all-to-all-done = f32[20,32,512]{2,0,1:T(8,128)S(1)} async-done(((f32[20,32,512]{2,0,1:T(8,128)}), f32[20,32,512]{2,0,1:T(8,128)S(1)}, u32[]{:S(2)}, u32[]{:S(2)}) %all-to-all-start) | async-done | bytes 1310752 | tf_op jit(solution)/shard_map/all_to_all | solution.py:26
  58.2 118.1 %all-reduce.5.cloned.1.call-done = f32[80,256]{1,0:T(8,128)} async-done(((f32[80,256]{1,0:T(8,128)}), f32[80,256]{1,0:T(8,128)}) %all-reduce.5.cloned.1.call-update) | async-done | bytes 81936 | tf_op jit(solution)/shard_map/psum | solution.py:12
  176.4 0.9 reduce_sum.115
  177.3 0.9 multiply_reduce_fusion.3
  178.3 0.9 multiply_add_fusion.3
  179.2 3.6 fusion.15
  182.9 4.2 fusion.32
  189.0 121.3 %all-reduce.7.cloned.1.call-done = f32[80,256]{1,0:T(8,128)} async-done(((f32[80,256]{1,0:T(8,128)}), f32[80,256]{1,0:T(8,128)}) %all-reduce.7.cloned.1.call-update) | async-done | bytes 81936 | tf_op jit(solution)/shard_map/psum | solution.py:12
  310.2 0.9 reduce_sum.120
  311.2 0.9 multiply_reduce_fusion.2
  312.1 0.9 multiply_add_fusion.2
  313.1 3.6 fusion.4
  316.7 4.2 fusion.33
  320.8 1.1 copy-done
  323.9 121.3 %all-reduce.9.cloned.1.call-done = f32[80,256]{1,0:T(8,128)} async-done(((f32[80,256]{1,0:T(8,128)}), f32[80,256]{1,0:T(8,128)}) %all-reduce.9.cloned.1.call-update) | async-done | bytes 81936 | tf_op jit(solution)/shard_map/psum | solution.py:12
  445.2 0.9 reduce_sum.123
  446.1 0.9 multiply_reduce_fusion.1
  447.1 0.9 multiply_add_fusion.1
  448.0 3.6 fusion.2
  451.6 4.2 fusion.34
  457.5 121.5 %all-reduce.11.cloned.1.call-done = f32[80,256]{1,0:T(8,128)} async-done(((f32[80,256]{1,0:T(8,128)}), f32[80,256]{1,0:T(8,128)}) %all-reduce.11.cloned.1.call-update) | async-done | bytes 81936 | tf_op jit(solution)/shard_map/psum | solution.py:12
  579.0 0.9 reduce_sum.126
  579.9 0.9 multiply_reduce_fusion
  580.9 0.9 multiply_add_fusion
  581.8 3.6 fusion
  585.4 4.4 bitcast_add_fusion
  589.8 44.4 %all_to_all.35 = f32[32,20,512]{2,1,0:T(8,128)S(1)} all-to-all(f32[32,20,512]{2,1,0:T(8,128)S(1)} %bitcast.119), channel_id=1, replica_groups=mesh['mem'=4,'grid'=8] {'mem','grid'}, dimensions={0} | all-to-all | bytes 2621440 | tf_op jit(solution)/shard_map/all_to_all | solution.py:62
  634.2 0.8 copy.63
  635.2 2.1 copy.77
  (109 shorter events, 10.9 us)
Async XLA Ops:
  10.9 7.4 %copy-start.4 = (s32[4]{0:T(128)S(1)}, s32[4]{0:T(128)}, u32[]{:S(2)}) copy-start(s32[4]{0:T(128)} %param.15) | copy-start | bytes 52
  10.9 15.6 %copy-start.3 = (s32[4]{0:T(128)S(1)}, s32[4]{0:T(128)}, u32[]{:S(2)}) copy-start(s32[4]{0:T(128)} %param.10) | copy-start | bytes 52
  10.9 19.0 %copy-start.5 = (s32[4,256]{1,0:T(4,128)S(1)}, s32[4,256]{1,0:T(4,128)}, u32[]{:S(2)}) copy-start(s32[4,256]{1,0:T(4,128)} %param.11) | copy-start | bytes 12292
  10.9 19.1 %copy-start.2 = (s32[4,1024]{1,0:T(4,128)S(1)}, s32[4,1024]{1,0:T(4,128)}, u32[]{:S(2)}) copy-start(s32[4,1024]{1,0:T(4,128)} %param.14) | copy-start | bytes 49156
  10.9 45.0 %all-to-all-start = ((f32[20,32,512]{2,0,1:T(8,128)}), f32[20,32,512]{2,0,1:T(8,128)S(1)}, u32[]{:S(2)}, u32[]{:S(2)}) async-start(f32[20,32,512]{2,0,1:T(8,128)} %copy.50), calls=%async_computation | async-start | bytes 3145728 | tf_op jit(solution)/shard_map/all_to_all | solution.py:26
  18.2 158.2 %all-reduce.5.cloned.1.call-start = ((), (), s32[]{:S(2)}) async-start(), calls=%async_computation.2 | async-start | bytes 163840 | tf_op jit(solution)/shard_map/psum | solution.py:12
  57.7 252.6 %all-reduce.7.cloned.1.call-start = ((), (), s32[]{:S(2)}) async-start(), calls=%async_computation.3 | async-start | bytes 163840 | tf_op jit(solution)/shard_map/psum | solution.py:12
  58.0 120.2 %copy-start.6 = (f32[4,256]{1,0:T(4,128)S(1)}, f32[4,256]{1,0:T(4,128)}, u32[]{:S(2)}) copy-start(f32[4,256]{1,0:T(4,128)} %param.12) | copy-start | bytes 12292
  58.0 120.2 %copy-start.7 = (f32[4,256]{1,0:T(4,128)S(1)}, f32[4,256]{1,0:T(4,128)}, u32[]{:S(2)}) copy-start(f32[4,256]{1,0:T(4,128)} %param.13) | copy-start | bytes 12292
  188.7 256.5 %all-reduce.9.cloned.1.call-start = ((), (), s32[]{:S(2)}) async-start(), calls=%async_computation.4 | async-start | bytes 163840 | tf_op jit(solution)/shard_map/psum | solution.py:12
  320.8 1.1 copy-start
  322.1 125.9 %copy-start.1 = (f32[4,8,20,512]{3,2,1,0:T(8,128)S(1)}, f32[4,8,20,512]{3,2,1,0:T(8,128)}, u32[]{:S(2)}) copy-start(f32[4,8,20,512]{3,2,1,0:T(8,128)} %copy-done) | copy-start | bytes 3932164
  323.7 255.3 %all-reduce.11.cloned.1.call-start = ((), (), s32[]{:S(2)}) async-start(), calls=%async_computation.5 | async-start | bytes 163840 | tf_op jit(solution)/shard_map/psum | solution.py:12
Sparse Core Ops, SparseCore 0:
  57.8 118.5 all-reduce.4
  188.8 121.3 all-reduce.6
  323.8 121.3 all-reduce.8
  457.6 121.3 all-reduce.10
where the time goes:
time: 653 us; the launch traced here: 644 us
  waiting for transfers between devices  507 us (78%)
  blocking collectives  44.4 us (7%)
  matrix products  31.3 us (5%)
  between operations  24.5 us (4%)
  local copies, waits for them, and re-layouts  15.2 us (2%)
  other arithmetic  14.2 us (2%)
  starting transfers between devices  7.85 us (1%)
    psum x4, waiting for transfers between devices, from_root(): return lax.psum(jnp.where(mine, value, jnp.zeros_like(value)), axis)  482 us
    all_to_all x1, blocking collectives, on_device(): lax.all_to_all(flat, ('mem', 'grid'), split_axis=0, concat_axis=1, tiled=...  44.4 us
    all_to_all x1, waiting for transfers between devices, on_device(): lax.all_to_all(state, ('mem', 'grid'), split_axis=1, concat_axis=0, tiled...  24.5 us
    dot_general x4, matrix products, on_device(): incr = jnp.einsum('gpo,amo->agmp', coef, dy_inc, precision=highest)  16.9 us
    dot_general x4, matrix products, on_device(): coef = jnp.einsum('agmp,amo->gpo', anom, weighted, precision=highest)  14.4 us
  transfers between devices with their start and end apart: 5, of which 5 were waited for; matrix products, arithmetic and copies ran while one was open for 0% of the time, Pallas kernels for 0%

commit v1 on v0

v1 whole, which is shorter than its diff:
```python
import functools
import math

import jax
import jax.numpy as jnp
from jax import lax
from jax.experimental import pallas as pl
from jax.experimental.pallas import tpu as pltpu
from jax.sharding import PartitionSpec as P

BLOCKS = 4
TILE = 128
HIGHEST = lax.Precision.HIGHEST
VMEM = pl.BlockSpec(memory_space=pltpu.VMEM)
SMEM = pl.BlockSpec(memory_space=pltpu.SMEM)


def pack_kernel(n_mem, parts, start_ref, x_ref, *outs):
    mem_loc = x_ref.shape[0]
    for d in range(n_mem):
        piece = outs[d]
        width = piece.shape[1]
        for p in range(parts):
            col = pl.multiple_of(start_ref[d] + p * width, TILE)
            piece[p * mem_loc : (p + 1) * mem_loc, :] = x_ref[:, pl.ds(col, width)]
    seen = outs[n_mem]
    for k in range(BLOCKS):
        col = pl.multiple_of(start_ref[n_mem + k], TILE)
        seen[k * mem_loc : (k + 1) * mem_loc, :] = x_ref[:, pl.ds(col, TILE)]


def pick_kernel(n_grid, shift_ref, *refs):
    out = refs[n_grid]
    mem_loc = out.shape[0] // BLOCKS
    for k in range(BLOCKS):
        rows = slice(k * mem_loc, (k + 1) * mem_loc)
        value = refs[0][rows, :]
        for d in range(1, n_grid):
            value = jnp.where(shift_ref[k] == d, refs[d][rows, :], value)
        out[rows, :] = value


def chain_kernel(n_mem, code_ref, offset_ref, value_ref, error_ref, *refs):
    pieces, out, slab = refs[:n_mem], refs[n_mem], refs[n_mem + 1]
    mem_loc = pieces[0].shape[0] // BLOCKS
    members = mem_loc * n_mem
    obs = offset_ref.shape[0]
    for d in range(n_mem):
        for k in range(BLOCKS):
            slab[k, d * mem_loc : (d + 1) * mem_loc, :] = pieces[d][k * mem_loc : (k + 1) * mem_loc, :]
    row = lax.broadcasted_iota(jnp.int32, (members, TILE), 0)
    lane = lax.broadcasted_iota(jnp.int32, (members, TILE), 1)
    out[:, 0:TILE] = jnp.where(row == lane, 1.0, 0.0)
    place = lax.broadcasted_iota(jnp.int32, (obs, TILE), 1)
    for k in range(BLOCKS):
        x = slab[k]
        ybar = jnp.sum(x, axis=0, keepdims=True) / members
        dev = x - ybar
        var = jnp.sum(dev * dev, axis=0, keepdims=True) / (members - 1.0)
        hit = offset_ref[:, k : k + 1] == place
        error = error_ref[:, k : k + 1]
        total = var + error
        shrink = jnp.where(hit, jnp.sqrt(error / total) - 1.0, 0.0)
        shift = jnp.where(hit, var / total * (value_ref[:, k : k + 1] - ybar), 0.0)
        scale = 1.0 / ((members - 1.0) * (var + 1e-05))
        shrink = jnp.sum(shrink, axis=0, keepdims=True) * scale
        shift = jnp.sum(shift, axis=0, keepdims=True) * scale
        centred = dev - jnp.sum(dev, axis=0, keepdims=True) / members
        gain = lax.dot_general(
            dev * shrink + shift,
            centred,
            (((1,), (1,)), ((), ())),
            precision=HIGHEST,
            preferred_element_type=jnp.float32,
        )
        for j in range(k + 1, BLOCKS):
            old = slab[j]
            new = old + jnp.dot(gain, old, precision=HIGHEST, preferred_element_type=jnp.float32)
            slab[j] = jnp.where(((code_ref[j] >> k) & 1) == 1, new, old)
        span = TILE << k
        so_far = out[:, 0:span]
        out[:, span : 2 * span] = so_far + jnp.dot(
            gain, so_far, precision=HIGHEST, preferred_element_type=jnp.float32
        )


def apply_kernel(n_mem, parts, code_ref, t_ref, *refs):
    pieces, outs = refs[:n_mem], refs[n_mem : 2 * n_mem]
    mem_loc = pieces[0].shape[0] // parts
    members = mem_loc * n_mem
    tiles = pieces[0].shape[1] // TILE
    for p in range(parts):
        rows = slice(p * mem_loc, (p + 1) * mem_loc)
        for t in range(tiles):
            cols = slice(t * TILE, (t + 1) * TILE)
            x = jnp.concatenate([piece[rows, cols] for piece in pieces], axis=0)
            first = pl.multiple_of(code_ref[p * tiles + t] * TILE, TILE)
            matrix = t_ref[:, pl.ds(first, TILE)][:, 0:members]
            y = jnp.dot(matrix, x, precision=HIGHEST, preferred_element_type=jnp.float32)
            for d in range(n_mem):
                outs[d][rows, cols] = y[d * mem_loc : (d + 1) * mem_loc, :]


def unpack_kernel(n_mem, parts, start_ref, *refs):
    out = refs[n_mem]
    mem_loc = out.shape[0]
    for d in range(n_mem):
        width = refs[d].shape[1]
        for p in range(parts):
            col = pl.multiple_of(start_ref[d] + p * width, TILE)
            out[:, pl.ds(col, width)] = refs[d][p * mem_loc : (p + 1) * mem_loc, :]


def on_device(state, obs_tile, obs_offset, obs_value, obs_error, loc_mask, block_order):
    f32 = jnp.float32
    n_mem = lax.axis_size("mem")
    n_grid = lax.axis_size("grid")
    mem_idx = lax.axis_index("mem")
    grid_idx = lax.axis_index("grid")
    mem_loc, grid_width = state.shape
    members = mem_loc * n_mem
    quarter = grid_width // n_mem
    parts = 8 // math.gcd(mem_loc, 8)
    piece = jax.ShapeDtypeStruct((parts * mem_loc, quarter // parts), f32)
    seen = jax.ShapeDtypeStruct((BLOCKS * mem_loc, TILE), f32)

    tile = obs_tile[block_order]
    tiles_here = grid_width // TILE
    masks = loc_mask[block_order]
    code = jnp.sum(masks << jnp.arange(BLOCKS, dtype=jnp.int32)[:, None], axis=0)
    code_here = lax.dynamic_slice_in_dim(
        code, grid_idx * tiles_here + mem_idx * (quarter // TILE), quarter // TILE
    )
    owner = tile // tiles_here
    starts = (mem_idx + jnp.arange(n_mem, dtype=jnp.int32)) % n_mem * quarter
    starts = jnp.concatenate([starts, tile % tiles_here * TILE])

    packed = pl.pallas_call(
        functools.partial(pack_kernel, n_mem, parts),
        out_shape=[piece] * n_mem + [seen],
        in_specs=[SMEM, VMEM],
        out_specs=[VMEM] * (n_mem + 1),
        name="pack",
    )(starts, state)
    own, mine = packed[0], packed[n_mem]

    def send(value, axis, size, by):
        return lax.ppermute(value, axis, [(j, (j + by) % size) for j in range(size)])

    candidates = [mine] + [send(mine, "grid", n_grid, d) for d in range(1, n_grid)]
    arrived = [own] + [send(packed[d], "mem", n_mem, d) for d in range(1, n_mem)]
    picked = pl.pallas_call(
        functools.partial(pick_kernel, n_grid),
        out_shape=seen,
        in_specs=[SMEM] + [VMEM] * n_grid,
        out_specs=VMEM,
        name="pick",
    )((grid_idx - owner) % n_grid, *candidates)
    slabs = [picked] + [send(picked, "mem", n_mem, d) for d in range(1, n_mem)]
    matrices = pl.pallas_call(
        functools.partial(chain_kernel, n_mem),
        out_shape=jax.ShapeDtypeStruct((members, TILE << BLOCKS), f32),
        in_specs=[SMEM] + [VMEM] * (3 + n_mem),
        out_specs=VMEM,
        scratch_shapes=[pltpu.VMEM((BLOCKS, members, TILE), f32)],
        name="chain",
    )(code[tile], obs_offset[block_order].T, obs_value[block_order].T, obs_error[block_order].T, *slabs)
    updated = pl.pallas_call(
        functools.partial(apply_kernel, n_mem, parts),
        out_shape=[piece] * n_mem,
        in_specs=[SMEM] + [VMEM] * (1 + n_mem),
        out_specs=[VMEM] * n_mem,
        name="apply",
    )(code_here, matrices, *arrived)
    back = [updated[0]] + [send(updated[d], "mem", n_mem, -d) for d in range(1, n_mem)]
    return pl.pallas_call(
        functools.partial(unpack_kernel, n_mem, parts),
        out_shape=jax.ShapeDtypeStruct(state.shape, f32),
        in_specs=[SMEM] + [VMEM] * n_mem,
        out_specs=VMEM,
        name="unpack",
    )(starts, *back)


def solution(mesh):
    placed = (P("mem", "grid"), P(), P(), P(), P(), P(), P())
    return jax.shard_map(
        on_device, mesh=mesh, in_specs=placed, out_specs=P("mem", "grid"), check_vma=False
    )
```

time: 653 us -> 101 us (0.15); the launches traced: 644 us -> 101 us
  waiting for transfers between devices: 507 us -> 45.1 us
  blocking collectives: 44.4 us -> 0 us
  matrix products: 31.3 us -> 0 us
  between operations: 24.5 us -> 0.2 us
  starting transfers between devices: 7.85 us -> 27.5 us
  Pallas kernels: 0 us -> 15 us
  other arithmetic: 14.2 us -> 1.97 us
    psum x4 -> x0, waiting for transfers between devices: 482 us -> none  [from_root(): return lax.psum(jnp.where(mine, value, jnp.zeros_like(value)), axis)]
    ppermute x0 -> x16, waiting for transfers between devices: none -> 45.1 us  [send(): lax.ppermute(value, axis, [(j, (j + by) % size) for j in range(size)])]
    all_to_all x1 -> x0, blocking collectives: 44.4 us -> none  [on_device(): lax.all_to_all(flat, ('mem', 'grid'), split_axis=0, concat_axis=1, tiled=...]
    dot_general x8 -> x0, matrix products: 31.3 us -> none  [the longest x4 16.9 us: on_device(): incr = jnp.einsum('gpo,amo->agmp', coef, dy_inc, precision=highest)]
    ppermute x0 -> x16, starting transfers between devices: none -> 27.5 us  [send(): lax.ppermute(value, axis, [(j, (j + by) % size) for j in range(size)])]
    all_to_all x1 -> x0, waiting for transfers between devices: 24.5 us -> none  [on_device(): lax.all_to_all(state, ('mem', 'grid'), split_axis=1, concat_axis=0, tiled...]
    pallas_call x0 -> x5, Pallas kernels: none -> 15 us  [the longest x1 4.49 us: on_device(): pl.pallas_call(functools.partial(chain_kernel, n_mem), out_shape=jax.Shap...]
    reduce_sum x10 -> x1, other arithmetic: 7.57 us -> 0.02 us  [on_device(): jnp.sum(masks << jnp.arange(BLOCKS, dtype=jnp.int32)[:, None], axis=0)]
  transfers between devices with their start and end apart: 5 -> 16, of which waited for: 5 -> 3; matrix products, arithmetic and copies ran while one was open for 0% -> 7% of each run, Pallas kernels for 0% -> 6%
where the time goes in v1:
time: 101 us
  waiting for transfers between devices  45.1 us (45%)
  starting transfers between devices  27.5 us (27%)
  Pallas kernels  15 us (15%)
  local copies, waits for them, and re-layouts  10.8 us (11%)
  other arithmetic  1.97 us (2%)
    ppermute x16, waiting for transfers between devices, send(): lax.ppermute(value, axis, [(j, (j + by) % size) for j in range(size)])  45.1 us
    ppermute x16, starting transfers between devices, send(): lax.ppermute(value, axis, [(j, (j + by) % size) for j in range(size)])  27.5 us
    pallas_call x1, Pallas kernels, on_device(): pl.pallas_call(functools.partial(chain_kernel, n_mem), out_shape=jax.Shap...  4.49 us
    pallas_call x1, Pallas kernels, on_device(): pl.pallas_call(functools.partial(apply_kernel, n_mem, parts), out_shape=[...  3.82 us
    unnamed x40, local copies, waits for them, and re-layouts  3 us
    pallas_call x1, Pallas kernels, on_device(): pl.pallas_call(functools.partial(pack_kernel, n_mem, parts), out_shape=[p...  2.62 us
    pallas_call x1, Pallas kernels, on_device(): pl.pallas_call(functools.partial(unpack_kernel, n_mem, parts), out_shape=...  2.54 us
  transfers between devices with their start and end apart: 16, of which 3 were waited for; matrix products, arithmetic and copies ran while one was open for 7% of the time, Pallas kernels for 6%

profile of v1, /device:TPU:0, one launch (start us, length us, event | category | flops | bytes accessed | tf_op | source)
XLA Modules:
  0.0 100.6 jit_solution(13128150082933110852)
XLA Ops:
  0.0 0.7 compare_select_fusion.1
  0.7 1.3 %gather_fusion = s32[4]{0:T(128)S(1)} fusion(s32[4]{0:T(128)} %param.8, s32[1024]{0:T(1024)S(1)} %pad_clamp_fusion.1), kind=kCustom, calls=%fused_computation | custom fusion | bytes 48 | tf_op jit(solution)/shard_map/gather | solution.py:127
  2.0 0.6 and_select_fusion
  2.6 0.6 pad_add_fusion.start_ref
  3.3 2.6 %pack.1 = (f32[40,2048]{1,0:T(8,128)}, f32[40,2048]{1,0:T(8,128)}, f32[40,2048]{1,0:T(8,128)}, f32[40,2048]{1,0:T(8,128)}, f32[80,128]{1,0:T(8,128)}) custom-call(s32[8]{0:T(128)} %pad_add_fusion.start_ref, f32[20,16384]{1,0:T(8,128)} %x_ref.1), custom_call_target="tpu_custom_call" | custom-call | tf_op jit(solution)/shard_map/pack/pallas_call | solution.py:138
  5.9 3.3 %collective-permute-start.6 = (f32[80,128]{1,0:T(8,128)}, f32[80,128]{1,0:T(8,128)S(1)}, u32[]{:S(2)}, u32[]{:S(2)}) collective-permute-start(f32[80,128]{1,0:T(8,128)} %get-tuple-element.14.refs_0_), channel_id=1, source_target_pairs={{0,7},{1,0},{2,1},{3,2},{4,3},{5,4},{6,5},{7,6},{8,15},{9,8},{10,9... | collective-permute-start | bytes 122888 | tf_op jit(solution)/shard_map/ppermute | solution.py:148
  9.2 0.6 collective-permute-start.5
  10.1 1.5 %collective-permute-start.3 = (f32[80,128]{1,0:T(8,128)}, f32[80,128]{1,0:T(8,128)S(1)}, u32[]{:S(2)}, u32[]{:S(2)}) collective-permute-start(f32[80,128]{1,0:T(8,128)} %get-tuple-element.14.refs_0_), channel_id=1, source_target_pairs={{0,4},{1,5},{2,6},{3,7},{4,0},{5,1},{6,2},{7,3},{8,12},{9,13},{10,... | collective-permute-start | bytes 122888 | tf_op jit(solution)/shard_map/ppermute | solution.py:148
  11.8 2.4 %collective-permute-start.1 = (f32[80,128]{1,0:T(8,128)}, f32[80,128]{1,0:T(8,128)S(1)}, u32[]{:S(2)}, u32[]{:S(2)}) collective-permute-start(f32[80,128]{1,0:T(8,128)} %get-tuple-element.14.refs_0_), channel_id=1, source_target_pairs={{0,2},{1,3},{2,4},{3,5},{4,6},{5,7},{6,0},{7,1},{8,10},{9,11},{10,... | collective-permute-start | bytes 122888 | tf_op jit(solution)/shard_map/ppermute | solution.py:148
  14.1 1.6 %collective-permute-start.10 = (f32[40,2048]{1,0:T(8,128)}, f32[40,2048]{1,0:T(8,128)S(1)}, u32[]{:S(2)}, u32[]{:S(2)}) collective-permute-start(f32[40,2048]{1,0:T(8,128)} %get-tuple-element.16), channel_id=1, source_target_pairs={{0,8},{8,16},{16,24},{24,0},{1,9},{9,17},{17,25},{25,1},{2,10},{10... | collective-permute-start | bytes 983048 | tf_op jit(solution)/shard_map/ppermute | solution.py:148
  15.8 2.6 %collective-permute-start.11 = (f32[40,2048]{1,0:T(8,128)}, f32[40,2048]{1,0:T(8,128)S(1)}, u32[]{:S(2)}, u32[]{:S(2)}) collective-permute-start(f32[40,2048]{1,0:T(8,128)} %get-tuple-element.17), channel_id=1, source_target_pairs={{0,16},{8,24},{16,0},{24,8},{1,17},{9,25},{17,1},{25,9},{2,18},{10... | collective-permute-start | bytes 983048 | tf_op jit(solution)/shard_map/ppermute | solution.py:148
  18.4 1.3 %collective-permute-start.12 = (f32[40,2048]{1,0:T(8,128)}, f32[40,2048]{1,0:T(8,128)S(1)}, u32[]{:S(2)}, u32[]{:S(2)}) collective-permute-start(f32[40,2048]{1,0:T(8,128)} %get-tuple-element.18), channel_id=1, source_target_pairs={{0,24},{8,0},{16,8},{24,16},{1,25},{9,1},{17,9},{25,17},{2,26},{10... | collective-permute-start | bytes 983048 | tf_op jit(solution)/shard_map/ppermute | solution.py:148
  19.8 0.6 gather_fusion.1
  21.0 1.6 %pick.1.refs_0_ = f32[80,128]{1,0:T(8,128)} custom-call(s32[4]{0:T(128)} %get-tuple-element.23.shift_ref, f32[80,128]{1,0:T(8,128)} %get-tuple-element.14.refs_0_, f32[80,128]{1,0:T(8,128)} %copy-done.19, f32[80,128]{1,0:T(8,128)} %copy-done.18, f32[80,128]{1,0:T(8,128)} %copy-done.17, f32[80,128]{1,0:T(8,128)} %copy-done.16, f32[80,128]{1,0:T(8,128)} %copy-done.15, ...), custom_call_target="tpu_custom_call" | custom-call | tf_op jit(solution)/shard_map/pick/pallas_call | solution.py:152
  22.5 1.9 %collective-permute-start.9 = (f32[80,128]{1,0:T(8,128)}, f32[80,128]{1,0:T(8,128)S(1)}, u32[]{:S(2)}, u32[]{:S(2)}) collective-permute-start(f32[80,128]{1,0:T(8,128)} %pick.1.refs_0_), channel_id=1, source_target_pairs={{0,24},{8,0},{16,8},{24,16},{1,25},{9,1},{17,9},{25,17},{2,26},{10... | collective-permute-start | bytes 122888 | tf_op jit(solution)/shard_map/ppermute | solution.py:148
  24.8 16.7 %collective-permute-done.9.refs_3_ = f32[80,128]{1,0:T(8,128)S(1)} collective-permute-done((f32[80,128]{1,0:T(8,128)}, f32[80,128]{1,0:T(8,128)S(1)}, u32[]{:S(2)}, u32[]{:S(2)}) %collective-permute-start.9) | collective-permute-done | bytes 40992 | tf_op jit(solution)/shard_map/ppermute | solution.py:148
  41.5 9.5 %collective-permute-start.7 = (f32[80,128]{1,0:T(8,128)}, f32[80,128]{1,0:T(8,128)S(1)}, u32[]{:S(2)}, u32[]{:S(2)}) collective-permute-start(f32[80,128]{1,0:T(8,128)} %pick.1.refs_0_), channel_id=1, source_target_pairs={{0,8},{8,16},{16,24},{24,0},{1,9},{9,17},{17,25},{25,1},{2,10},{10... | collective-permute-start | bytes 122888 | tf_op jit(solution)/shard_map/ppermute | solution.py:148
  52.1 0.6 gather_fusion.3
  52.7 1.2 %gather_fusion.2 = s32[4]{0:T(128)} fusion(s32[1024]{0:T(1024)S(1)} %shift-left_reduce_fusion, s32[1024]{0:T(1024)S(1)} %pad_clamp_fusion), kind=kCustom, calls=%fused_computation.2 | custom fusion | bytes 48 | tf_op jit(solution)/shard_map/gather | solution.py:167
  53.9 0.7 dynamic_slice.3.code_ref
  54.5 0.8 copy.11
  55.4 0.8 copy.12
  56.2 0.8 copy.13
  57.0 0.6 copy-done.11
  57.6 4.5 %chain.1.t_ref = f32[80,2048]{1,0:T(8,128)} custom-call(s32[4]{0:T(128)} %gather_fusion.2, s32[256,4]{1,0:T(8,128)} %bitcast.7, f32[256,4]{1,0:T(8,128)} %bitcast.8, f32[256,4]{1,0:T(8,128)} %bitcast.9, f32[80,128]{1,0:T(8,128)} %pick.1.refs_0_, f32[80,128]{1,0:T(8,128)} %copy-done.12, f32[80,128]{1,0:T(8,128)} %copy-done.11, f32[80,128]{1,0:T(8,128)} %copy-done.10), custom_call_target="tpu_custom_call" | custom-call | tf_op jit(solution)/shard_map/chain/pallas_call | solution.py:160
  62.1 0.7 copy-done.4
  63.1 3.8 %apply.1 = (f32[40,2048]{1,0:T(8,128)}, f32[40,2048]{1,0:T(8,128)}, f32[40,2048]{1,0:T(8,128)}, f32[40,2048]{1,0:T(8,128)}) custom-call(s32[32]{0:T(128)} %dynamic_slice.3.code_ref, f32[80,2048]{1,0:T(8,128)} %chain.1.t_ref, f32[40,2048]{1,0:T(8,128)} %get-tuple-element.15.refs_0_, f32[40,2048]{1,0:T(8,128)} %copy-done.4, f32[40,2048]{1,0:T(8,128)} %copy-done.5, ...), custom_call_target="tpu_custom_call" | custom-call | tf_op jit(solution)/shard_map/apply/pallas_call | solution.py:168
  66.9 1.5 %collective-permute-start.14 = (f32[40,2048]{1,0:T(8,128)}, f32[40,2048]{1,0:T(8,128)S(1)}, u32[]{:S(2)}, u32[]{:S(2)}) collective-permute-start(f32[40,2048]{1,0:T(8,128)} %get-tuple-element.21), channel_id=1, source_target_pairs={{0,16},{8,24},{16,0},{24,8},{1,17},{9,25},{17,1},{25,9},{2,18},{10... | collective-permute-start | bytes 983048 | tf_op jit(solution)/shard_map/ppermute | solution.py:148
  68.9 7.6 %collective-permute-done.13.refs_1_ = f32[40,2048]{1,0:T(8,128)S(1)} collective-permute-done((f32[40,2048]{1,0:T(8,128)}, f32[40,2048]{1,0:T(8,128)S(1)}, u32[]{:S(2)}, u32[]{:S(2)}) %collective-permute-start.13) | collective-permute-done | bytes 327712 | tf_op jit(solution)/shard_map/ppermute | solution.py:148
  76.5 20.7 %collective-permute-done.14.refs_2_ = f32[40,2048]{1,0:T(8,128)S(1)} collective-permute-done((f32[40,2048]{1,0:T(8,128)}, f32[40,2048]{1,0:T(8,128)S(1)}, u32[]{:S(2)}, u32[]{:S(2)}) %collective-permute-start.14) | collective-permute-done | bytes 327712 | tf_op jit(solution)/shard_map/ppermute | solution.py:148
  97.2 0.7 copy-done.2
  98.1 2.5 %unpack.1 = f32[20,16384]{1,0:T(8,128)} custom-call(s32[8]{0:T(128)} %pad_add_fusion.start_ref, f32[40,2048]{1,0:T(8,128)} %get-tuple-element.19.refs_0_, f32[40,2048]{1,0:T(8,128)} %copy-done.1, f32[40,2048]{1,0:T(8,128)} %copy-done.2, f32[40,2048]{1,0:T(8,128)} %copy-done.3), custom_call_target="tpu_custom_call" | custom-call | tf_op jit(solution)/shard_map/unpack/pallas_call | solution.py:176
  (62 shorter events, 3.5 us)
Async XLA Ops:
  0.0 19.8 %copy-start = (s32[4,1024]{1,0:T(4,128)S(1)}, s32[4,1024]{1,0:T(4,128)}, u32[]{:S(2)}) copy-start(s32[4,1024]{1,0:T(4,128)} %param.12) | copy-start | bytes 49156
  0.0 51.0 %copy-start.7 = (f32[4,256]{1,0:T(4,128)S(1)}, f32[4,256]{1,0:T(4,128)}, u32[]{:S(2)}) copy-start(f32[4,256]{1,0:T(4,128)} %param.11) | copy-start | bytes 12292
  0.0 51.5 %copy-start.8 = (f32[4,256]{1,0:T(4,128)S(1)}, f32[4,256]{1,0:T(4,128)}, u32[]{:S(2)}) copy-start(f32[4,256]{1,0:T(4,128)} %param.10) | copy-start | bytes 12292
  0.0 52.1 %copy-start.9 = (s32[4,256]{1,0:T(4,128)S(1)}, s32[4,256]{1,0:T(4,128)}, u32[]{:S(2)}) copy-start(s32[4,256]{1,0:T(4,128)} %param.9) | copy-start | bytes 12292
  5.9 5.9 %collective-permute-start.6 = (f32[80,128]{1,0:T(8,128)}, f32[80,128]{1,0:T(8,128)S(1)}, u32[]{:S(2)}, u32[]{:S(2)}) collective-permute-start(f32[80,128]{1,0:T(8,128)} %get-tuple-element.14.refs_0_), channel_id=1, source_target_pairs={{0,7},{1,0},{2,1},{3,2},{4,3},{5,4},{6,5},{7,6},{8,15},{9,8},{10,9... | collective-permute-start | bytes 122888 | tf_op jit(solution)/shard_map/ppermute | solution.py:148
  9.2 4.9 %collective-permute-start.5 = (f32[80,128]{1,0:T(8,128)}, f32[80,128]{1,0:T(8,128)S(1)}, u32[]{:S(2)}, u32[]{:S(2)}) collective-permute-start(f32[80,128]{1,0:T(8,128)} %get-tuple-element.14.refs_0_), channel_id=1, source_target_pairs={{0,6},{1,7},{2,0},{3,1},{4,2},{5,3},{6,4},{7,5},{8,14},{9,15},{10,... | collective-permute-start | bytes 122888 | tf_op jit(solution)/shard_map/ppermute | solution.py:148
  9.8 4.4 %collective-permute-start.4 = (f32[80,128]{1,0:T(8,128)}, f32[80,128]{1,0:T(8,128)S(1)}, u32[]{:S(2)}, u32[]{:S(2)}) collective-permute-start(f32[80,128]{1,0:T(8,128)} %get-tuple-element.14.refs_0_), channel_id=1, source_target_pairs={{0,5},{1,6},{2,7},{3,0},{4,1},{5,2},{6,3},{7,4},{8,13},{9,14},{10,... | collective-permute-start | bytes 122888 | tf_op jit(solution)/shard_map/ppermute | solution.py:148
  10.1 5.7 %collective-permute-start.3 = (f32[80,128]{1,0:T(8,128)}, f32[80,128]{1,0:T(8,128)S(1)}, u32[]{:S(2)}, u32[]{:S(2)}) collective-permute-start(f32[80,128]{1,0:T(8,128)} %get-tuple-element.14.refs_0_), channel_id=1, source_target_pairs={{0,4},{1,5},{2,6},{3,7},{4,0},{5,1},{6,2},{7,3},{8,12},{9,13},{10,... | collective-permute-start | bytes 122888 | tf_op jit(solution)/shard_map/ppermute | solution.py:148
  11.6 6.8 %collective-permute-start.2 = (f32[80,128]{1,0:T(8,128)}, f32[80,128]{1,0:T(8,128)S(1)}, u32[]{:S(2)}, u32[]{:S(2)}) collective-permute-start(f32[80,128]{1,0:T(8,128)} %get-tuple-element.14.refs_0_), channel_id=1, source_target_pairs={{0,3},{1,4},{2,5},{3,6},{4,7},{5,0},{6,1},{7,2},{8,11},{9,12},{10,... | collective-permute-start | bytes 122888 | tf_op jit(solution)/shard_map/ppermute | solution.py:148
  11.7 8.6 %copy-start.13 = (f32[80,128]{1,0:T(8,128)}, f32[80,128]{1,0:T(8,128)S(1)}, u32[]{:S(2)}) copy-start(f32[80,128]{1,0:T(8,128)S(1)} %collective-permute-done.6.refs_7_) | copy-start | bytes 122884
  11.8 8.6 %collective-permute-start.1 = (f32[80,128]{1,0:T(8,128)}, f32[80,128]{1,0:T(8,128)S(1)}, u32[]{:S(2)}, u32[]{:S(2)}) collective-permute-start(f32[80,128]{1,0:T(8,128)} %get-tuple-element.14.refs_0_), channel_id=1, source_target_pairs={{0,2},{1,3},{2,4},{3,5},{4,6},{5,7},{6,0},{7,1},{8,10},{9,11},{10,... | collective-permute-start | bytes 122888 | tf_op jit(solution)/shard_map/ppermute | solution.py:148
  14.1 6.3 %copy-start.14 = (f32[80,128]{1,0:T(8,128)}, f32[80,128]{1,0:T(8,128)S(1)}, u32[]{:S(2)}) copy-start(f32[80,128]{1,0:T(8,128)S(1)} %collective-permute-done.5.refs_6_) | copy-start | bytes 122884
  14.1 6.2 %collective-permute-start = (f32[80,128]{1,0:T(8,128)}, f32[80,128]{1,0:T(8,128)S(1)}, u32[]{:S(2)}, u32[]{:S(2)}) collective-permute-start(f32[80,128]{1,0:T(8,128)} %get-tuple-element.14.refs_0_), channel_id=1, source_target_pairs={{0,1},{1,2},{2,3},{3,4},{4,5},{5,6},{6,7},{7,0},{8,9},{9,10},{10,1... | collective-permute-start | bytes 122888 | tf_op jit(solution)/shard_map/ppermute | solution.py:148
  14.1 6.2 %copy-start.15 = (f32[80,128]{1,0:T(8,128)}, f32[80,128]{1,0:T(8,128)S(1)}, u32[]{:S(2)}) copy-start(f32[80,128]{1,0:T(8,128)S(1)} %collective-permute-done.4.refs_5_) | copy-start | bytes 122884
  14.1 47.9 %collective-permute-start.10 = (f32[40,2048]{1,0:T(8,128)}, f32[40,2048]{1,0:T(8,128)S(1)}, u32[]{:S(2)}, u32[]{:S(2)}) collective-permute-start(f32[40,2048]{1,0:T(8,128)} %get-tuple-element.16), channel_id=1, source_target_pairs={{0,8},{8,16},{16,24},{24,0},{1,9},{9,17},{17,25},{25,1},{2,10},{10... | collective-permute-start | bytes 983048 | tf_op jit(solution)/shard_map/ppermute | solution.py:148
  15.8 4.6 %copy-start.16 = (f32[80,128]{1,0:T(8,128)}, f32[80,128]{1,0:T(8,128)S(1)}, u32[]{:S(2)}) copy-start(f32[80,128]{1,0:T(8,128)S(1)} %collective-permute-done.3.refs_4_) | copy-start | bytes 122884
  15.8 46.3 %collective-permute-start.11 = (f32[40,2048]{1,0:T(8,128)}, f32[40,2048]{1,0:T(8,128)S(1)}, u32[]{:S(2)}, u32[]{:S(2)}) collective-permute-start(f32[40,2048]{1,0:T(8,128)} %get-tuple-element.17), channel_id=1, source_target_pairs={{0,16},{8,24},{16,0},{24,8},{1,17},{9,25},{17,1},{25,9},{2,18},{10... | collective-permute-start | bytes 983048 | tf_op jit(solution)/shard_map/ppermute | solution.py:148
  18.4 2.0 %copy-start.17 = (f32[80,128]{1,0:T(8,128)}, f32[80,128]{1,0:T(8,128)S(1)}, u32[]{:S(2)}) copy-start(f32[80,128]{1,0:T(8,128)S(1)} %collective-permute-done.2.refs_3_) | copy-start | bytes 122884
  18.4 43.7 %collective-permute-start.12 = (f32[40,2048]{1,0:T(8,128)}, f32[40,2048]{1,0:T(8,128)S(1)}, u32[]{:S(2)}, u32[]{:S(2)}) collective-permute-start(f32[40,2048]{1,0:T(8,128)} %get-tuple-element.18), channel_id=1, source_target_pairs={{0,24},{8,0},{16,8},{24,16},{1,25},{9,1},{17,9},{25,17},{2,26},{10... | collective-permute-start | bytes 983048 | tf_op jit(solution)/shard_map/ppermute | solution.py:148
  22.5 18.9 %collective-permute-start.9 = (f32[80,128]{1,0:T(8,128)}, f32[80,128]{1,0:T(8,128)S(1)}, u32[]{:S(2)}, u32[]{:S(2)}) collective-permute-start(f32[80,128]{1,0:T(8,128)} %pick.1.refs_0_), channel_id=1, source_target_pairs={{0,24},{8,0},{16,8},{24,16},{1,25},{9,1},{17,9},{25,17},{2,26},{10... | collective-permute-start | bytes 122888 | tf_op jit(solution)/shard_map/ppermute | solution.py:148
  24.5 32.5 %collective-permute-start.8 = (f32[80,128]{1,0:T(8,128)}, f32[80,128]{1,0:T(8,128)S(1)}, u32[]{:S(2)}, u32[]{:S(2)}) collective-permute-start(f32[80,128]{1,0:T(8,128)} %pick.1.refs_0_), channel_id=1, source_target_pairs={{0,16},{8,24},{16,0},{24,8},{1,17},{9,25},{17,1},{25,9},{2,18},{10... | collective-permute-start | bytes 122888 | tf_op jit(solution)/shard_map/ppermute | solution.py:148
  41.5 15.5 %copy-start.10 = (f32[80,128]{1,0:T(8,128)}, f32[80,128]{1,0:T(8,128)S(1)}, u32[]{:S(2)}) copy-start(f32[80,128]{1,0:T(8,128)S(1)} %collective-permute-done.9.refs_3_) | copy-start | bytes 122884
  41.5 15.5 %collective-permute-start.7 = (f32[80,128]{1,0:T(8,128)}, f32[80,128]{1,0:T(8,128)S(1)}, u32[]{:S(2)}, u32[]{:S(2)}) collective-permute-start(f32[80,128]{1,0:T(8,128)} %pick.1.refs_0_), channel_id=1, source_target_pairs={{0,8},{8,16},{16,24},{24,0},{1,9},{9,17},{17,25},{25,1},{2,10},{10... | collective-permute-start | bytes 122888 | tf_op jit(solution)/shard_map/ppermute | solution.py:148
  62.1 0.7 copy-start.4
  62.1 0.8 copy-start.5
  62.1 0.9 copy-start.6
  66.9 9.6 %collective-permute-start.13 = (f32[40,2048]{1,0:T(8,128)}, f32[40,2048]{1,0:T(8,128)S(1)}, u32[]{:S(2)}, u32[]{:S(2)}) collective-permute-start(f32[40,2048]{1,0:T(8,128)} %get-tuple-element.20), channel_id=1, source_target_pairs={{0,24},{8,0},{16,8},{24,16},{1,25},{9,1},{17,9},{25,17},{2,26},{10... | collective-permute-start | bytes 983048 | tf_op jit(solution)/shard_map/ppermute | solution.py:148
  66.9 30.4 %collective-permute-start.14 = (f32[40,2048]{1,0:T(8,128)}, f32[40,2048]{1,0:T(8,128)S(1)}, u32[]{:S(2)}, u32[]{:S(2)}) collective-permute-start(f32[40,2048]{1,0:T(8,128)} %get-tuple-element.21), channel_id=1, source_target_pairs={{0,16},{8,24},{16,0},{24,8},{1,17},{9,25},{17,1},{25,9},{2,18},{10... | collective-permute-start | bytes 983048 | tf_op jit(solution)/shard_map/ppermute | solution.py:148
  68.4 28.9 %collective-permute-start.15 = (f32[40,2048]{1,0:T(8,128)}, f32[40,2048]{1,0:T(8,128)S(1)}, u32[]{:S(2)}, u32[]{:S(2)}) collective-permute-start(f32[40,2048]{1,0:T(8,128)} %get-tuple-element.22), channel_id=1, source_target_pairs={{0,8},{8,16},{16,24},{24,0},{1,9},{9,17},{17,25},{25,1},{2,10},{10... | collective-permute-start | bytes 983048 | tf_op jit(solution)/shard_map/ppermute | solution.py:148
  76.5 20.8 %copy-start.1 = (f32[40,2048]{1,0:T(8,128)}, f32[40,2048]{1,0:T(8,128)S(1)}, u32[]{:S(2)}) copy-start(f32[40,2048]{1,0:T(8,128)S(1)} %collective-permute-done.13.refs_1_) | copy-start | bytes 983044
  97.2 0.7 copy-start.2
  97.2 0.9 copy-start.3
  (4 other events, 2.5 us)

commit v2 on v1

v2 whole, which is shorter than its diff:
```python
import functools
import math

import jax
import jax.numpy as jnp
from jax import lax
from jax.experimental import pallas as pl
from jax.experimental.pallas import tpu as pltpu
from jax.sharding import PartitionSpec as P

BLOCKS = 4
TILE = 128
HIGHEST = lax.Precision.HIGHEST
VMEM = pl.BlockSpec(memory_space=pltpu.VMEM)
SMEM = pl.BlockSpec(memory_space=pltpu.SMEM)
ANY = pl.BlockSpec(memory_space=pl.ANY)


def piece_column(d, quarter, first):
    n_mem = lax.axis_size("mem")
    return lax.rem(lax.axis_index("mem") + d, n_mem) * quarter + first


def pack(x_ref, outs, parts, quarter, first):
    mem_loc = x_ref.shape[0]
    for d, out in enumerate(outs):
        width = out.shape[1]
        for p in range(parts):
            col = pl.multiple_of(piece_column(d, quarter, first) + p * width, TILE)
            out[p * mem_loc : (p + 1) * mem_loc, :] = x_ref[:, pl.ds(col, width)]


def first_kernel(parts, quarter, tile_ref, order_ref, x_ref, *outs):
    seen, outs = outs[-1], outs[:-1]
    mem_loc, grid_width = x_ref.shape
    for k in range(BLOCKS):
        tile = tile_ref[order_ref[k]]
        col = pl.multiple_of(lax.rem(tile, grid_width // TILE) * TILE, TILE)
        seen[k * mem_loc : (k + 1) * mem_loc, :] = x_ref[:, pl.ds(col, TILE)]
    pack(x_ref, outs, parts, quarter, 0)


def second_kernel(parts, quarter, first, order_ref, offset_ref, value_ref, error_ref, x_ref, after_ref, *outs):
    del after_ref
    pack(x_ref, outs[:-3], parts, quarter, first)
    obs = offset_ref.shape[1]
    for k in range(BLOCKS):
        row = pl.ds(order_ref[k], 1)
        for ref, out in zip((offset_ref, value_ref, error_ref), outs[-3:]):
            out[k] = jnp.transpose(jnp.broadcast_to(ref[row, :], (TILE, obs)))


def pick_kernel(tiles_here, tile_ref, order_ref, gathered_ref, out):
    mem_loc = out.shape[0] // BLOCKS
    for k in range(BLOCKS):
        owner = tile_ref[order_ref[k]] // tiles_here
        rows = slice(k * mem_loc, (k + 1) * mem_loc)
        out[rows, :] = gathered_ref[owner, rows, :]


def chain_kernel(n_mem, tile_ref, order_ref, mask_ref, offset_ref, value_ref, error_ref, *refs):
    pieces, out, slab = refs[:n_mem], refs[n_mem], refs[n_mem + 1]
    mem_loc = pieces[0].shape[0] // BLOCKS
    members = mem_loc * n_mem
    obs = offset_ref.shape[1]
    for d in range(n_mem):
        for k in range(BLOCKS):
            slab[k, d * mem_loc : (d + 1) * mem_loc, :] = pieces[d][k * mem_loc : (k + 1) * mem_loc, :]
    row = lax.broadcasted_iota(jnp.int32, (members, TILE), 0)
    lane = lax.broadcasted_iota(jnp.int32, (members, TILE), 1)
    out[:, 0:TILE] = jnp.where(row == lane, 1.0, 0.0)
    place = lax.broadcasted_iota(jnp.int32, (obs, TILE), 1)
    for k in range(BLOCKS):
        x = slab[k]
        ybar = jnp.sum(x, axis=0, keepdims=True) / members
        dev = x - ybar
        var = jnp.sum(dev * dev, axis=0, keepdims=True) / (members - 1.0)
        hit = offset_ref[k] == place
        error = error_ref[k]
        total = var + error
        shrink = jnp.where(hit, jnp.sqrt(error / total) - 1.0, 0.0)
        shift = jnp.where(hit, var / total * (value_ref[k] - ybar), 0.0)
        scale = 1.0 / ((members - 1.0) * (var + 1e-05))
        shrink = jnp.sum(shrink, axis=0, keepdims=True) * scale
        shift = jnp.sum(shift, axis=0, keepdims=True) * scale
        centred = dev - jnp.sum(dev, axis=0, keepdims=True) / members
        gain = lax.dot_general(
            dev * shrink + shift,
            centred,
            (((1,), (1,)), ((), ())),
            precision=HIGHEST,
            preferred_element_type=jnp.float32,
        )
        for j in range(k + 1, BLOCKS):
            old = slab[j]
            new = old + jnp.dot(gain, old, precision=HIGHEST, preferred_element_type=jnp.float32)
            used = mask_ref[order_ref[k], tile_ref[order_ref[j]]]
            slab[j] = jnp.where(used == 1, new, old)
        span = TILE << k
        so_far = out[:, 0:span]
        out[:, span : 2 * span] = so_far + jnp.dot(
            gain, so_far, precision=HIGHEST, preferred_element_type=jnp.float32
        )


def apply_kernel(n_mem, parts, quarter, first, order_ref, mask_ref, t_ref, *refs):
    pieces, outs = refs[:n_mem], refs[n_mem : 2 * n_mem]
    mem_loc = pieces[0].shape[0] // parts
    members = mem_loc * n_mem
    tiles = pieces[0].shape[1] // TILE
    base = (lax.axis_index("grid") * n_mem + lax.axis_index("mem")) * (quarter // TILE) + first // TILE
    for p in range(parts):
        rows = slice(p * mem_loc, (p + 1) * mem_loc)
        for t in range(tiles):
            cols = slice(t * TILE, (t + 1) * TILE)
            x = jnp.concatenate([piece[rows, cols] for piece in pieces], axis=0)
            code = 0
            for k in range(BLOCKS):
                code = code + (mask_ref[order_ref[k], base + p * tiles + t] << k)
            matrix = t_ref[:, pl.ds(pl.multiple_of(code * TILE, TILE), TILE)][:, 0:members]
            y = jnp.dot(matrix, x, precision=HIGHEST, preferred_element_type=jnp.float32)
            for d in range(n_mem):
                outs[d][rows, cols] = y[d * mem_loc : (d + 1) * mem_loc, :]


def unpack_kernel(n_mem, parts, quarter, firsts, *refs):
    out = refs[-1]
    mem_loc = out.shape[0]
    for c, first in enumerate(firsts):
        for d in range(n_mem):
            piece = refs[c * n_mem + d]
            width = piece.shape[1]
            for p in range(parts):
                col = pl.multiple_of(piece_column(d, quarter, first) + p * width, TILE)
                out[:, pl.ds(col, width)] = piece[p * mem_loc : (p + 1) * mem_loc, :]


def on_device(state, obs_tile, obs_offset, obs_value, obs_error, loc_mask, block_order):
    f32 = jnp.float32
    n_mem = lax.axis_size("mem")
    mem_loc, grid_width = state.shape
    members = mem_loc * n_mem
    quarter = grid_width // n_mem
    parts = 8 // math.gcd(mem_loc, 8)
    obs = obs_value.shape[1]
    unit = parts * TILE
    half = quarter // unit // 2 * unit
    firsts = (0, half)
    pieces = [
        jax.ShapeDtypeStruct((parts * mem_loc, width // parts), f32) for width in (half, quarter - half)
    ]
    seen = jax.ShapeDtypeStruct((BLOCKS * mem_loc, TILE), f32)
    dense = [jax.ShapeDtypeStruct((BLOCKS, obs, TILE), kind) for kind in (jnp.int32, f32, f32)]

    def send(value, by):
        return lax.ppermute(value, "mem", [(j, (j + by) % n_mem) for j in range(n_mem)])

    def exchange(values, sign):
        return [values[0]] + [send(values[d], sign * d) for d in range(1, n_mem)]

    *chunk, mine = pl.pallas_call(
        functools.partial(first_kernel, parts, quarter),
        out_shape=[pieces[0]] * n_mem + [seen],
        in_specs=[SMEM, SMEM, VMEM],
        out_specs=[VMEM] * (n_mem + 1),
        name="first",
    )(obs_tile, block_order, state)
    gathered = lax.all_gather(mine, "grid", axis=0)
    arrived_a = exchange(chunk, 1)
    picked = pl.pallas_call(
        functools.partial(pick_kernel, grid_width // TILE),
        out_shape=seen,
        in_specs=[SMEM, SMEM, VMEM],
        out_specs=VMEM,
        name="pick",
    )(obs_tile, block_order, gathered)
    slabs = exchange([picked] * n_mem, 1)
    *chunk, offset, value, error = pl.pallas_call(
        functools.partial(second_kernel, parts, quarter, half),
        out_shape=[pieces[1]] * n_mem + dense,
        in_specs=[SMEM] + [VMEM] * 4 + [ANY],
        out_specs=[VMEM] * (n_mem + 3),
        name="second",
    )(block_order, obs_offset, obs_value, obs_error, state, picked)
    arrived_b = exchange(chunk, 1)
    matrices = pl.pallas_call(
        functools.partial(chain_kernel, n_mem),
        out_shape=jax.ShapeDtypeStruct((members, TILE << BLOCKS), f32),
        in_specs=[SMEM] * 3 + [VMEM] * (3 + n_mem),
        out_specs=VMEM,
        scratch_shapes=[pltpu.VMEM((BLOCKS, members, TILE), f32)],
        name="chain",
    )(obs_tile, block_order, loc_mask, offset, value, error, *slabs)
    back = []
    for arrived, piece, first in zip((arrived_a, arrived_b), pieces, firsts):
        updated = pl.pallas_call(
            functools.partial(apply_kernel, n_mem, parts, quarter, first),
            out_shape=[piece] * n_mem,
            in_specs=[SMEM] * 2 + [VMEM] * (1 + n_mem),
            out_specs=[VMEM] * n_mem,
            name="apply",
        )(block_order, loc_mask, matrices, *arrived)
        back += exchange(updated, -1)
    return pl.pallas_call(
        functools.partial(unpack_kernel, n_mem, parts, quarter, firsts),
        out_shape=jax.ShapeDtypeStruct(state.shape, f32),
        in_specs=[VMEM] * len(back),
        out_specs=VMEM,
        name="unpack",
    )(*back)


def solution(mesh):
    placed = (P("mem", "grid"), P(), P(), P(), P(), P(), P())
    return jax.shard_map(
        on_device, mesh=mesh, in_specs=placed, out_specs=P("mem", "grid"), check_vma=False
    )
```

time: 101 us -> 79.9 us (0.79)
  waiting for transfers between devices: 45.1 us -> 16 us
  blocking collectives: 0 us -> 11.3 us
  local copies, waits for them, and re-layouts: 10.8 us -> 2.14 us
  Pallas kernels: 15 us -> 20.5 us
  starting transfers between devices: 27.5 us -> 29.5 us
  other arithmetic: 1.97 us -> 0 us
    ppermute x16 -> x15, waiting for transfers between devices: 45.1 us -> 16 us  [send(): lax.ppermute(value, 'mem', [(j, (j + by) % n_mem) for j in range(n_mem)])]
    all_gather x0 -> x1, blocking collectives: none -> 11.3 us  [on_device(): gathered = lax.all_gather(mine, 'grid', axis=0)]
    gather x9 -> x0, local copies, waits for them, and re-layouts: 7.17 us -> none  [the longest x2 1.37 us: on_device(): obs_offset[block_order]]
    pallas_call x4 -> x6, Pallas kernels: 10.5 us -> 15.7 us  [the longest x2 5.81 us: on_device(): pl.pallas_call(functools.partial(apply_kernel, n_mem, parts, quarter, fir...]
    ppermute x16 -> x15, starting transfers between devices: 27.5 us -> 29.5 us  [send(): lax.ppermute(value, 'mem', [(j, (j + by) % n_mem) for j in range(n_mem)])]
    select_n x3 -> x0, other arithmetic: 1.29 us -> none  [the longest x1 0.7 us: on_device(): tile = obs_tile[block_order]]
    unnamed x40 -> x30, local copies, waits for them, and re-layouts: 3 us -> 2.14 us
  transfers between devices with their start and end apart: 16 -> 15, of which waited for: 3 -> 5; matrix products, arithmetic and copies ran while one was open for 7% -> 0% of each run, Pallas kernels for 6% -> 19%
where the time goes in v2:
time: 79.9 us; the launch traced here: 79.5 us
  starting transfers between devices  29.5 us (37%)
  Pallas kernels  20.5 us (26%)
  waiting for transfers between devices  16 us (20%)
  blocking collectives  11.3 us (14%)
  local copies, waits for them, and re-layouts  2.14 us (3%)
    ppermute x15, starting transfers between devices, send(): lax.ppermute(value, 'mem', [(j, (j + by) % n_mem) for j in range(n_mem)])  29.5 us
    ppermute x15, waiting for transfers between devices, send(): lax.ppermute(value, 'mem', [(j, (j + by) % n_mem) for j in range(n_mem)])  16 us
    all_gather x1, blocking collectives, on_device(): gathered = lax.all_gather(mine, 'grid', axis=0)  11.3 us
    pallas_call x2, Pallas kernels, on_device(): pl.pallas_call(functools.partial(apply_kernel, n_mem, parts, quarter, fir...  5.81 us
    pallas_call x1, Pallas kernels, on_device(): pl.pallas_call(functools.partial(chain_kernel, n_mem), out_shape=jax.Shap...  4.79 us
    pallas_call x1, Pallas kernels, on_device(): pl.pallas_call(functools.partial(second_kernel, parts, quarter, half), ou...  3.26 us
    pallas_call x1, Pallas kernels, on_device(): pl.pallas_call(functools.partial(unpack_kernel, n_mem, parts, quarter, fi...  2.66 us
    pallas_call x1, Pallas kernels, on_device(): pl.pallas_call(functools.partial(first_kernel, parts, quarter), out_shape...  2.34 us
  transfers between devices with their start and end apart: 15, of which 5 were waited for; matrix products, arithmetic and copies ran while one was open for 0% of the time, Pallas kernels for 19%

profile of v2, /device:TPU:0, one launch (start us, length us, event | category | flops | bytes accessed | tf_op | source)
XLA Modules:
  0.0 79.5 jit_solution(14076436596612015368)
XLA Ops:
  0.0 2.3 %first.1 = (f32[40,1024]{1,0:T(8,128)}, f32[40,1024]{1,0:T(8,128)}, f32[40,1024]{1,0:T(8,128)}, f32[40,1024]{1,0:T(8,128)}, f32[80,128]{1,0:T(8,128)}) custom-call(s32[4]{0:T(128)} %tile_ref.5, s32[4]{0:T(128)} %order_ref.11, f32[20,16384]{1,0:T(8,128)} %x_ref.3), custom_call_target="tpu_custom_call" | custom-call | tf_op jit(solution)/shard_map/first/pallas_call | solution.py:161
  2.3 3.0 %collective-permute-start.3 = (f32[40,1024]{1,0:T(8,128)}, f32[40,1024]{1,0:T(8,128)S(1)}, u32[]{:S(2)}, u32[]{:S(2)}) collective-permute-start(f32[40,1024]{1,0:T(8,128)} %get-tuple-element.30), channel_id=1, source_target_pairs={{0,8},{8,16},{16,24},{24,0},{1,9},{9,17},{17,25},{25,1},{2,10},{10... | collective-permute-start | bytes 491528 | tf_op jit(solution)/shard_map/ppermute | solution.py:156
  5.4 2.6 %collective-permute-start.4 = (f32[40,1024]{1,0:T(8,128)}, f32[40,1024]{1,0:T(8,128)S(1)}, u32[]{:S(2)}, u32[]{:S(2)}) collective-permute-start(f32[40,1024]{1,0:T(8,128)} %get-tuple-element.31), channel_id=1, source_target_pairs={{0,16},{8,24},{16,0},{24,8},{1,17},{9,25},{17,1},{25,9},{2,18},{10... | collective-permute-start | bytes 491528 | tf_op jit(solution)/shard_map/ppermute | solution.py:156
  8.0 1.3 %collective-permute-start.5 = (f32[40,1024]{1,0:T(8,128)}, f32[40,1024]{1,0:T(8,128)S(1)}, u32[]{:S(2)}, u32[]{:S(2)}) collective-permute-start(f32[40,1024]{1,0:T(8,128)} %get-tuple-element.32), channel_id=1, source_target_pairs={{0,24},{8,0},{16,8},{24,16},{1,25},{9,1},{17,9},{25,17},{2,26},{10... | collective-permute-start | bytes 491528 | tf_op jit(solution)/shard_map/ppermute | solution.py:156
  9.3 11.3 %all-gather = f32[640,128]{1,0:T(8,128)} all-gather(f32[80,128]{1,0:T(8,128)} %get-tuple-element.25), channel_id=2, replica_groups=mesh['mem'=4,'grid'=8] {'grid'}, dimensions={0}, use_global_device_ids=true | all-gather | bytes 368640 | tf_op jit(solution)/shard_map/all_gather | solution.py:168
  20.6 1.6 %pick.1.after_ref.refs_0_ = f32[80,128]{1,0:T(8,128)} custom-call(s32[4]{0:T(128)} %tile_ref.5, s32[4]{0:T(128)} %order_ref.11, f32[8,80,128]{2,1,0:T(8,128)} %bitcast.1), custom_call_target="tpu_custom_call" | custom-call | tf_op jit(solution)/shard_map/pick/pallas_call | solution.py:170
  22.2 0.4 collective-permute-start.2
  22.6 1.7 %collective-permute-start.1 = (f32[80,128]{1,0:T(8,128)}, f32[80,128]{1,0:T(8,128)S(1)}, u32[]{:S(2)}, u32[]{:S(2)}) collective-permute-start(f32[80,128]{1,0:T(8,128)} %pick.1.after_ref.refs_0_), channel_id=1, source_target_pairs={{0,16},{8,24},{16,0},{24,8},{1,17},{9,25},{17,1},{25,9},{2,18},{10... | collective-permute-start | bytes 122888 | tf_op jit(solution)/shard_map/ppermute | solution.py:156
  24.3 2.1 %collective-permute-done.2.refs_3_ = f32[80,128]{1,0:T(8,128)S(1)} collective-permute-done((f32[80,128]{1,0:T(8,128)}, f32[80,128]{1,0:T(8,128)S(1)}, u32[]{:S(2)}, u32[]{:S(2)}) %collective-permute-start.2) | collective-permute-done | bytes 40992 | tf_op jit(solution)/shard_map/ppermute | solution.py:156
  26.4 0.8 collective-permute-start
  27.2 3.3 %second.1 = (f32[40,1024]{1,0:T(8,128)}, f32[40,1024]{1,0:T(8,128)}, f32[40,1024]{1,0:T(8,128)}, f32[40,1024]{1,0:T(8,128)}, s32[4,256,128]{2,1,0:T(8,128)}, /*i...) custom-call(s32[4]{0:T(128)} %order_ref.11, s32[4,256]{1,0:T(4,128)} %offset_ref.1, f32[4,256]{1,0:T(4,128)} %value_ref.1, ...), custom_call_target="tpu_custom_call" | custom-call | tf_op jit(solution)/shard_map/second/pallas_call | solution.py:178
  30.4 0.2 collective-permute-start.9
  30.6 1.8 %collective-permute-done.refs_1_ = f32[80,128]{1,0:T(8,128)S(1)} collective-permute-done((f32[80,128]{1,0:T(8,128)}, f32[80,128]{1,0:T(8,128)S(1)}, u32[]{:S(2)}, u32[]{:S(2)}) %collective-permute-start) | collective-permute-done | bytes 40992 | tf_op jit(solution)/shard_map/ppermute | solution.py:156
  32.4 1.7 %collective-permute-start.10 = (f32[40,1024]{1,0:T(8,128)}, f32[40,1024]{1,0:T(8,128)S(1)}, u32[]{:S(2)}, u32[]{:S(2)}) collective-permute-start(f32[40,1024]{1,0:T(8,128)} %get-tuple-element.39), channel_id=1, source_target_pairs={{0,16},{8,24},{16,0},{24,8},{1,17},{9,25},{17,1},{25,9},{2,18},{10... | collective-permute-start | bytes 491528 | tf_op jit(solution)/shard_map/ppermute | solution.py:156
  34.1 1.3 %collective-permute-start.11 = (f32[40,1024]{1,0:T(8,128)}, f32[40,1024]{1,0:T(8,128)S(1)}, u32[]{:S(2)}, u32[]{:S(2)}) collective-permute-start(f32[40,1024]{1,0:T(8,128)} %get-tuple-element.40), channel_id=1, source_target_pairs={{0,24},{8,0},{16,8},{24,16},{1,25},{9,1},{17,9},{25,17},{2,26},{10... | collective-permute-start | bytes 491528 | tf_op jit(solution)/shard_map/ppermute | solution.py:156
  35.5 4.8 %chain.1.t_ref = f32[80,2048]{1,0:T(8,128)} custom-call(s32[4]{0:T(128)} %tile_ref.5, s32[4]{0:T(128)} %order_ref.11, s32[4,1024]{1,0:T(4,128)} %mask_ref.5, s32[4,256,128]{2,1,0:T(8,128)} %get-tuple-element.26.offset_ref, f32[4,256,128]{2,1,0:T(8,128)} %get-tuple-element.27.value_ref, f32[4,256,128]{2,1,0:T(8,128)} %get-tuple-element.28.error_ref, ...), custom_call_target="tpu_custom_call" | custom-call | tf_op jit(solution)/shard_map/chain/pallas_call | solution.py:186
  40.3 0.6 copy-done.7
  40.9 0.1 copy-done.8
  41.0 2.9 %apply.2 = (f32[40,1024]{1,0:T(8,128)}, f32[40,1024]{1,0:T(8,128)}, f32[40,1024]{1,0:T(8,128)}, f32[40,1024]{1,0:T(8,128)}) custom-call(s32[4]{0:T(128)} %order_ref.11, s32[4,1024]{1,0:T(4,128)} %mask_ref.5, f32[80,2048]{1,0:T(8,128)} %chain.1.t_ref, f32[40,1024]{1,0:T(8,128)} %get-tuple-element.29.refs_0_, f32[40,1024]{1,0:T(8,128)} %copy-done.6, ...), custom_call_target="tpu_custom_call" | custom-call | tf_op jit(solution)/shard_map/apply/pallas_call | solution.py:196
  43.9 1.3 %collective-permute-start.6 = (f32[40,1024]{1,0:T(8,128)}, f32[40,1024]{1,0:T(8,128)S(1)}, u32[]{:S(2)}, u32[]{:S(2)}) collective-permute-start(f32[40,1024]{1,0:T(8,128)} %get-tuple-element.34), channel_id=1, source_target_pairs={{0,24},{8,0},{16,8},{24,16},{1,25},{9,1},{17,9},{25,17},{2,26},{10... | collective-permute-start | bytes 491528 | tf_op jit(solution)/shard_map/ppermute | solution.py:156
  45.3 0.8 %collective-permute-start.7 = (f32[40,1024]{1,0:T(8,128)}, f32[40,1024]{1,0:T(8,128)S(1)}, u32[]{:S(2)}, u32[]{:S(2)}) collective-permute-start(f32[40,1024]{1,0:T(8,128)} %get-tuple-element.35), channel_id=1, source_target_pairs={{0,16},{8,24},{16,0},{24,8},{1,17},{9,25},{17,1},{25,9},{2,18},{10... | collective-permute-start | bytes 491528 | tf_op jit(solution)/shard_map/ppermute | solution.py:156
  46.1 0.8 collective-permute-start.8
  46.9 0.6 copy-done.10
  47.5 0.1 copy-done.11
  47.6 2.9 %apply.3 = (f32[40,1024]{1,0:T(8,128)}, f32[40,1024]{1,0:T(8,128)}, f32[40,1024]{1,0:T(8,128)}, f32[40,1024]{1,0:T(8,128)}) custom-call(s32[4]{0:T(128)} %order_ref.11, s32[4,1024]{1,0:T(4,128)} %mask_ref.5, f32[80,2048]{1,0:T(8,128)} %chain.1.t_ref, f32[40,1024]{1,0:T(8,128)} %get-tuple-element.37.refs_0_, f32[40,1024]{1,0:T(8,128)} %copy-done.9, ...), custom_call_target="tpu_custom_call" | custom-call | tf_op jit(solution)/shard_map/apply/pallas_call | solution.py:196
  50.5 12.9 %collective-permute-start.12 = (f32[40,1024]{1,0:T(8,128)}, f32[40,1024]{1,0:T(8,128)S(1)}, u32[]{:S(2)}, u32[]{:S(2)}) collective-permute-start(f32[40,1024]{1,0:T(8,128)} %get-tuple-element.42), channel_id=1, source_target_pairs={{0,24},{8,0},{16,8},{24,16},{1,25},{9,1},{17,9},{25,17},{2,26},{10... | collective-permute-start | bytes 491528 | tf_op jit(solution)/shard_map/ppermute | solution.py:156
  63.3 0.6 collective-permute-start.14
  63.9 1.7 %collective-permute-done.7.refs_2_ = f32[40,1024]{1,0:T(8,128)S(1)} collective-permute-done((f32[40,1024]{1,0:T(8,128)}, f32[40,1024]{1,0:T(8,128)S(1)}, u32[]{:S(2)}, u32[]{:S(2)}) %collective-permute-start.7) | collective-permute-done | bytes 163872 | tf_op jit(solution)/shard_map/ppermute | solution.py:156
  65.7 1.6 %collective-permute-done.12.refs_5_ = f32[40,1024]{1,0:T(8,128)S(1)} collective-permute-done((f32[40,1024]{1,0:T(8,128)}, f32[40,1024]{1,0:T(8,128)S(1)}, u32[]{:S(2)}, u32[]{:S(2)}) %collective-permute-start.12) | collective-permute-done | bytes 163872 | tf_op jit(solution)/shard_map/ppermute | solution.py:156
  67.3 8.8 %collective-permute-done.13.refs_6_ = f32[40,1024]{1,0:T(8,128)S(1)} collective-permute-done((f32[40,1024]{1,0:T(8,128)}, f32[40,1024]{1,0:T(8,128)S(1)}, u32[]{:S(2)}, u32[]{:S(2)}) %collective-permute-start.13) | collective-permute-done | bytes 163872 | tf_op jit(solution)/shard_map/ppermute | solution.py:156
  76.1 0.6 copy-done.4
  76.8 2.7 %unpack.1 = f32[20,16384]{1,0:T(8,128)} custom-call(f32[40,1024]{1,0:T(8,128)} %get-tuple-element.33.refs_0_, f32[40,1024]{1,0:T(8,128)} %copy-done, f32[40,1024]{1,0:T(8,128)} %copy-done.1, f32[40,1024]{1,0:T(8,128)} %copy-done.2, f32[40,1024]{1,0:T(8,128)} %get-tuple-element.41.refs_4_, f32[40,1024]{1,0:T(8,128)} %copy-done.3, f32[40,1024]{1,0:T(8,128)} %copy-done.4, ...), custom_call_target="tpu_custom_call" | custom-call | tf_op jit(solution)/shard_map/unpack/pallas_call | solution.py:204
  (36 shorter events, 0.1 us)
Async XLA Ops:
  2.3 31.8 %collective-permute-start.3 = (f32[40,1024]{1,0:T(8,128)}, f32[40,1024]{1,0:T(8,128)S(1)}, u32[]{:S(2)}, u32[]{:S(2)}) collective-permute-start(f32[40,1024]{1,0:T(8,128)} %get-tuple-element.30), channel_id=1, source_target_pairs={{0,8},{8,16},{16,24},{24,0},{1,9},{9,17},{17,25},{25,1},{2,10},{10... | collective-permute-start | bytes 491528 | tf_op jit(solution)/shard_map/ppermute | solution.py:156
  5.4 34.9 %collective-permute-start.4 = (f32[40,1024]{1,0:T(8,128)}, f32[40,1024]{1,0:T(8,128)S(1)}, u32[]{:S(2)}, u32[]{:S(2)}) collective-permute-start(f32[40,1024]{1,0:T(8,128)} %get-tuple-element.31), channel_id=1, source_target_pairs={{0,16},{8,24},{16,0},{24,8},{1,17},{9,25},{17,1},{25,9},{2,18},{10... | collective-permute-start | bytes 491528 | tf_op jit(solution)/shard_map/ppermute | solution.py:156
  8.0 32.3 %collective-permute-start.5 = (f32[40,1024]{1,0:T(8,128)}, f32[40,1024]{1,0:T(8,128)S(1)}, u32[]{:S(2)}, u32[]{:S(2)}) collective-permute-start(f32[40,1024]{1,0:T(8,128)} %get-tuple-element.32), channel_id=1, source_target_pairs={{0,24},{8,0},{16,8},{24,16},{1,25},{9,1},{17,9},{25,17},{2,26},{10... | collective-permute-start | bytes 491528 | tf_op jit(solution)/shard_map/ppermute | solution.py:156
  22.2 4.2 %collective-permute-start.2 = (f32[80,128]{1,0:T(8,128)}, f32[80,128]{1,0:T(8,128)S(1)}, u32[]{:S(2)}, u32[]{:S(2)}) collective-permute-start(f32[80,128]{1,0:T(8,128)} %pick.1.after_ref.refs_0_), channel_id=1, source_target_pairs={{0,24},{8,0},{16,8},{24,16},{1,25},{9,1},{17,9},{25,17},{2,26},{10... | collective-permute-start | bytes 122888 | tf_op jit(solution)/shard_map/ppermute | solution.py:156
  22.6 7.8 %collective-permute-start.1 = (f32[80,128]{1,0:T(8,128)}, f32[80,128]{1,0:T(8,128)S(1)}, u32[]{:S(2)}, u32[]{:S(2)}) collective-permute-start(f32[80,128]{1,0:T(8,128)} %pick.1.after_ref.refs_0_), channel_id=1, source_target_pairs={{0,16},{8,24},{16,0},{24,8},{1,17},{9,25},{17,1},{25,9},{2,18},{10... | collective-permute-start | bytes 122888 | tf_op jit(solution)/shard_map/ppermute | solution.py:156
  26.4 9.1 %copy-start.12 = (f32[80,128]{1,0:T(8,128)}, f32[80,128]{1,0:T(8,128)S(1)}, u32[]{:S(2)}) copy-start(f32[80,128]{1,0:T(8,128)S(1)} %collective-permute-done.2.refs_3_) | copy-start | bytes 122884
  26.4 6.0 %collective-permute-start = (f32[80,128]{1,0:T(8,128)}, f32[80,128]{1,0:T(8,128)S(1)}, u32[]{:S(2)}, u32[]{:S(2)}) collective-permute-start(f32[80,128]{1,0:T(8,128)} %pick.1.after_ref.refs_0_), channel_id=1, source_target_pairs={{0,8},{8,16},{16,24},{24,0},{1,9},{9,17},{17,25},{25,1},{2,10},{10... | collective-permute-start | bytes 122888 | tf_op jit(solution)/shard_map/ppermute | solution.py:156
  30.4 5.0 %copy-start.13 = (f32[80,128]{1,0:T(8,128)}, f32[80,128]{1,0:T(8,128)S(1)}, u32[]{:S(2)}) copy-start(f32[80,128]{1,0:T(8,128)S(1)} %collective-permute-done.1.refs_2_) | copy-start | bytes 122884
  30.4 15.6 %collective-permute-start.9 = (f32[40,1024]{1,0:T(8,128)}, f32[40,1024]{1,0:T(8,128)S(1)}, u32[]{:S(2)}, u32[]{:S(2)}) collective-permute-start(f32[40,1024]{1,0:T(8,128)} %get-tuple-element.38), channel_id=1, source_target_pairs={{0,8},{8,16},{16,24},{24,0},{1,9},{9,17},{17,25},{25,1},{2,10},{10... | collective-permute-start | bytes 491528 | tf_op jit(solution)/shard_map/ppermute | solution.py:156
  32.4 3.1 %copy-start.14 = (f32[80,128]{1,0:T(8,128)}, f32[80,128]{1,0:T(8,128)S(1)}, u32[]{:S(2)}) copy-start(f32[80,128]{1,0:T(8,128)S(1)} %collective-permute-done.refs_1_) | copy-start | bytes 122884
  32.4 14.4 %collective-permute-start.10 = (f32[40,1024]{1,0:T(8,128)}, f32[40,1024]{1,0:T(8,128)S(1)}, u32[]{:S(2)}, u32[]{:S(2)}) collective-permute-start(f32[40,1024]{1,0:T(8,128)} %get-tuple-element.39), channel_id=1, source_target_pairs={{0,16},{8,24},{16,0},{24,8},{1,17},{9,25},{17,1},{25,9},{2,18},{10... | collective-permute-start | bytes 491528 | tf_op jit(solution)/shard_map/ppermute | solution.py:156
  34.1 6.2 %copy-start.6 = (f32[40,1024]{1,0:T(8,128)}, f32[40,1024]{1,0:T(8,128)S(1)}, u32[]{:S(2)}) copy-start(f32[40,1024]{1,0:T(8,128)S(1)} %collective-permute-done.3.refs_1_) | copy-start | bytes 491524
  34.1 12.7 %collective-permute-start.11 = (f32[40,1024]{1,0:T(8,128)}, f32[40,1024]{1,0:T(8,128)S(1)}, u32[]{:S(2)}, u32[]{:S(2)}) collective-permute-start(f32[40,1024]{1,0:T(8,128)} %get-tuple-element.40), channel_id=1, source_target_pairs={{0,24},{8,0},{16,8},{24,16},{1,25},{9,1},{17,9},{25,17},{2,26},{10... | collective-permute-start | bytes 491528 | tf_op jit(solution)/shard_map/ppermute | solution.py:156
  40.3 0.7 copy-start.7
  40.3 0.7 copy-start.8
  43.9 19.4 %collective-permute-start.6 = (f32[40,1024]{1,0:T(8,128)}, f32[40,1024]{1,0:T(8,128)S(1)}, u32[]{:S(2)}, u32[]{:S(2)}) collective-permute-start(f32[40,1024]{1,0:T(8,128)} %get-tuple-element.34), channel_id=1, source_target_pairs={{0,24},{8,0},{16,8},{24,16},{1,25},{9,1},{17,9},{25,17},{2,26},{10... | collective-permute-start | bytes 491528 | tf_op jit(solution)/shard_map/ppermute | solution.py:156
  45.3 20.4 %collective-permute-start.7 = (f32[40,1024]{1,0:T(8,128)}, f32[40,1024]{1,0:T(8,128)S(1)}, u32[]{:S(2)}, u32[]{:S(2)}) collective-permute-start(f32[40,1024]{1,0:T(8,128)} %get-tuple-element.35), channel_id=1, source_target_pairs={{0,16},{8,24},{16,0},{24,8},{1,17},{9,25},{17,1},{25,9},{2,18},{10... | collective-permute-start | bytes 491528 | tf_op jit(solution)/shard_map/ppermute | solution.py:156
  46.1 0.8 %copy-start.9 = (f32[40,1024]{1,0:T(8,128)}, f32[40,1024]{1,0:T(8,128)S(1)}, u32[]{:S(2)}) copy-start(f32[40,1024]{1,0:T(8,128)S(1)} %collective-permute-done.9.refs_1_) | copy-start | bytes 491524
  46.1 19.6 %collective-permute-start.8 = (f32[40,1024]{1,0:T(8,128)}, f32[40,1024]{1,0:T(8,128)S(1)}, u32[]{:S(2)}, u32[]{:S(2)}) collective-permute-start(f32[40,1024]{1,0:T(8,128)} %get-tuple-element.36), channel_id=1, source_target_pairs={{0,8},{8,16},{16,24},{24,0},{1,9},{9,17},{17,25},{25,1},{2,10},{10... | collective-permute-start | bytes 491528 | tf_op jit(solution)/shard_map/ppermute | solution.py:156
  46.8 0.7 copy-start.10
  46.8 0.7 copy-start.11
  50.5 16.8 %collective-permute-start.12 = (f32[40,1024]{1,0:T(8,128)}, f32[40,1024]{1,0:T(8,128)S(1)}, u32[]{:S(2)}, u32[]{:S(2)}) collective-permute-start(f32[40,1024]{1,0:T(8,128)} %get-tuple-element.42), channel_id=1, source_target_pairs={{0,24},{8,0},{16,8},{24,16},{1,25},{9,1},{17,9},{25,17},{2,26},{10... | collective-permute-start | bytes 491528 | tf_op jit(solution)/shard_map/ppermute | solution.py:156
  63.3 12.8 %collective-permute-start.13 = (f32[40,1024]{1,0:T(8,128)}, f32[40,1024]{1,0:T(8,128)S(1)}, u32[]{:S(2)}, u32[]{:S(2)}) collective-permute-start(f32[40,1024]{1,0:T(8,128)} %get-tuple-element.43), channel_id=1, source_target_pairs={{0,16},{8,24},{16,0},{24,8},{1,17},{9,25},{17,1},{25,9},{2,18},{10... | collective-permute-start | bytes 491528 | tf_op jit(solution)/shard_map/ppermute | solution.py:156
  63.3 12.8 %copy-start = (f32[40,1024]{1,0:T(8,128)}, f32[40,1024]{1,0:T(8,128)S(1)}, u32[]{:S(2)}) copy-start(f32[40,1024]{1,0:T(8,128)S(1)} %collective-permute-done.6.refs_1_) | copy-start | bytes 491524
  63.3 12.7 %collective-permute-start.14 = (f32[40,1024]{1,0:T(8,128)}, f32[40,1024]{1,0:T(8,128)S(1)}, u32[]{:S(2)}, u32[]{:S(2)}) collective-permute-start(f32[40,1024]{1,0:T(8,128)} %get-tuple-element.44), channel_id=1, source_target_pairs={{0,8},{8,16},{16,24},{24,0},{1,9},{9,17},{17,25},{25,1},{2,10},{10... | collective-permute-start | bytes 491528 | tf_op jit(solution)/shard_map/ppermute | solution.py:156
  65.7 10.5 %copy-start.1 = (f32[40,1024]{1,0:T(8,128)}, f32[40,1024]{1,0:T(8,128)S(1)}, u32[]{:S(2)}) copy-start(f32[40,1024]{1,0:T(8,128)S(1)} %collective-permute-done.7.refs_2_) | copy-start | bytes 491524
  65.7 10.5 %copy-start.2 = (f32[40,1024]{1,0:T(8,128)}, f32[40,1024]{1,0:T(8,128)S(1)}, u32[]{:S(2)}) copy-start(f32[40,1024]{1,0:T(8,128)S(1)} %collective-permute-done.8.refs_3_) | copy-start | bytes 491524
  67.3 8.9 %copy-start.3 = (f32[40,1024]{1,0:T(8,128)}, f32[40,1024]{1,0:T(8,128)S(1)}, u32[]{:S(2)}) copy-start(f32[40,1024]{1,0:T(8,128)S(1)} %collective-permute-done.12.refs_5_) | copy-start | bytes 491524
  76.1 0.7 copy-start.4
  76.1 0.7 copy-start.5

commit v3 on v2

v3 whole, which is shorter than its diff:
```python
import functools
import math

import jax
import jax.numpy as jnp
from jax import lax
from jax.experimental import pallas as pl
from jax.experimental.pallas import tpu as pltpu
from jax.sharding import PartitionSpec as P

BLOCKS = 4
TILE = 128
HIGHEST = lax.Precision.HIGHEST
VMEM = pl.BlockSpec(memory_space=pltpu.VMEM)
SMEM = pl.BlockSpec(memory_space=pltpu.SMEM)
ANY = pl.BlockSpec(memory_space=pl.ANY)
HBM = pl.BlockSpec(memory_space=pltpu.HBM)


def kernel_call(kernel, name, out_shape, in_specs, out_specs, scratch_shapes=(), aliases=None, vmem=12):
    return pl.pallas_call(
        kernel,
        name=name,
        out_shape=out_shape,
        in_specs=in_specs,
        out_specs=out_specs,
        scratch_shapes=scratch_shapes,
        input_output_aliases=aliases or {},
        compiler_params=pltpu.CompilerParams(vmem_limit_bytes=vmem << 20),
    )


def run_all(copies):
    for copy in copies:
        copy.start()
    for copy in copies:
        copy.wait()


def seen_kernel(tile_ref, order_ref, x_ref, out, tile, order, held, sem):
    mem_loc, grid_width = x_ref.shape
    tiles_here = grid_width // TILE
    run_all(
        [
            pltpu.make_async_copy(tile_ref, tile, sem.at[0]),
            pltpu.make_async_copy(order_ref, order, sem.at[1]),
        ]
    )
    copies = []
    for k in range(BLOCKS):
        col = pl.multiple_of(lax.rem(tile[order[k]], tiles_here) * TILE, TILE)
        copies.append(pltpu.make_async_copy(x_ref.at[:, pl.ds(col, TILE)], held.at[k], sem.at[k]))
    run_all(copies)
    for k in range(BLOCKS):
        here = tile[order[k]] // tiles_here == lax.axis_index("grid")
        out[k * mem_loc : (k + 1) * mem_loc, :] = jnp.where(here, held[k], 0.0)


def piece_columns(d, quarter, first, width):
    return pl.ds(pl.multiple_of((lax.axis_index("mem") ^ d) * quarter + first, TILE), width)


def pack_kernel(parts, quarter, jobs, x_ref, after_ref, *outs):
    del after_ref
    mem_loc = x_ref.shape[0]
    for (d, chunks), out in zip(jobs, outs):
        to = 0
        for first, width in chunks:
            width = width // parts
            for p in range(parts):
                cols = piece_columns(d, quarter, first + p * width, width)
                out[p * mem_loc : (p + 1) * mem_loc, to : to + width] = x_ref[:, cols]
            to += width


def unpack_kernel(parts, quarter, first, pieces, *refs):
    out, held, sem = refs[-3:]
    mem_loc = out.shape[0]
    copies = []
    for i, d in enumerate(pieces):
        width = refs[i].shape[1]
        for p in range(parts):
            held[i, :, p * width : (p + 1) * width] = refs[i][p * mem_loc : (p + 1) * mem_loc, :]
        cols = piece_columns(d, quarter, first, parts * width)
        copies.append(pltpu.make_async_copy(held.at[i], out.at[:, cols], sem.at[i]))
        copies[i].start()
    for copy in copies:
        copy.wait()


def chain_kernel(
    places, tile_ref, order_ref, mask_ref, offset_ref, value_ref, error_ref, one_ref, two_ref, out, slab, rows_ref
):
    members = slab.shape[1]
    mem_loc = members // len(places)
    obs = offset_ref.shape[1]
    for k in range(BLOCKS):
        for i, ref in enumerate((offset_ref, value_ref, error_ref)):
            rows_ref[3 * k + i : 3 * k + i + 1, :] = ref[pl.ds(order_ref[k], 1), :].astype(jnp.float32)
    columns = jnp.transpose(rows_ref[...])
    for i, d in enumerate(places):
        for k in range(BLOCKS):
            rows = slice((i * BLOCKS + k) * mem_loc, (i * BLOCKS + k + 1) * mem_loc)
            slab[k, d * mem_loc : (d + 1) * mem_loc, :] = one_ref[rows, :] + two_ref[rows, :]
    row = lax.broadcasted_iota(jnp.int32, (members, TILE), 0)
    lane = lax.broadcasted_iota(jnp.int32, (members, TILE), 1)
    out[:, 0:TILE] = jnp.where(row == lane, 1.0, 0.0)
    place = lax.broadcasted_iota(jnp.int32, (obs, TILE), 1).astype(jnp.float32)
    for k in range(BLOCKS):
        x = slab[k]
        ybar = jnp.sum(x, axis=0, keepdims=True) / members
        dev = x - ybar
        var = jnp.sum(dev * dev, axis=0, keepdims=True) / (members - 1.0)
        offset, value, error = (columns[:, 3 * k + i : 3 * k + i + 1] for i in range(3))
        hit = offset == place
        total = var + error
        shrink = jnp.where(hit, jnp.sqrt(error / total) - 1.0, 0.0)
        shift = jnp.where(hit, var / total * (value - ybar), 0.0)
        scale = 1.0 / ((members - 1.0) * (var + 1e-05))
        shrink = jnp.sum(shrink, axis=0, keepdims=True) * scale
        shift = jnp.sum(shift, axis=0, keepdims=True) * scale
        centred = dev - jnp.sum(dev, axis=0, keepdims=True) / members
        gain = lax.dot_general(
            dev * shrink + shift,
            centred,
            (((1,), (1,)), ((), ())),
            precision=HIGHEST,
            preferred_element_type=jnp.float32,
        )
        for j in range(k + 1, BLOCKS):
            old = slab[j]
            new = old + jnp.dot(gain, old, precision=HIGHEST, preferred_element_type=jnp.float32)
            used = mask_ref[order_ref[k], tile_ref[order_ref[j]]]
            slab[j] = jnp.where(used == 1, new, old)
        span = TILE << k
        so_far = out[:, 0:span]
        out[:, span : 2 * span] = so_far + jnp.dot(
            gain, so_far, precision=HIGHEST, preferred_element_type=jnp.float32
        )


def apply_kernel(n_mem, parts, quarter, first, starts, order_ref, mask_ref, t_ref, *refs):
    pieces, outs = refs[:n_mem], refs[n_mem : 2 * n_mem]
    mem_loc = pieces[0].shape[0] // parts
    members = mem_loc * n_mem
    tiles = outs[0].shape[1] // TILE
    base = (lax.axis_index("grid") * n_mem + lax.axis_index("mem")) * (quarter // TILE) + first // TILE
    for p in range(parts):
        rows = slice(p * mem_loc, (p + 1) * mem_loc)
        for t in range(tiles):
            cols = slice(t * TILE, (t + 1) * TILE)
            x = jnp.concatenate(
                [piece[rows, start + t * TILE : start + (t + 1) * TILE] for piece, start in zip(pieces, starts)],
                axis=0,
            )
            code = 0
            for k in range(BLOCKS):
                code = code + (mask_ref[order_ref[k], base + p * tiles + t] << k)
            matrix = t_ref[:, pl.ds(pl.multiple_of(code * TILE, TILE), TILE)][:, 0:members]
            y = jnp.dot(matrix, x, precision=HIGHEST, preferred_element_type=jnp.float32)
            for d in range(n_mem):
                outs[d][rows, cols] = y[d * mem_loc : (d + 1) * mem_loc, :]


def on_device(state, obs_tile, obs_offset, obs_value, obs_error, loc_mask, block_order):
    f32 = jnp.float32
    n_mem = lax.axis_size("mem")
    n_grid = lax.axis_size("grid")
    mem_loc, grid_width = state.shape
    members = mem_loc * n_mem
    quarter = grid_width // n_mem
    parts = 8 // math.gcd(mem_loc, 8)
    obs = obs_value.shape[1]
    unit = parts * TILE
    half = quarter // unit * 8 // 16 * unit
    firsts = (0, half)
    widths = (half, quarter - half)
    pieces = [jax.ShapeDtypeStruct((parts * mem_loc, width // parts), f32) for width in widths]

    def swap(value, axis, by):
        return lax.ppermute(value, axis, [(j, j ^ by) for j in range(lax.axis_size(axis))])

    def pack(jobs, after):
        chunks = [(d, [(firsts[c], widths[c]) for c in which]) for d, which in jobs]
        total = [sum(width for _, width in each) for _, each in chunks]
        return kernel_call(
            functools.partial(pack_kernel, parts, quarter, chunks),
            "pack",
            [jax.ShapeDtypeStruct((parts * mem_loc, width // parts), f32) for width in total],
            [VMEM, ANY],
            [VMEM] * len(jobs),
        )(state, after)

    def update_matrices(slab):
        hop = 1
        while True:
            other = swap(slab, "grid", hop)
            hop *= 2
            if hop >= n_grid:
                break
            slab = slab + other
        return kernel_call(
            functools.partial(chain_kernel, places),
            "chain",
            jax.ShapeDtypeStruct((members, TILE << BLOCKS), f32),
            [SMEM] * 3 + [VMEM] * 5,
            VMEM,
            [pltpu.VMEM((BLOCKS, members, TILE), f32), pltpu.VMEM((TILE, obs), f32)],
        )(obs_tile, block_order, loc_mask, obs_offset, obs_value, obs_error, slab, other)

    def no_updates(slab):
        return jnp.tile(jnp.eye(members, TILE, dtype=f32), (1, 1 << BLOCKS))

    mine = kernel_call(
        seen_kernel,
        "seen",
        jax.ShapeDtypeStruct((BLOCKS * mem_loc, TILE), f32),
        [HBM] * 3,
        VMEM,
        [
            pltpu.SMEM((BLOCKS,), jnp.int32),
            pltpu.SMEM((BLOCKS,), jnp.int32),
            pltpu.VMEM((BLOCKS, mem_loc, TILE), f32),
            pltpu.SemaphoreType.DMA((BLOCKS,)),
        ],
        vmem=12,
    )(obs_tile, block_order, state)
    places = range(n_mem)
    seen = [mine] + [swap(mine, "mem", d) for d in places[1:]]
    slab = jnp.concatenate(seen, axis=0)
    held = {}

    def start(jobs, after):
        for job, value in zip(jobs, pack(jobs, after)):
            held[job] = swap(value, "mem", job[0]) if job[0] else value

    start([(d, (0, 1)) for d in range(n_mem - 1)] + [(n_mem - 1, (0,))], slab)
    matrices = lax.cond(jnp.any(loc_mask > 0), update_matrices, no_updates, slab)
    start([(n_mem - 1, (1,))], matrices)
    arrived, starts = [], []
    for c in range(2):
        arrived.append([held.get((d, (c,)), held.get((d, (0, 1)))) for d in range(n_mem)])
        starts.append([0 if (d, (c,)) in held else firsts[c] // parts for d in range(n_mem)])
    result = []
    for c in range(2):
        updated = kernel_call(
            functools.partial(apply_kernel, n_mem, parts, quarter, firsts[c], starts[c]),
            "apply",
            [pieces[c]] * n_mem,
            [SMEM] * 2 + [VMEM] * (1 + n_mem),
            [VMEM] * n_mem,
        )(block_order, loc_mask, matrices, *arrived[c])
        back = [updated[0]] + [swap(updated[d], "mem", d) for d in range(1, n_mem)]
        result = kernel_call(
            functools.partial(unpack_kernel, parts, quarter, firsts[c], range(n_mem)),
            "unpack",
            [jax.ShapeDtypeStruct(state.shape, f32)],
            [VMEM] * n_mem + [HBM] * len(result),
            [HBM],
            [pltpu.VMEM((n_mem, mem_loc, widths[c]), f32), pltpu.SemaphoreType.DMA((n_mem,))],
            {n_mem: 0} if result else None,
        )(*back, *result)
    return result[0]


def solution(mesh):
    placed = (P("mem", "grid"), P(), P(), P(), P(), P(), P())
    return jax.shard_map(
        on_device, mesh=mesh, in_specs=placed, out_specs=P("mem", "grid"), check_vma=False
    )
```

time: 79.9 us -> 72.6 us (0.909)
  waiting for transfers between devices: 16 us -> 33.8 us
  blocking collectives: 11.3 us -> 0 us
  Pallas kernels: 20.5 us -> 10.3 us
  starting transfers between devices: 29.5 us -> 23.9 us
  other arithmetic: 0 us -> 1.61 us
    ppermute x15 -> x16, waiting for transfers between devices: 16 us -> 33.8 us  [swap(): lax.ppermute(value, axis, [(j, j ^ by) for j in range(lax.axis_size(axis))])]
    all_gather x1 -> x0, blocking collectives: 11.3 us -> none  [on_device(): gathered = lax.all_gather(mine, 'grid', axis=0)]
    pallas_call x7 -> x8, Pallas kernels: 20.5 us -> 10.3 us  [the longest x1 4.36 us: update_matrices(): kernel_call(functools.partial(chain_kernel, places), 'chain', jax.ShapeDt...]
    ppermute x15 -> x16, starting transfers between devices: 29.5 us -> 23.9 us  [swap(): lax.ppermute(value, axis, [(j, j ^ by) for j in range(lax.axis_size(axis))])]
    add x0 -> x2, other arithmetic: none -> 0.96 us  [update_matrices(): slab = slab + other]
    unnamed x30 -> x12, local copies, waits for them, and re-layouts: 2.14 us -> 1.96 us
  transfers between devices with their start and end apart: 15 -> 16, of which waited for: 5 -> 9; matrix products, arithmetic and copies ran while one was open for 0% -> 2% of each run, Pallas kernels for 19% -> 12%
where the time goes in v3:
time: 72.6 us; the launch traced here: 72.3 us
  waiting for transfers between devices  33.8 us (47%)
  starting transfers between devices  23.9 us (33%)
  Pallas kernels  10.3 us (14%)
  local copies, waits for them, and re-layouts  1.96 us (3%)
  other arithmetic  1.61 us (2%)
  between operations  0.77 us (1%)
    ppermute x16, waiting for transfers between devices, swap(): lax.ppermute(value, axis, [(j, j ^ by) for j in range(lax.axis_size(axis))])  33.8 us
    ppermute x16, starting transfers between devices, swap(): lax.ppermute(value, axis, [(j, j ^ by) for j in range(lax.axis_size(axis))])  23.9 us
    pallas_call x1, Pallas kernels, update_matrices(): kernel_call(functools.partial(chain_kernel, places), 'chain', jax.ShapeDt...  4.36 us
    pallas_call x2, Pallas kernels, on_device(): kernel_call(functools.partial(apply_kernel, n_mem, parts, quarter, firsts...  3.03 us
    unnamed x12, local copies, waits for them, and re-layouts  1.96 us
    pallas_call x2, Pallas kernels, on_device(): kernel_call(functools.partial(unpack_kernel, parts, quarter, firsts[c], r...  1.86 us
  transfers between devices with their start and end apart: 16, of which 9 were waited for; matrix products, arithmetic and copies ran while one was open for 2% of the time, Pallas kernels for 12%

profile of v3, /device:TPU:0, one launch (start us, length us, event | category | flops | bytes accessed | tf_op | source)
XLA Modules:
  0.0 72.3 jit_solution(9376440535209614199)
XLA Ops:
  0.0 1.4 %copy-done = f32[20,16384]{1,0:T(8,128)S(1)} copy-done((f32[20,16384]{1,0:T(8,128)S(1)}, f32[20,16384]{1,0:T(8,128)}, u32[]{:S(2)}) %copy-start) | copy-done | bytes 1310744
  1.4 0.9 %seen.1 = f32[80,128]{1,0:T(8,128)S(1)} custom-call(s32[4]{0:T(128)} %tile_ref.1, s32[4]{0:T(128)} %order_ref.5, f32[20,16384]{1,0:T(8,128)S(1)} %copy-done), custom_call_target="tpu_custom_call" | custom-call | tf_op jit(solution)/shard_map/seen/pallas_call | solution.py:214
  2.3 5.1 %collective-permute-start.5 = (f32[80,128]{1,0:T(8,128)S(1)}, f32[80,128]{1,0:T(8,128)S(1)}, u32[]{:S(2)}, u32[]{:S(2)}) collective-permute-start(f32[80,128]{1,0:T(8,128)S(1)} %seen.1), channel_id=1, source_target_pairs={{0,24},{8,16},{16,8},{24,0},{1,25},{9,17},{17,9},{25,1},{2,26},{10... | collective-permute-start | bytes 122888 | tf_op jit(solution)/shard_map/ppermute | solution.py:181
  7.5 0.6 collective-permute-start.3
  8.1 1.4 %collective-permute-done.5 = f32[80,128]{1,0:T(8,128)S(1)} collective-permute-done((f32[80,128]{1,0:T(8,128)S(1)}, f32[80,128]{1,0:T(8,128)S(1)}, u32[]{:S(2)}, u32[]{:S(2)}) %collective-permute-start.5) | collective-permute-done | bytes 40992 | tf_op jit(solution)/shard_map/ppermute | solution.py:181
  9.5 2.9 %collective-permute-done.4 = f32[80,128]{1,0:T(8,128)S(1)} collective-permute-done((f32[80,128]{1,0:T(8,128)S(1)}, f32[80,128]{1,0:T(8,128)S(1)}, u32[]{:S(2)}, u32[]{:S(2)}) %collective-permute-start.4) | collective-permute-done | bytes 40992 | tf_op jit(solution)/shard_map/ppermute | solution.py:181
  12.5 0.5 copy-done.3
  13.2 2.0 %collective-permute-start.7 = (f32[40,2048]{1,0:T(8,128)S(1)}, f32[40,2048]{1,0:T(8,128)S(1)}, u32[]{:S(2)}, u32[]{:S(2)}) collective-permute-start(f32[40,2048]{1,0:T(8,128)S(1)} %get-tuple-element.43), channel_id=1, source_target_pairs={{0,16},{8,24},{16,0},{24,8},{1,17},{9,25},{17,1},{25,9},{2,18},{10... | collective-permute-start | bytes 983048 | tf_op jit(solution)/shard_map/ppermute | solution.py:181
  15.2 2.2 %collective-permute-start.12 = (f32[40,1024]{1,0:T(8,128)S(1)}, f32[40,1024]{1,0:T(8,128)S(1)}, u32[]{:S(2)}, u32[]{:S(2)}) collective-permute-start(f32[40,1024]{1,0:T(8,128)S(1)} %get-tuple-element.48), channel_id=1, source_target_pairs={{0,24},{8,16},{16,8},{24,0},{1,25},{9,17},{17,9},{25,1},{2,26},{10... | collective-permute-start | bytes 491528 | tf_op jit(solution)/shard_map/ppermute | solution.py:181
  17.4 0.6 compare_reduce_fusion
  18.7 18.8 %conditional.1 = (f32[80,2048]{1,0:T(8,128)}) conditional(s32[]{:T(128)} %convert_element_type.10, () %tuple.11, (f32[320,128]{1,0:T(8,128)}, s32[4]{0:T(128)}, s32[4]{0:T(128)}, s32[4,1024]{1,0:T(4,128)S(1)}, s32[4,256]{1,0:T(4,128)}, /*index=5*/f32[4,256]{1,0:T(4,128)}, f32[4,256]{1,0:T(4,128)}) %tuple.16), branch_computations={%region_1.0_spmd, %region_2.0_spmd} | conditional | flops 81920 | bytes 2949248 | solution.py:238
  18.8 1.6 %collective-permute-done = f32[320,128]{1,0:T(8,128)S(1)} collective-permute-done((f32[320,128]{1,0:T(8,128)}, f32[320,128]{1,0:T(8,128)S(1)}, u32[]{:S(2)}, u32[]{:S(2)}) %collective-permute-start) | collective-permute-done | bytes 163872 | tf_op jit(solution)/shard_map/cond/branch_1_fun/ppermute | solution.py:181
  20.4 0.9 %add.4 = f32[320,128]{1,0:T(8,128)S(1)} add(f32[320,128]{1,0:T(8,128)} %get-tuple-element.28, f32[320,128]{1,0:T(8,128)S(1)} %collective-permute-done) | non-fusion elementwise | flops 40960 | bytes 491520 | tf_op jit(solution)/shard_map/cond/branch_1_fun/add | solution.py:201
  21.4 1.6 %collective-permute-start.1 = (f32[320,128]{1,0:T(8,128)S(1)}, f32[320,128]{1,0:T(8,128)S(1)}, u32[]{:S(2)}, u32[]{:S(2)}) collective-permute-start(f32[320,128]{1,0:T(8,128)S(1)} %add.4), channel_id=1, source_target_pairs={{0,2},{1,3},{2,0},{3,1},{4,6},{5,7},{6,4},{7,5},{8,10},{9,11},{10,... | collective-permute-start | bytes 491528 | tf_op jit(solution)/shard_map/cond/branch_1_fun/ppermute | solution.py:181
  22.9 4.8 %collective-permute-done.1 = f32[320,128]{1,0:T(8,128)S(1)} collective-permute-done((f32[320,128]{1,0:T(8,128)S(1)}, f32[320,128]{1,0:T(8,128)S(1)}, u32[]{:S(2)}, u32[]{:S(2)}) %collective-permute-start.1) | collective-permute-done | bytes 163872 | tf_op jit(solution)/shard_map/cond/branch_1_fun/ppermute | solution.py:181
  27.7 1.6 %collective-permute-start.2 = (f32[320,128]{1,0:T(8,128)S(1)}, f32[320,128]{1,0:T(8,128)S(1)}, u32[]{:S(2)}, u32[]{:S(2)}) collective-permute-start(f32[320,128]{1,0:T(8,128)S(1)} %add.5.one_ref), channel_id=1, source_target_pairs={{0,4},{1,5},{2,6},{3,7},{4,0},{5,1},{6,2},{7,3},{8,12},{9,13},{10,... | collective-permute-start | bytes 491528 | tf_op jit(solution)/shard_map/cond/branch_1_fun/ppermute | solution.py:181
  29.3 3.9 %collective-permute-done.2.two_ref = f32[320,128]{1,0:T(8,128)S(1)} collective-permute-done((f32[320,128]{1,0:T(8,128)S(1)}, f32[320,128]{1,0:T(8,128)S(1)}, u32[]{:S(2)}, u32[]{:S(2)}) %collective-permute-start.2) | collective-permute-done | bytes 163872 | tf_op jit(solution)/shard_map/cond/branch_1_fun/ppermute | solution.py:181
  33.2 4.4 %chain.1 = f32[80,2048]{1,0:T(8,128)} custom-call(s32[4]{0:T(128)} %get-tuple-element.22.tile_ref, s32[4]{0:T(128)} %get-tuple-element.23.order_ref, s32[4,1024]{1,0:T(4,128)S(1)} %get-tuple-element.24.mask_ref, s32[4,256]{1,0:T(4,128)} %get-tuple-element.56.offset_ref, f32[4,256]{1,0:T(4,128)} %get-tuple-element.57.value_ref, ...), custom_call_target="tpu_custom_call" | custom-call | tf_op jit(solution)/shard_map/cond/branch_1_fun/chain/pallas_call | solution.py:202
  37.6 1.6 %collective-permute-start.8 = (f32[40,1024]{1,0:T(8,128)S(1)}, f32[40,1024]{1,0:T(8,128)S(1)}, u32[]{:S(2)}, u32[]{:S(2)}) collective-permute-start(f32[40,1024]{1,0:T(8,128)S(1)} %pack.3), channel_id=1, source_target_pairs={{0,24},{8,16},{16,8},{24,0},{1,25},{9,17},{17,9},{25,1},{2,26},{10... | collective-permute-start | bytes 491528 | tf_op jit(solution)/shard_map/ppermute | solution.py:181
  39.3 1.5 %apply.3 = (f32[40,1024]{1,0:T(8,128)S(1)}, f32[40,1024]{1,0:T(8,128)S(1)}, f32[40,1024]{1,0:T(8,128)S(1)}, f32[40,1024]{1,0:T(8,128)S(1)}) custom-call(s32[4]{0:T(128)S(1)} %copy-done.5, s32[4,1024]{1,0:T(4,128)S(1)} %copy-done.4, f32[80,2048]{1,0:T(8,128)S(1)} %copy-done.2, f32[40,2048]{1,0:T(8,128)S(1)} %get-tuple-element.41.refs_0_, ...), custom_call_target="tpu_custom_call" | custom-call | tf_op jit(solution)/shard_map/apply/pallas_call | solution.py:246
  41.0 2.7 %collective-permute-start.14 = (f32[40,1024]{1,0:T(8,128)S(1)}, f32[40,1024]{1,0:T(8,128)S(1)}, u32[]{:S(2)}, u32[]{:S(2)}) collective-permute-start(f32[40,1024]{1,0:T(8,128)S(1)} %get-tuple-element.51), channel_id=1, source_target_pairs={{0,16},{8,24},{16,0},{24,8},{1,17},{9,25},{17,1},{25,9},{2,18},{10... | collective-permute-start | bytes 491528 | tf_op jit(solution)/shard_map/ppermute | solution.py:181
  43.7 1.6 %collective-permute-start.15 = (f32[40,1024]{1,0:T(8,128)S(1)}, f32[40,1024]{1,0:T(8,128)S(1)}, u32[]{:S(2)}, u32[]{:S(2)}) collective-permute-start(f32[40,1024]{1,0:T(8,128)S(1)} %get-tuple-element.52), channel_id=1, source_target_pairs={{0,24},{8,16},{16,8},{24,0},{1,25},{9,17},{17,9},{25,1},{2,26},{10... | collective-permute-start | bytes 491528 | tf_op jit(solution)/shard_map/ppermute | solution.py:181
  45.2 1.5 %collective-permute-done.8.refs_3_ = f32[40,1024]{1,0:T(8,128)S(1)} collective-permute-done((f32[40,1024]{1,0:T(8,128)S(1)}, f32[40,1024]{1,0:T(8,128)S(1)}, u32[]{:S(2)}, u32[]{:S(2)}) %collective-permute-start.8) | collective-permute-done | bytes 163872 | tf_op jit(solution)/shard_map/ppermute | solution.py:181
  46.7 1.5 %apply.2 = (f32[40,1024]{1,0:T(8,128)S(1)}, f32[40,1024]{1,0:T(8,128)S(1)}, f32[40,1024]{1,0:T(8,128)S(1)}, f32[40,1024]{1,0:T(8,128)S(1)}) custom-call(s32[4]{0:T(128)S(1)} %copy-done.5, s32[4,1024]{1,0:T(4,128)S(1)} %copy-done.4, f32[80,2048]{1,0:T(8,128)S(1)} %copy-done.2, f32[40,2048]{1,0:T(8,128)S(1)} %get-tuple-element.41.refs_0_, ...), custom_call_target="tpu_custom_call" | custom-call | tf_op jit(solution)/shard_map/apply/pallas_call | solution.py:246
  48.2 2.6 %collective-permute-start.9 = (f32[40,1024]{1,0:T(8,128)S(1)}, f32[40,1024]{1,0:T(8,128)S(1)}, u32[]{:S(2)}, u32[]{:S(2)}) collective-permute-start(f32[40,1024]{1,0:T(8,128)S(1)} %get-tuple-element.45), channel_id=1, source_target_pairs={{0,8},{8,0},{16,24},{24,16},{1,9},{9,1},{17,25},{25,17},{2,10},{10... | collective-permute-start | bytes 491528 | tf_op jit(solution)/shard_map/ppermute | solution.py:181
  50.8 1.0 %collective-permute-start.10 = (f32[40,1024]{1,0:T(8,128)S(1)}, f32[40,1024]{1,0:T(8,128)S(1)}, u32[]{:S(2)}, u32[]{:S(2)}) collective-permute-start(f32[40,1024]{1,0:T(8,128)S(1)} %get-tuple-element.46), channel_id=1, source_target_pairs={{0,16},{8,24},{16,0},{24,8},{1,17},{9,25},{17,1},{25,9},{2,18},{10... | collective-permute-start | bytes 491528 | tf_op jit(solution)/shard_map/ppermute | solution.py:181
  51.9 0.6 collective-permute-done.13.refs_1_
  52.5 0.8 %collective-permute-start.11 = (f32[40,1024]{1,0:T(8,128)S(1)}, f32[40,1024]{1,0:T(8,128)S(1)}, u32[]{:S(2)}, u32[]{:S(2)}) collective-permute-start(f32[40,1024]{1,0:T(8,128)S(1)} %get-tuple-element.47), channel_id=1, source_target_pairs={{0,24},{8,16},{16,8},{24,0},{1,25},{9,17},{17,9},{25,1},{2,26},{10... | collective-permute-start | bytes 491528 | tf_op jit(solution)/shard_map/ppermute | solution.py:181
  53.3 5.9 %collective-permute-done.14.refs_2_ = f32[40,1024]{1,0:T(8,128)S(1)} collective-permute-done((f32[40,1024]{1,0:T(8,128)S(1)}, f32[40,1024]{1,0:T(8,128)S(1)}, u32[]{:S(2)}, u32[]{:S(2)}) %collective-permute-start.14) | collective-permute-done | bytes 163872 | tf_op jit(solution)/shard_map/ppermute | solution.py:181
  59.2 0.9 %unpack.2.refs_4_ = f32[20,16384]{1,0:T(8,128)} custom-call(f32[40,1024]{1,0:T(8,128)S(1)} %get-tuple-element.49.refs_0_, f32[40,1024]{1,0:T(8,128)S(1)} %collective-permute-done.13.refs_1_, f32[40,1024]{1,0:T(8,128)S(1)} %collective-permute-done.14.refs_2_, f32[40,1024]{1,0:T(8,128)S(1)} %collective-permute-done.15.refs_3_), custom_call_target="tpu_custom_call" | custom-call | tf_op jit(solution)/shard_map/unpack/pallas_call | solution.py:254
  60.2 11.2 %collective-permute-done.10.refs_2_ = f32[40,1024]{1,0:T(8,128)S(1)} collective-permute-done((f32[40,1024]{1,0:T(8,128)S(1)}, f32[40,1024]{1,0:T(8,128)S(1)}, u32[]{:S(2)}, u32[]{:S(2)}) %collective-permute-start.10) | collective-permute-done | bytes 163872 | tf_op jit(solution)/shard_map/ppermute | solution.py:181
  71.4 0.9 %unpack.3 = f32[20,16384]{1,0:T(8,128)} custom-call(f32[40,1024]{1,0:T(8,128)S(1)} %get-tuple-element.44.refs_0_, f32[40,1024]{1,0:T(8,128)S(1)} %collective-permute-done.9.refs_1_, f32[40,1024]{1,0:T(8,128)S(1)} %collective-permute-done.10.refs_2_, f32[40,1024]{1,0:T(8,128)S(1)} %collective-permute-done.11.refs_3_, ...), custom_call_target="tpu_custom_call", output_to_operand_aliasing={{}: (4, {})} | custom-call | tf_op jit(solution)/shard_map/unpack/pallas_call | solution.py:254
  (25 shorter events, 0.6 us)
Async XLA Ops:
  0.0 1.4 %copy-start = (f32[20,16384]{1,0:T(8,128)S(1)}, f32[20,16384]{1,0:T(8,128)}, u32[]{:S(2)}) copy-start(f32[20,16384]{1,0:T(8,128)} %x_ref.5) | copy-start | bytes 3932164
  1.4 16.0 %copy-start.4 = (s32[4,1024]{1,0:T(4,128)S(1)}, s32[4,1024]{1,0:T(4,128)}, u32[]{:S(2)}) copy-start(s32[4,1024]{1,0:T(4,128)} %mask_ref.3) | copy-start | bytes 49156
  2.3 7.1 %collective-permute-start.5 = (f32[80,128]{1,0:T(8,128)S(1)}, f32[80,128]{1,0:T(8,128)S(1)}, u32[]{:S(2)}, u32[]{:S(2)}) collective-permute-start(f32[80,128]{1,0:T(8,128)S(1)} %seen.1), channel_id=1, source_target_pairs={{0,24},{8,16},{16,8},{24,0},{1,25},{9,17},{17,9},{25,1},{2,26},{10... | collective-permute-start | bytes 122888 | tf_op jit(solution)/shard_map/ppermute | solution.py:181
  7.5 4.9 %collective-permute-start.4 = (f32[80,128]{1,0:T(8,128)S(1)}, f32[80,128]{1,0:T(8,128)S(1)}, u32[]{:S(2)}, u32[]{:S(2)}) collective-permute-start(f32[80,128]{1,0:T(8,128)S(1)} %seen.1), channel_id=1, source_target_pairs={{0,16},{8,24},{16,0},{24,8},{1,17},{9,25},{17,1},{25,9},{2,18},{10... | collective-permute-start | bytes 122888 | tf_op jit(solution)/shard_map/ppermute | solution.py:181
  7.5 4.9 %collective-permute-start.3 = (f32[80,128]{1,0:T(8,128)S(1)}, f32[80,128]{1,0:T(8,128)S(1)}, u32[]{:S(2)}, u32[]{:S(2)}) collective-permute-start(f32[80,128]{1,0:T(8,128)S(1)} %seen.1), channel_id=1, source_target_pairs={{0,8},{8,0},{16,24},{24,16},{1,9},{9,1},{17,25},{25,17},{2,10},{10... | collective-permute-start | bytes 122888 | tf_op jit(solution)/shard_map/ppermute | solution.py:181
  12.4 0.7 copy-start.3
  13.0 26.2 %collective-permute-start.6 = (f32[40,2048]{1,0:T(8,128)S(1)}, f32[40,2048]{1,0:T(8,128)S(1)}, u32[]{:S(2)}, u32[]{:S(2)}) collective-permute-start(f32[40,2048]{1,0:T(8,128)S(1)} %get-tuple-element.42), channel_id=1, source_target_pairs={{0,8},{8,0},{16,24},{24,16},{1,9},{9,1},{17,25},{25,17},{2,10},{10... | collective-permute-start | bytes 983048 | tf_op jit(solution)/shard_map/ppermute | solution.py:181
  13.2 26.1 %collective-permute-start.7 = (f32[40,2048]{1,0:T(8,128)S(1)}, f32[40,2048]{1,0:T(8,128)S(1)}, u32[]{:S(2)}, u32[]{:S(2)}) collective-permute-start(f32[40,2048]{1,0:T(8,128)S(1)} %get-tuple-element.43), channel_id=1, source_target_pairs={{0,16},{8,24},{16,0},{24,8},{1,17},{9,25},{17,1},{25,9},{2,18},{10... | collective-permute-start | bytes 983048 | tf_op jit(solution)/shard_map/ppermute | solution.py:181
  15.2 24.1 %collective-permute-start.12 = (f32[40,1024]{1,0:T(8,128)S(1)}, f32[40,1024]{1,0:T(8,128)S(1)}, u32[]{:S(2)}, u32[]{:S(2)}) collective-permute-start(f32[40,1024]{1,0:T(8,128)S(1)} %get-tuple-element.48), channel_id=1, source_target_pairs={{0,24},{8,16},{16,8},{24,0},{1,25},{9,17},{17,9},{25,1},{2,26},{10... | collective-permute-start | bytes 491528 | tf_op jit(solution)/shard_map/ppermute | solution.py:181
  18.7 18.8 %copy-start.1 = (f32[20,16384]{1,0:T(8,128)S(1)}, f32[20,16384]{1,0:T(8,128)}, u32[]{:S(2)}) copy-start(f32[20,16384]{1,0:T(8,128)} %x_ref.5) | copy-start | bytes 3932164
  18.8 1.7 %collective-permute-start = (f32[320,128]{1,0:T(8,128)}, f32[320,128]{1,0:T(8,128)S(1)}, u32[]{:S(2)}, u32[]{:S(2)}) collective-permute-start(f32[320,128]{1,0:T(8,128)} %get-tuple-element.28), channel_id=1, source_target_pairs={{0,1},{1,0},{2,3},{3,2},{4,5},{5,4},{6,7},{7,6},{8,9},{9,8},{10,11... | collective-permute-start | bytes 491528 | tf_op jit(solution)/shard_map/cond/branch_1_fun/ppermute | solution.py:181
  21.4 6.3 %collective-permute-start.1 = (f32[320,128]{1,0:T(8,128)S(1)}, f32[320,128]{1,0:T(8,128)S(1)}, u32[]{:S(2)}, u32[]{:S(2)}) collective-permute-start(f32[320,128]{1,0:T(8,128)S(1)} %add.4), channel_id=1, source_target_pairs={{0,2},{1,3},{2,0},{3,1},{4,6},{5,7},{6,4},{7,5},{8,10},{9,11},{10,... | collective-permute-start | bytes 491528 | tf_op jit(solution)/shard_map/cond/branch_1_fun/ppermute | solution.py:181
  27.7 5.5 %collective-permute-start.2 = (f32[320,128]{1,0:T(8,128)S(1)}, f32[320,128]{1,0:T(8,128)S(1)}, u32[]{:S(2)}, u32[]{:S(2)}) collective-permute-start(f32[320,128]{1,0:T(8,128)S(1)} %add.5.one_ref), channel_id=1, source_target_pairs={{0,4},{1,5},{2,6},{3,7},{4,0},{5,1},{6,2},{7,3},{8,12},{9,13},{10,... | collective-permute-start | bytes 491528 | tf_op jit(solution)/shard_map/cond/branch_1_fun/ppermute | solution.py:181
  37.5 1.7 %copy-start.2 = (f32[80,2048]{1,0:T(8,128)S(1)}, f32[80,2048]{1,0:T(8,128)}, u32[]{:S(2)}) copy-start(f32[80,2048]{1,0:T(8,128)} %get-tuple-element.59.after_ref.t_ref) | copy-start | bytes 1966084
  37.6 1.7 %copy-start.5 = (s32[4]{0:T(128)S(1)}, s32[4]{0:T(128)}, u32[]{:S(2)}) copy-start(s32[4]{0:T(128)} %order_ref.5) | copy-start | bytes 52
  37.6 9.1 %collective-permute-start.8 = (f32[40,1024]{1,0:T(8,128)S(1)}, f32[40,1024]{1,0:T(8,128)S(1)}, u32[]{:S(2)}, u32[]{:S(2)}) collective-permute-start(f32[40,1024]{1,0:T(8,128)S(1)} %pack.3), channel_id=1, source_target_pairs={{0,24},{8,16},{16,8},{24,0},{1,25},{9,17},{17,9},{25,1},{2,26},{10... | collective-permute-start | bytes 491528 | tf_op jit(solution)/shard_map/ppermute | solution.py:181
  40.8 11.7 %collective-permute-start.13 = (f32[40,1024]{1,0:T(8,128)S(1)}, f32[40,1024]{1,0:T(8,128)S(1)}, u32[]{:S(2)}, u32[]{:S(2)}) collective-permute-start(f32[40,1024]{1,0:T(8,128)S(1)} %get-tuple-element.50), channel_id=1, source_target_pairs={{0,8},{8,0},{16,24},{24,16},{1,9},{9,1},{17,25},{25,17},{2,10},{10... | collective-permute-start | bytes 491528 | tf_op jit(solution)/shard_map/ppermute | solution.py:181
  41.0 18.2 %collective-permute-start.14 = (f32[40,1024]{1,0:T(8,128)S(1)}, f32[40,1024]{1,0:T(8,128)S(1)}, u32[]{:S(2)}, u32[]{:S(2)}) collective-permute-start(f32[40,1024]{1,0:T(8,128)S(1)} %get-tuple-element.51), channel_id=1, source_target_pairs={{0,16},{8,24},{16,0},{24,8},{1,17},{9,25},{17,1},{25,9},{2,18},{10... | collective-permute-start | bytes 491528 | tf_op jit(solution)/shard_map/ppermute | solution.py:181
  43.7 15.5 %collective-permute-start.15 = (f32[40,1024]{1,0:T(8,128)S(1)}, f32[40,1024]{1,0:T(8,128)S(1)}, u32[]{:S(2)}, u32[]{:S(2)}) collective-permute-start(f32[40,1024]{1,0:T(8,128)S(1)} %get-tuple-element.52), channel_id=1, source_target_pairs={{0,24},{8,16},{16,8},{24,0},{1,25},{9,17},{17,9},{25,1},{2,26},{10... | collective-permute-start | bytes 491528 | tf_op jit(solution)/shard_map/ppermute | solution.py:181
  48.2 11.9 %collective-permute-start.9 = (f32[40,1024]{1,0:T(8,128)S(1)}, f32[40,1024]{1,0:T(8,128)S(1)}, u32[]{:S(2)}, u32[]{:S(2)}) collective-permute-start(f32[40,1024]{1,0:T(8,128)S(1)} %get-tuple-element.45), channel_id=1, source_target_pairs={{0,8},{8,0},{16,24},{24,16},{1,9},{9,1},{17,25},{25,17},{2,10},{10... | collective-permute-start | bytes 491528 | tf_op jit(solution)/shard_map/ppermute | solution.py:181
  50.8 20.6 %collective-permute-start.10 = (f32[40,1024]{1,0:T(8,128)S(1)}, f32[40,1024]{1,0:T(8,128)S(1)}, u32[]{:S(2)}, u32[]{:S(2)}) collective-permute-start(f32[40,1024]{1,0:T(8,128)S(1)} %get-tuple-element.46), channel_id=1, source_target_pairs={{0,16},{8,24},{16,0},{24,8},{1,17},{9,25},{17,1},{25,9},{2,18},{10... | collective-permute-start | bytes 491528 | tf_op jit(solution)/shard_map/ppermute | solution.py:181
  52.5 18.9 %collective-permute-start.11 = (f32[40,1024]{1,0:T(8,128)S(1)}, f32[40,1024]{1,0:T(8,128)S(1)}, u32[]{:S(2)}, u32[]{:S(2)}) collective-permute-start(f32[40,1024]{1,0:T(8,128)S(1)} %get-tuple-element.47), channel_id=1, source_target_pairs={{0,24},{8,16},{16,8},{24,0},{1,25},{9,17},{17,9},{25,1},{2,26},{10... | collective-permute-start | bytes 491528 | tf_op jit(solution)/shard_map/ppermute | solution.py:181

commit v4 on v3

--- a/solution.py
+++ b/solution.py
@@ -37,7 +37,7 @@
         copy.wait()
 
 
-def seen_kernel(tile_ref, order_ref, x_ref, out, tile, order, held, sem):
+def seen_kernel(tile_ref, order_ref, x_ref, out, tile, order, sem):
     mem_loc, grid_width = x_ref.shape
     tiles_here = grid_width // TILE
     run_all(
@@ -46,22 +46,19 @@
             pltpu.make_async_copy(order_ref, order, sem.at[1]),
         ]
     )
-    copies = []
     for k in range(BLOCKS):
-        col = pl.multiple_of(lax.rem(tile[order[k]], tiles_here) * TILE, TILE)
-        copies.append(pltpu.make_async_copy(x_ref.at[:, pl.ds(col, TILE)], held.at[k], sem.at[k]))
-    run_all(copies)
-    for k in range(BLOCKS):
-        here = tile[order[k]] // tiles_here == lax.axis_index("grid")
-        out[k * mem_loc : (k + 1) * mem_loc, :] = jnp.where(here, held[k], 0.0)
+        at = tile[order[k]]
+        cols = pl.ds(pl.multiple_of(lax.rem(at, tiles_here) * TILE, TILE), TILE)
+        here = at // tiles_here == lax.axis_index("grid")
+        out[k * mem_loc : (k + 1) * mem_loc, :] = jnp.where(here, x_ref[:, cols], 0.0)
 
 
 def piece_columns(d, quarter, first, width):
     return pl.ds(pl.multiple_of((lax.axis_index("mem") ^ d) * quarter + first, TILE), width)
 
 
-def pack_kernel(parts, quarter, jobs, x_ref, after_ref, *outs):
-    del after_ref
+def pack_kernel(parts, quarter, jobs, x_ref, *refs):
+    outs = refs[-len(jobs) :]
     mem_loc = x_ref.shape[0]
     for (d, chunks), out in zip(jobs, outs):
         to = 0
@@ -73,19 +70,31 @@
             to += width
 
 
-def unpack_kernel(parts, quarter, first, pieces, *refs):
+def unpack_kernel(parts, quarter, chunks, n_mem, *refs):
     out, held, sem = refs[-3:]
     mem_loc = out.shape[0]
     copies = []
-    for i, d in enumerate(pieces):
-        width = refs[i].shape[1]
-        for p in range(parts):
-            held[i, :, p * width : (p + 1) * width] = refs[i][p * mem_loc : (p + 1) * mem_loc, :]
-        cols = piece_columns(d, quarter, first, parts * width)
-        copies.append(pltpu.make_async_copy(held.at[i], out.at[:, cols], sem.at[i]))
-        copies[i].start()
+    for d in range(n_mem):
+        at = 0
+        for first, width in chunks:
+            side = width // parts
+            for p in range(parts):
+                part = refs[d][p * mem_loc : (p + 1) * mem_loc, at // parts : at // parts + side]
+                held[d, :, at + p * side : at + (p + 1) * side] = part
+            at += width
+        first, total = chunks[0][0], sum(width for _, width in chunks)
+        copies.append(
+            pltpu.make_async_copy(held.at[d], out.at[:, piece_columns(d, quarter, first, total)], sem.at[d])
+        )
+        copies[d].start()
     for copy in copies:
         copy.wait()
+
+
+def join_kernel(count, *refs):
+    rows = refs[0].shape[0]
+    for i in range(count):
+        refs[-1][i * rows : (i + 1) * rows, :] = refs[i][...]
 
 
 def chain_kernel(
@@ -139,27 +148,28 @@
         )
 
 
-def apply_kernel(n_mem, parts, quarter, first, starts, order_ref, mask_ref, t_ref, *refs):
-    pieces, outs = refs[:n_mem], refs[n_mem : 2 * n_mem]
-    mem_loc = pieces[0].shape[0] // parts
+def apply_kernel(n_mem, parts, quarter, chunks, order_ref, mask_ref, t_ref, *refs):
+    refs, outs = refs[:-n_mem], refs[-n_mem:]
+    mem_loc = outs[0].shape[0] // parts
     members = mem_loc * n_mem
-    tiles = outs[0].shape[1] // TILE
-    base = (lax.axis_index("grid") * n_mem + lax.axis_index("mem")) * (quarter // TILE) + first // TILE
-    for p in range(parts):
-        rows = slice(p * mem_loc, (p + 1) * mem_loc)
-        for t in range(tiles):
-            cols = slice(t * TILE, (t + 1) * TILE)
-            x = jnp.concatenate(
-                [piece[rows, start + t * TILE : start + (t + 1) * TILE] for piece, start in zip(pieces, starts)],
-                axis=0,
-            )
-            code = 0
-            for k in range(BLOCKS):
-                code = code + (mask_ref[order_ref[k], base + p * tiles + t] << k)
-            matrix = t_ref[:, pl.ds(pl.multiple_of(code * TILE, TILE), TILE)][:, 0:members]
-            y = jnp.dot(matrix, x, precision=HIGHEST, preferred_element_type=jnp.float32)
-            for d in range(n_mem):
-                outs[d][rows, cols] = y[d * mem_loc : (d + 1) * mem_loc, :]
+    base = (lax.axis_index("grid") * n_mem + lax.axis_index("mem")) * (quarter // TILE)
+    at = 0
+    for first, width, sources in chunks:
+        tiles = width // parts // TILE
+        for p in range(parts):
+            rows = slice(p * mem_loc, (p + 1) * mem_loc)
+            for t in range(tiles):
+                x = jnp.concatenate(
+                    [refs[i][rows, start + t * TILE : start + (t + 1) * TILE] for i, start in sources], axis=0
+                )
+                code = 0
+                for k in range(BLOCKS):
+                    code = code + (mask_ref[order_ref[k], base + first // TILE + p * tiles + t] << k)
+                matrix = t_ref[:, pl.ds(pl.multiple_of(code * TILE, TILE), TILE)][:, 0:members]
+                y = jnp.dot(matrix, x, precision=HIGHEST, preferred_element_type=jnp.float32)
+                for d in range(n_mem):
+                    outs[d][rows, at + t * TILE : at + (t + 1) * TILE] = y[d * mem_loc : (d + 1) * mem_loc, :]
+        at += width // parts
 
 
 def on_device(state, obs_tile, obs_offset, obs_value, obs_error, loc_mask, block_order):
@@ -172,24 +182,25 @@
     parts = 8 // math.gcd(mem_loc, 8)
     obs = obs_value.shape[1]
     unit = parts * TILE
-    half = quarter // unit * 8 // 16 * unit
-    firsts = (0, half)
-    widths = (half, quarter - half)
-    pieces = [jax.ShapeDtypeStruct((parts * mem_loc, width // parts), f32) for width in widths]
+    units = quarter // unit
+    cuts = [units * cut // 16 * unit for cut in (8,)]
+    firsts = [0] + cuts
+    widths = [end - first for first, end in zip(firsts, cuts + [quarter])]
+    every = tuple(range(len(firsts)))
 
     def swap(value, axis, by):
         return lax.ppermute(value, axis, [(j, j ^ by) for j in range(lax.axis_size(axis))])
 
-    def pack(jobs, after):
+    def pack(jobs, *after):
         chunks = [(d, [(firsts[c], widths[c]) for c in which]) for d, which in jobs]
         total = [sum(width for _, width in each) for _, each in chunks]
         return kernel_call(
             functools.partial(pack_kernel, parts, quarter, chunks),
             "pack",
             [jax.ShapeDtypeStruct((parts * mem_loc, width // parts), f32) for width in total],
-            [VMEM, ANY],
+            [VMEM] + [ANY] * len(after),
             [VMEM] * len(jobs),
-        )(state, after)
+        )(state, *after)
 
     def update_matrices(slab):
         hop = 1
@@ -215,49 +226,60 @@
         seen_kernel,
         "seen",
         jax.ShapeDtypeStruct((BLOCKS * mem_loc, TILE), f32),
-        [HBM] * 3,
+        [HBM, HBM, VMEM],
         VMEM,
         [
             pltpu.SMEM((BLOCKS,), jnp.int32),
             pltpu.SMEM((BLOCKS,), jnp.int32),
-            pltpu.VMEM((BLOCKS, mem_loc, TILE), f32),
-            pltpu.SemaphoreType.DMA((BLOCKS,)),
+            pltpu.SemaphoreType.DMA((2,)),
         ],
-        vmem=12,
     )(obs_tile, block_order, state)
     places = range(n_mem)
     seen = [mine] + [swap(mine, "mem", d) for d in places[1:]]
-    slab = jnp.concatenate(seen, axis=0)
     held = {}
 
-    def start(jobs, after):
-        for job, value in zip(jobs, pack(jobs, after)):
+    def start(jobs, *after):
+        for job, value in zip(jobs, pack(jobs, *after)):
             held[job] = swap(value, "mem", job[0]) if job[0] else value
 
-    start([(d, (0, 1)) for d in range(n_mem - 1)] + [(n_mem - 1, (0,))], slab)
+    last = n_mem - 1
+
+    start([(d, every) for d in range(last)] + [(last, (0,)), (last, (1,))], *seen)
+
+    slab = kernel_call(
+        functools.partial(join_kernel, n_mem),
+        "join",
+        jax.ShapeDtypeStruct((n_mem * BLOCKS * mem_loc, TILE), f32),
+        [VMEM] * n_mem,
+        VMEM,
+    )(*seen)
     matrices = lax.cond(jnp.any(loc_mask > 0), update_matrices, no_updates, slab)
-    start([(n_mem - 1, (1,))], matrices)
-    arrived, starts = [], []
-    for c in range(2):
-        arrived.append([held.get((d, (c,)), held.get((d, (0, 1)))) for d in range(n_mem)])
-        starts.append([0 if (d, (c,)) in held else firsts[c] // parts for d in range(n_mem)])
     result = []
-    for c in range(2):
+    for group in ((0,), (1,)):
+        jobs = sorted({job for job in held if set(job[1]) & set(group)})
+        chunks = []
+        for c in group:
+            sources = []
+            for d in range(n_mem):
+                job = next(job for job in jobs if job[0] == d and c in job[1])
+                sources.append((jobs.index(job), sum(widths[b] for b in job[1] if b < c) // parts))
+            chunks.append((firsts[c], widths[c], sources))
+        total = sum(widths[c] for c in group)
         updated = kernel_call(
-            functools.partial(apply_kernel, n_mem, parts, quarter, firsts[c], starts[c]),
+            functools.partial(apply_kernel, n_mem, parts, quarter, chunks),
             "apply",
-            [pieces[c]] * n_mem,
-            [SMEM] * 2 + [VMEM] * (1 + n_mem),
+            [jax.ShapeDtypeStruct((parts * mem_loc, total // parts), f32)] * n_mem,
+            [SMEM] * 2 + [VMEM] * (1 + len(jobs)),
             [VMEM] * n_mem,
-        )(block_order, loc_mask, matrices, *arrived[c])
+        )(block_order, loc_mask, matrices, *[held[job] for job in jobs])
         back = [updated[0]] + [swap(updated[d], "mem", d) for d in range(1, n_mem)]
         result = kernel_call(
-            functools.partial(unpack_kernel, parts, quarter, firsts[c], range(n_mem)),
+            functools.partial(unpack_kernel, parts, quarter, [chunk[:2] for chunk in chunks], n_mem),
             "unpack",
             [jax.ShapeDtypeStruct(state.shape, f32)],
             [VMEM] * n_mem + [HBM] * len(result),
             [HBM],
-            [pltpu.VMEM((n_mem, mem_loc, widths[c]), f32), pltpu.SemaphoreType.DMA((n_mem,))],
+            [pltpu.VMEM((n_mem, mem_loc, total), f32), pltpu.SemaphoreType.DMA((n_mem,))],
             {n_mem: 0} if result else None,
         )(*back, *result)
     return result[0]

time: 72.6 us -> 70.1 us (0.966)
  waiting for transfers between devices: 33.8 us -> 30.1 us
  starting transfers between devices: 23.9 us -> 27.2 us
  other arithmetic: 1.61 us -> 0.68 us
  Pallas kernels: 10.3 us -> 9.39 us
    ppermute x16, waiting for transfers between devices: 33.8 us -> 30.1 us  [swap(): lax.ppermute(value, axis, [(j, j ^ by) for j in range(lax.axis_size(axis))])]
    ppermute x16, starting transfers between devices: 23.9 us -> 27.2 us  [swap(): lax.ppermute(value, axis, [(j, j ^ by) for j in range(lax.axis_size(axis))])]
    add x2, other arithmetic: 0.96 us -> 0.04 us  [update_matrices(): slab = slab + other]
    pallas_call x1, Pallas kernels: 4.36 us -> 3.51 us  [update_matrices(): kernel_call(functools.partial(chain_kernel, places), 'chain', jax.ShapeDt...]
    unnamed x12 -> x14, local copies, waits for them, and re-layouts: 1.96 us -> 1.43 us
    pallas_call x4 -> x5, Pallas kernels: 4.88 us -> 4.9 us  [the longest x2 3.03 us: on_device(): kernel_call(functools.partial(apply_kernel, n_mem, parts, quarter, chunks...]
  transfers between devices with their start and end apart: 16 -> 16, of which waited for: 9 -> 9; matrix products, arithmetic and copies ran while one was open for 2% -> 1% of each run, Pallas kernels for 12% -> 11%
where the time goes in v4:
time: 70.1 us; the launch traced here: 69.6 us
  waiting for transfers between devices  30.1 us (43%)
  starting transfers between devices  27.2 us (39%)
  Pallas kernels  9.39 us (13%)
  local copies, waits for them, and re-layouts  1.43 us (2%)
  between operations  0.8 us (1%)
    ppermute x16, waiting for transfers between devices, swap(): lax.ppermute(value, axis, [(j, j ^ by) for j in range(lax.axis_size(axis))])  30.1 us
    ppermute x16, starting transfers between devices, swap(): lax.ppermute(value, axis, [(j, j ^ by) for j in range(lax.axis_size(axis))])  27.2 us
    pallas_call x1, Pallas kernels, update_matrices(): kernel_call(functools.partial(chain_kernel, places), 'chain', jax.ShapeDt...  3.51 us
    pallas_call x2, Pallas kernels, on_device(): kernel_call(functools.partial(apply_kernel, n_mem, parts, quarter, chunks...  3.03 us
    pallas_call x2, Pallas kernels, on_device(): kernel_call(functools.partial(unpack_kernel, parts, quarter, [chunk[:2] f...  1.86 us
    unnamed x14, local copies, waits for them, and re-layouts  1.43 us
  transfers between devices with their start and end apart: 16, of which 9 were waited for; matrix products, arithmetic and copies ran while one was open for 1% of the time, Pallas kernels for 11%

profile of v4, /device:TPU:0, one launch (start us, length us, event | category | flops | bytes accessed | tf_op | source)
XLA Modules:
  0.0 69.6 jit_solution(7754520082185613193)
XLA Ops:
  0.0 1.4 %copy-done = f32[20,16384]{1,0:T(8,128)S(1)} copy-done((f32[20,16384]{1,0:T(8,128)S(1)}, f32[20,16384]{1,0:T(8,128)}, u32[]{:S(2)}) %copy-start) | copy-done | bytes 1310744
  1.4 0.9 %seen.1.refs_0_ = f32[80,128]{1,0:T(8,128)S(1)} custom-call(s32[4]{0:T(128)} %tile_ref.1, s32[4]{0:T(128)} %order_ref.5, f32[20,16384]{1,0:T(8,128)S(1)} %copy-done), custom_call_target="tpu_custom_call" | custom-call | tf_op jit(solution)/shard_map/seen/pallas_call | solution.py:225
  2.3 5.1 %collective-permute-start.5 = (f32[80,128]{1,0:T(8,128)S(1)}, f32[80,128]{1,0:T(8,128)S(1)}, u32[]{:S(2)}, u32[]{:S(2)}) collective-permute-start(f32[80,128]{1,0:T(8,128)S(1)} %seen.1.refs_0_), channel_id=1, source_target_pairs={{0,24},{8,16},{16,8},{24,0},{1,25},{9,17},{17,9},{25,1},{2,26},{10... | collective-permute-start | bytes 122888 | tf_op jit(solution)/shard_map/ppermute | solution.py:192
  7.4 0.6 collective-permute-start.3
  8.1 1.4 %collective-permute-done.5.refs_3_ = f32[80,128]{1,0:T(8,128)S(1)} collective-permute-done((f32[80,128]{1,0:T(8,128)S(1)}, f32[80,128]{1,0:T(8,128)S(1)}, u32[]{:S(2)}, u32[]{:S(2)}) %collective-permute-start.5) | collective-permute-done | bytes 40992 | tf_op jit(solution)/shard_map/ppermute | solution.py:192
  9.4 2.9 %collective-permute-done.4.refs_2_ = f32[80,128]{1,0:T(8,128)S(1)} collective-permute-done((f32[80,128]{1,0:T(8,128)S(1)}, f32[80,128]{1,0:T(8,128)S(1)}, u32[]{:S(2)}, u32[]{:S(2)}) %collective-permute-start.4) | collective-permute-done | bytes 40992 | tf_op jit(solution)/shard_map/ppermute | solution.py:192
  12.4 0.2 collective-permute-start.6
  12.7 2.0 %collective-permute-start.7 = (f32[40,2048]{1,0:T(8,128)S(1)}, f32[40,2048]{1,0:T(8,128)S(1)}, u32[]{:S(2)}, u32[]{:S(2)}) collective-permute-start(f32[40,2048]{1,0:T(8,128)S(1)} %get-tuple-element.44), channel_id=1, source_target_pairs={{0,16},{8,24},{16,0},{24,8},{1,17},{9,25},{17,1},{25,9},{2,18},{10... | collective-permute-start | bytes 983048 | tf_op jit(solution)/shard_map/ppermute | solution.py:192
  14.7 2.2 %collective-permute-start.12 = (f32[40,1024]{1,0:T(8,128)S(1)}, f32[40,1024]{1,0:T(8,128)S(1)}, u32[]{:S(2)}, u32[]{:S(2)}) collective-permute-start(f32[40,1024]{1,0:T(8,128)S(1)} %get-tuple-element.50), channel_id=1, source_target_pairs={{0,24},{8,16},{16,8},{24,0},{1,25},{9,17},{17,9},{25,1},{2,26},{10... | collective-permute-start | bytes 491528 | tf_op jit(solution)/shard_map/ppermute | solution.py:192
  16.9 0.6 compare_reduce_fusion
  18.2 1.6 %collective-permute-start.8 = (f32[40,1024]{1,0:T(8,128)S(1)}, f32[40,1024]{1,0:T(8,128)S(1)}, u32[]{:S(2)}, u32[]{:S(2)}) collective-permute-start(f32[40,1024]{1,0:T(8,128)S(1)} %get-tuple-element.45), channel_id=1, source_target_pairs={{0,24},{8,16},{16,8},{24,0},{1,25},{9,17},{17,9},{25,1},{2,26},{10... | collective-permute-start | bytes 491528 | tf_op jit(solution)/shard_map/ppermute | solution.py:192
  19.9 16.8 %conditional.1 = (f32[80,2048]{1,0:T(8,128)S(1)}) conditional(s32[]{:T(128)} %convert_element_type.10, () %tuple.11, (f32[320,128]{1,0:T(8,128)S(1)}, s32[4]{0:T(128)S(1)}, s32[4]{0:T(128)S(1)}, s32[4,1024]{1,0:T(4,128)S(1)}, s32[4,256]{1,0:T(4,128)S(1)}, /*index=5*/f32[4,256]{1,0:T(4,128)S(1)}, f32[4,256]{1,0:T(4,128)S(1)}) %tuple.20), branch_computations={%region_1.0_spmd, %region_2.0_spmd} | conditional | flops 81920 | bytes 2949248 | solution.py:256
  20.0 1.4 %collective-permute-done = f32[320,128]{1,0:T(8,128)S(1)} collective-permute-done((f32[320,128]{1,0:T(8,128)S(1)}, f32[320,128]{1,0:T(8,128)S(1)}, u32[]{:S(2)}, u32[]{:S(2)}) %collective-permute-start) | collective-permute-done | bytes 163872 | tf_op jit(solution)/shard_map/cond/branch_1_fun/ppermute | solution.py:192
  21.4 1.6 %collective-permute-start.1 = (f32[320,128]{1,0:T(8,128)S(1)}, f32[320,128]{1,0:T(8,128)S(1)}, u32[]{:S(2)}, u32[]{:S(2)}) collective-permute-start(f32[320,128]{1,0:T(8,128)S(1)} %add.4), channel_id=1, source_target_pairs={{0,2},{1,3},{2,0},{3,1},{4,6},{5,7},{6,4},{7,5},{8,10},{9,11},{10,... | collective-permute-start | bytes 491528 | tf_op jit(solution)/shard_map/cond/branch_1_fun/ppermute | solution.py:192
  23.0 4.8 %collective-permute-done.1 = f32[320,128]{1,0:T(8,128)S(1)} collective-permute-done((f32[320,128]{1,0:T(8,128)S(1)}, f32[320,128]{1,0:T(8,128)S(1)}, u32[]{:S(2)}, u32[]{:S(2)}) %collective-permute-start.1) | collective-permute-done | bytes 163872 | tf_op jit(solution)/shard_map/cond/branch_1_fun/ppermute | solution.py:192
  27.7 1.6 %collective-permute-start.2 = (f32[320,128]{1,0:T(8,128)S(1)}, f32[320,128]{1,0:T(8,128)S(1)}, u32[]{:S(2)}, u32[]{:S(2)}) collective-permute-start(f32[320,128]{1,0:T(8,128)S(1)} %add.5.one_ref), channel_id=1, source_target_pairs={{0,4},{1,5},{2,6},{3,7},{4,0},{5,1},{6,2},{7,3},{8,12},{9,13},{10,... | collective-permute-start | bytes 491528 | tf_op jit(solution)/shard_map/cond/branch_1_fun/ppermute | solution.py:192
  29.3 3.9 %collective-permute-done.2.two_ref = f32[320,128]{1,0:T(8,128)S(1)} collective-permute-done((f32[320,128]{1,0:T(8,128)S(1)}, f32[320,128]{1,0:T(8,128)S(1)}, u32[]{:S(2)}, u32[]{:S(2)}) %collective-permute-start.2) | collective-permute-done | bytes 163872 | tf_op jit(solution)/shard_map/cond/branch_1_fun/ppermute | solution.py:192
  33.2 3.5 %chain.1 = f32[80,2048]{1,0:T(8,128)S(1)} custom-call(s32[4]{0:T(128)S(1)} %get-tuple-element.22.tile_ref, s32[4]{0:T(128)S(1)} %get-tuple-element.23.order_ref, s32[4,1024]{1,0:T(4,128)S(1)} %get-tuple-element.24.mask_ref, s32[4,256]{1,0:T(4,128)S(1)} %get-tuple-element.58.offset_ref, f32[4,256]{1,0:T(4,128)S(1)} %get-tuple-element.59.value_ref, ...), custom_call_target="tpu_custom_call" | custom-call | tf_op jit(solution)/shard_map/cond/branch_1_fun/chain/pallas_call | solution.py:213
  36.8 1.5 %collective-permute-done.7.refs_2_ = f32[40,2048]{1,0:T(8,128)S(1)} collective-permute-done((f32[40,2048]{1,0:T(8,128)S(1)}, f32[40,2048]{1,0:T(8,128)S(1)}, u32[]{:S(2)}, u32[]{:S(2)}) %collective-permute-start.7) | collective-permute-done | bytes 327712 | tf_op jit(solution)/shard_map/ppermute | solution.py:192
  38.3 1.5 %apply.3 = (f32[40,1024]{1,0:T(8,128)S(1)}, f32[40,1024]{1,0:T(8,128)S(1)}, f32[40,1024]{1,0:T(8,128)S(1)}, f32[40,1024]{1,0:T(8,128)S(1)}) custom-call(s32[4]{0:T(128)S(1)} %copy-done.2, s32[4,1024]{1,0:T(4,128)S(1)} %copy-done.1, f32[80,2048]{1,0:T(8,128)S(1)} %get-tuple-element.61.t_ref, f32[40,2048]{1,0:T(8,128)S(1)} %get-tuple-element.42.refs_0_, ...), custom_call_target="tpu_custom_call" | custom-call | tf_op jit(solution)/shard_map/apply/pallas_call | solution.py:268
  39.8 3.3 %collective-permute-start.13 = (f32[40,1024]{1,0:T(8,128)S(1)}, f32[40,1024]{1,0:T(8,128)S(1)}, u32[]{:S(2)}, u32[]{:S(2)}) collective-permute-start(f32[40,1024]{1,0:T(8,128)S(1)} %get-tuple-element.52), channel_id=1, source_target_pairs={{0,8},{8,0},{16,24},{24,16},{1,9},{9,1},{17,25},{25,17},{2,10},{10... | collective-permute-start | bytes 491528 | tf_op jit(solution)/shard_map/ppermute | solution.py:192
  43.1 1.7 %collective-permute-start.14 = (f32[40,1024]{1,0:T(8,128)S(1)}, f32[40,1024]{1,0:T(8,128)S(1)}, u32[]{:S(2)}, u32[]{:S(2)}) collective-permute-start(f32[40,1024]{1,0:T(8,128)S(1)} %get-tuple-element.53), channel_id=1, source_target_pairs={{0,16},{8,24},{16,0},{24,8},{1,17},{9,25},{17,1},{25,9},{2,18},{10... | collective-permute-start | bytes 491528 | tf_op jit(solution)/shard_map/ppermute | solution.py:192
  44.8 1.4 %collective-permute-start.15 = (f32[40,1024]{1,0:T(8,128)S(1)}, f32[40,1024]{1,0:T(8,128)S(1)}, u32[]{:S(2)}, u32[]{:S(2)}) collective-permute-start(f32[40,1024]{1,0:T(8,128)S(1)} %get-tuple-element.54), channel_id=1, source_target_pairs={{0,24},{8,16},{16,8},{24,0},{1,25},{9,17},{17,9},{25,1},{2,26},{10... | collective-permute-start | bytes 491528 | tf_op jit(solution)/shard_map/ppermute | solution.py:192
  46.2 1.5 %apply.2 = (f32[40,1024]{1,0:T(8,128)S(1)}, f32[40,1024]{1,0:T(8,128)S(1)}, f32[40,1024]{1,0:T(8,128)S(1)}, f32[40,1024]{1,0:T(8,128)S(1)}) custom-call(s32[4]{0:T(128)S(1)} %copy-done.2, s32[4,1024]{1,0:T(4,128)S(1)} %copy-done.1, f32[80,2048]{1,0:T(8,128)S(1)} %get-tuple-element.61.t_ref, f32[40,2048]{1,0:T(8,128)S(1)} %get-tuple-element.42.refs_0_, ...), custom_call_target="tpu_custom_call" | custom-call | tf_op jit(solution)/shard_map/apply/pallas_call | solution.py:268
  47.7 1.4 %collective-permute-start.9 = (f32[40,1024]{1,0:T(8,128)S(1)}, f32[40,1024]{1,0:T(8,128)S(1)}, u32[]{:S(2)}, u32[]{:S(2)}) collective-permute-start(f32[40,1024]{1,0:T(8,128)S(1)} %get-tuple-element.47), channel_id=1, source_target_pairs={{0,8},{8,0},{16,24},{24,16},{1,9},{9,1},{17,25},{25,17},{2,10},{10... | collective-permute-start | bytes 491528 | tf_op jit(solution)/shard_map/ppermute | solution.py:192
  49.1 2.0 %collective-permute-start.10 = (f32[40,1024]{1,0:T(8,128)S(1)}, f32[40,1024]{1,0:T(8,128)S(1)}, u32[]{:S(2)}, u32[]{:S(2)}) collective-permute-start(f32[40,1024]{1,0:T(8,128)S(1)} %get-tuple-element.48), channel_id=1, source_target_pairs={{0,16},{8,24},{16,0},{24,8},{1,17},{9,25},{17,1},{25,9},{2,18},{10... | collective-permute-start | bytes 491528 | tf_op jit(solution)/shard_map/ppermute | solution.py:192
  51.1 0.7 %collective-permute-done.13.refs_1_ = f32[40,1024]{1,0:T(8,128)S(1)} collective-permute-done((f32[40,1024]{1,0:T(8,128)S(1)}, f32[40,1024]{1,0:T(8,128)S(1)}, u32[]{:S(2)}, u32[]{:S(2)}) %collective-permute-start.13) | collective-permute-done | bytes 163872 | tf_op jit(solution)/shard_map/ppermute | solution.py:192
  51.8 2.3 %collective-permute-start.11 = (f32[40,1024]{1,0:T(8,128)S(1)}, f32[40,1024]{1,0:T(8,128)S(1)}, u32[]{:S(2)}, u32[]{:S(2)}) collective-permute-start(f32[40,1024]{1,0:T(8,128)S(1)} %get-tuple-element.49), channel_id=1, source_target_pairs={{0,24},{8,16},{16,8},{24,0},{1,25},{9,17},{17,9},{25,1},{2,26},{10... | collective-permute-start | bytes 491528 | tf_op jit(solution)/shard_map/ppermute | solution.py:192
  54.1 4.0 %collective-permute-done.14.refs_2_ = f32[40,1024]{1,0:T(8,128)S(1)} collective-permute-done((f32[40,1024]{1,0:T(8,128)S(1)}, f32[40,1024]{1,0:T(8,128)S(1)}, u32[]{:S(2)}, u32[]{:S(2)}) %collective-permute-start.14) | collective-permute-done | bytes 163872 | tf_op jit(solution)/shard_map/ppermute | solution.py:192
  58.2 0.9 %unpack.2.refs_4_ = f32[20,16384]{1,0:T(8,128)} custom-call(f32[40,1024]{1,0:T(8,128)S(1)} %get-tuple-element.51.refs_0_, f32[40,1024]{1,0:T(8,128)S(1)} %collective-permute-done.13.refs_1_, f32[40,1024]{1,0:T(8,128)S(1)} %collective-permute-done.14.refs_2_, f32[40,1024]{1,0:T(8,128)S(1)} %collective-permute-done.15.refs_3_), custom_call_target="tpu_custom_call" | custom-call | tf_op jit(solution)/shard_map/unpack/pallas_call | solution.py:276
  59.1 9.6 %collective-permute-done.10.refs_2_ = f32[40,1024]{1,0:T(8,128)S(1)} collective-permute-done((f32[40,1024]{1,0:T(8,128)S(1)}, f32[40,1024]{1,0:T(8,128)S(1)}, u32[]{:S(2)}, u32[]{:S(2)}) %collective-permute-start.10) | collective-permute-done | bytes 163872 | tf_op jit(solution)/shard_map/ppermute | solution.py:192
  68.7 0.9 %unpack.3 = f32[20,16384]{1,0:T(8,128)} custom-call(f32[40,1024]{1,0:T(8,128)S(1)} %get-tuple-element.46.refs_0_, f32[40,1024]{1,0:T(8,128)S(1)} %collective-permute-done.9.refs_1_, f32[40,1024]{1,0:T(8,128)S(1)} %collective-permute-done.10.refs_2_, f32[40,1024]{1,0:T(8,128)S(1)} %collective-permute-done.11.refs_3_, ...), custom_call_target="tpu_custom_call", output_to_operand_aliasing={{}: (4, {})} | custom-call | tf_op jit(solution)/shard_map/unpack/pallas_call | solution.py:276
  (26 shorter events, 0.3 us)
Async XLA Ops:
  0.0 1.4 %copy-start = (f32[20,16384]{1,0:T(8,128)S(1)}, f32[20,16384]{1,0:T(8,128)}, u32[]{:S(2)}) copy-start(f32[20,16384]{1,0:T(8,128)} %x_ref.3) | copy-start | bytes 3932164
  1.4 15.5 %copy-start.1 = (s32[4,1024]{1,0:T(4,128)S(1)}, s32[4,1024]{1,0:T(4,128)}, u32[]{:S(2)}) copy-start(s32[4,1024]{1,0:T(4,128)} %mask_ref.3) | copy-start | bytes 49156
  1.4 18.4 %copy-start.2 = (s32[4]{0:T(128)S(1)}, s32[4]{0:T(128)}, u32[]{:S(2)}) copy-start(s32[4]{0:T(128)} %order_ref.5) | copy-start | bytes 52
  1.4 18.5 %copy-start.3 = (s32[4,256]{1,0:T(4,128)S(1)}, s32[4,256]{1,0:T(4,128)}, u32[]{:S(2)}) copy-start(s32[4,256]{1,0:T(4,128)} %param.11) | copy-start | bytes 12292
  1.4 18.5 %copy-start.4 = (f32[4,256]{1,0:T(4,128)S(1)}, f32[4,256]{1,0:T(4,128)}, u32[]{:S(2)}) copy-start(f32[4,256]{1,0:T(4,128)} %param.12) | copy-start | bytes 12292
  1.4 18.5 %copy-start.5 = (f32[4,256]{1,0:T(4,128)S(1)}, f32[4,256]{1,0:T(4,128)}, u32[]{:S(2)}) copy-start(f32[4,256]{1,0:T(4,128)} %param.13) | copy-start | bytes 12292
  1.4 18.5 %copy-start.6 = (s32[4]{0:T(128)S(1)}, s32[4]{0:T(128)}, u32[]{:S(2)}) copy-start(s32[4]{0:T(128)} %tile_ref.1) | copy-start | bytes 52
  2.3 7.1 %collective-permute-start.5 = (f32[80,128]{1,0:T(8,128)S(1)}, f32[80,128]{1,0:T(8,128)S(1)}, u32[]{:S(2)}, u32[]{:S(2)}) collective-permute-start(f32[80,128]{1,0:T(8,128)S(1)} %seen.1.refs_0_), channel_id=1, source_target_pairs={{0,24},{8,16},{16,8},{24,0},{1,25},{9,17},{17,9},{25,1},{2,26},{10... | collective-permute-start | bytes 122888 | tf_op jit(solution)/shard_map/ppermute | solution.py:192
  7.4 4.9 %collective-permute-start.4 = (f32[80,128]{1,0:T(8,128)S(1)}, f32[80,128]{1,0:T(8,128)S(1)}, u32[]{:S(2)}, u32[]{:S(2)}) collective-permute-start(f32[80,128]{1,0:T(8,128)S(1)} %seen.1.refs_0_), channel_id=1, source_target_pairs={{0,16},{8,24},{16,0},{24,8},{1,17},{9,25},{17,1},{25,9},{2,18},{10... | collective-permute-start | bytes 122888 | tf_op jit(solution)/shard_map/ppermute | solution.py:192
  7.4 4.9 %collective-permute-start.3 = (f32[80,128]{1,0:T(8,128)S(1)}, f32[80,128]{1,0:T(8,128)S(1)}, u32[]{:S(2)}, u32[]{:S(2)}) collective-permute-start(f32[80,128]{1,0:T(8,128)S(1)} %seen.1.refs_0_), channel_id=1, source_target_pairs={{0,8},{8,0},{16,24},{24,16},{1,9},{9,1},{17,25},{25,17},{2,10},{10... | collective-permute-start | bytes 122888 | tf_op jit(solution)/shard_map/ppermute | solution.py:192
  12.4 24.3 %collective-permute-start.6 = (f32[40,2048]{1,0:T(8,128)S(1)}, f32[40,2048]{1,0:T(8,128)S(1)}, u32[]{:S(2)}, u32[]{:S(2)}) collective-permute-start(f32[40,2048]{1,0:T(8,128)S(1)} %get-tuple-element.43), channel_id=1, source_target_pairs={{0,8},{8,0},{16,24},{24,16},{1,9},{9,1},{17,25},{25,17},{2,10},{10... | collective-permute-start | bytes 983048 | tf_op jit(solution)/shard_map/ppermute | solution.py:192
  12.7 25.6 %collective-permute-start.7 = (f32[40,2048]{1,0:T(8,128)S(1)}, f32[40,2048]{1,0:T(8,128)S(1)}, u32[]{:S(2)}, u32[]{:S(2)}) collective-permute-start(f32[40,2048]{1,0:T(8,128)S(1)} %get-tuple-element.44), channel_id=1, source_target_pairs={{0,16},{8,24},{16,0},{24,8},{1,17},{9,25},{17,1},{25,9},{2,18},{10... | collective-permute-start | bytes 983048 | tf_op jit(solution)/shard_map/ppermute | solution.py:192
  14.7 22.1 %collective-permute-start.12 = (f32[40,1024]{1,0:T(8,128)S(1)}, f32[40,1024]{1,0:T(8,128)S(1)}, u32[]{:S(2)}, u32[]{:S(2)}) collective-permute-start(f32[40,1024]{1,0:T(8,128)S(1)} %get-tuple-element.50), channel_id=1, source_target_pairs={{0,24},{8,16},{16,8},{24,0},{1,25},{9,17},{17,9},{25,1},{2,26},{10... | collective-permute-start | bytes 491528 | tf_op jit(solution)/shard_map/ppermute | solution.py:192
  18.2 28.0 %collective-permute-start.8 = (f32[40,1024]{1,0:T(8,128)S(1)}, f32[40,1024]{1,0:T(8,128)S(1)}, u32[]{:S(2)}, u32[]{:S(2)}) collective-permute-start(f32[40,1024]{1,0:T(8,128)S(1)} %get-tuple-element.45), channel_id=1, source_target_pairs={{0,24},{8,16},{16,8},{24,0},{1,25},{9,17},{17,9},{25,1},{2,26},{10... | collective-permute-start | bytes 491528 | tf_op jit(solution)/shard_map/ppermute | solution.py:192
  19.9 1.5 %collective-permute-start = (f32[320,128]{1,0:T(8,128)S(1)}, f32[320,128]{1,0:T(8,128)S(1)}, u32[]{:S(2)}, u32[]{:S(2)}) collective-permute-start(f32[320,128]{1,0:T(8,128)S(1)} %get-tuple-element.28), channel_id=1, source_target_pairs={{0,1},{1,0},{2,3},{3,2},{4,5},{5,4},{6,7},{7,6},{8,9},{9,8},{10,11... | collective-permute-start | bytes 491528 | tf_op jit(solution)/shard_map/cond/branch_1_fun/ppermute | solution.py:192
  21.4 6.3 %collective-permute-start.1 = (f32[320,128]{1,0:T(8,128)S(1)}, f32[320,128]{1,0:T(8,128)S(1)}, u32[]{:S(2)}, u32[]{:S(2)}) collective-permute-start(f32[320,128]{1,0:T(8,128)S(1)} %add.4), channel_id=1, source_target_pairs={{0,2},{1,3},{2,0},{3,1},{4,6},{5,7},{6,4},{7,5},{8,10},{9,11},{10,... | collective-permute-start | bytes 491528 | tf_op jit(solution)/shard_map/cond/branch_1_fun/ppermute | solution.py:192
  27.7 5.5 %collective-permute-start.2 = (f32[320,128]{1,0:T(8,128)S(1)}, f32[320,128]{1,0:T(8,128)S(1)}, u32[]{:S(2)}, u32[]{:S(2)}) collective-permute-start(f32[320,128]{1,0:T(8,128)S(1)} %add.5.one_ref), channel_id=1, source_target_pairs={{0,4},{1,5},{2,6},{3,7},{4,0},{5,1},{6,2},{7,3},{8,12},{9,13},{10,... | collective-permute-start | bytes 491528 | tf_op jit(solution)/shard_map/cond/branch_1_fun/ppermute | solution.py:192
  39.8 12.0 %collective-permute-start.13 = (f32[40,1024]{1,0:T(8,128)S(1)}, f32[40,1024]{1,0:T(8,128)S(1)}, u32[]{:S(2)}, u32[]{:S(2)}) collective-permute-start(f32[40,1024]{1,0:T(8,128)S(1)} %get-tuple-element.52), channel_id=1, source_target_pairs={{0,8},{8,0},{16,24},{24,16},{1,9},{9,1},{17,25},{25,17},{2,10},{10... | collective-permute-start | bytes 491528 | tf_op jit(solution)/shard_map/ppermute | solution.py:192
  43.1 15.1 %collective-permute-start.14 = (f32[40,1024]{1,0:T(8,128)S(1)}, f32[40,1024]{1,0:T(8,128)S(1)}, u32[]{:S(2)}, u32[]{:S(2)}) collective-permute-start(f32[40,1024]{1,0:T(8,128)S(1)} %get-tuple-element.53), channel_id=1, source_target_pairs={{0,16},{8,24},{16,0},{24,8},{1,17},{9,25},{17,1},{25,9},{2,18},{10... | collective-permute-start | bytes 491528 | tf_op jit(solution)/shard_map/ppermute | solution.py:192
  44.8 13.3 %collective-permute-start.15 = (f32[40,1024]{1,0:T(8,128)S(1)}, f32[40,1024]{1,0:T(8,128)S(1)}, u32[]{:S(2)}, u32[]{:S(2)}) collective-permute-start(f32[40,1024]{1,0:T(8,128)S(1)} %get-tuple-element.54), channel_id=1, source_target_pairs={{0,24},{8,16},{16,8},{24,0},{1,25},{9,17},{17,9},{25,1},{2,26},{10... | collective-permute-start | bytes 491528 | tf_op jit(solution)/shard_map/ppermute | solution.py:192
  47.7 11.4 %collective-permute-start.9 = (f32[40,1024]{1,0:T(8,128)S(1)}, f32[40,1024]{1,0:T(8,128)S(1)}, u32[]{:S(2)}, u32[]{:S(2)}) collective-permute-start(f32[40,1024]{1,0:T(8,128)S(1)} %get-tuple-element.47), channel_id=1, source_target_pairs={{0,8},{8,0},{16,24},{24,16},{1,9},{9,1},{17,25},{25,17},{2,10},{10... | collective-permute-start | bytes 491528 | tf_op jit(solution)/shard_map/ppermute | solution.py:192
  49.1 19.6 %collective-permute-start.10 = (f32[40,1024]{1,0:T(8,128)S(1)}, f32[40,1024]{1,0:T(8,128)S(1)}, u32[]{:S(2)}, u32[]{:S(2)}) collective-permute-start(f32[40,1024]{1,0:T(8,128)S(1)} %get-tuple-element.48), channel_id=1, source_target_pairs={{0,16},{8,24},{16,0},{24,8},{1,17},{9,25},{17,1},{25,9},{2,18},{10... | collective-permute-start | bytes 491528 | tf_op jit(solution)/shard_map/ppermute | solution.py:192
  51.8 16.9 %collective-permute-start.11 = (f32[40,1024]{1,0:T(8,128)S(1)}, f32[40,1024]{1,0:T(8,128)S(1)}, u32[]{:S(2)}, u32[]{:S(2)}) collective-permute-start(f32[40,1024]{1,0:T(8,128)S(1)} %get-tuple-element.49), channel_id=1, source_target_pairs={{0,24},{8,16},{16,8},{24,0},{1,25},{9,17},{17,9},{25,1},{2,26},{10... | collective-permute-start | bytes 491528 | tf_op jit(solution)/shard_map/ppermute | solution.py:192

commit v5 on v4

--- a/solution.py
+++ b/solution.py
@@ -70,23 +70,23 @@
             to += width
 
 
-def unpack_kernel(parts, quarter, chunks, n_mem, *refs):
+def unpack_kernel(parts, quarter, chunks, shifts, *refs):
     out, held, sem = refs[-3:]
     mem_loc = out.shape[0]
     copies = []
-    for d in range(n_mem):
+    for i, d in enumerate(shifts):
         at = 0
         for first, width in chunks:
             side = width // parts
             for p in range(parts):
-                part = refs[d][p * mem_loc : (p + 1) * mem_loc, at // parts : at // parts + side]
-                held[d, :, at + p * side : at + (p + 1) * side] = part
+                part = refs[i][p * mem_loc : (p + 1) * mem_loc, at // parts : at // parts + side]
+                held[i, :, at + p * side : at + (p + 1) * side] = part
             at += width
         first, total = chunks[0][0], sum(width for _, width in chunks)
         copies.append(
-            pltpu.make_async_copy(held.at[d], out.at[:, piece_columns(d, quarter, first, total)], sem.at[d])
+            pltpu.make_async_copy(held.at[i], out.at[:, piece_columns(d, quarter, first, total)], sem.at[i])
         )
-        copies[d].start()
+        copies[i].start()
     for copy in copies:
         copy.wait()
 
@@ -273,15 +273,16 @@
             [VMEM] * n_mem,
         )(block_order, loc_mask, matrices, *[held[job] for job in jobs])
         back = [updated[0]] + [swap(updated[d], "mem", d) for d in range(1, n_mem)]
-        result = kernel_call(
-            functools.partial(unpack_kernel, parts, quarter, [chunk[:2] for chunk in chunks], n_mem),
-            "unpack",
-            [jax.ShapeDtypeStruct(state.shape, f32)],
-            [VMEM] * n_mem + [HBM] * len(result),
-            [HBM],
-            [pltpu.VMEM((n_mem, mem_loc, total), f32), pltpu.SemaphoreType.DMA((n_mem,))],
-            {n_mem: 0} if result else None,
-        )(*back, *result)
+        for shifts in (range(2), range(2, n_mem)):
+            result = kernel_call(
+                functools.partial(unpack_kernel, parts, quarter, [chunk[:2] for chunk in chunks], shifts),
+                "unpack",
+                [jax.ShapeDtypeStruct(state.shape, f32)],
+                [VMEM] * len(shifts) + [HBM] * len(result),
+                [HBM],
+                [pltpu.VMEM((len(shifts), mem_loc, total), f32), pltpu.SemaphoreType.DMA((len(shifts),))],
+                {len(shifts): 0} if result else None,
+            )(*[back[d] for d in shifts], *result)
     return result[0]
 
 

time: 70.1 us -> 69.9 us (level)
  waiting for transfers between devices: 30.1 us -> 28.7 us
  Pallas kernels: 9.39 us -> 10.7 us
    ppermute x16, waiting for transfers between devices: 30.1 us -> 28.7 us  [swap(): lax.ppermute(value, axis, [(j, j ^ by) for j in range(lax.axis_size(axis))])]
    pallas_call x2 -> x4, Pallas kernels: 1.86 us -> 3.13 us  [on_device(): kernel_call(functools.partial(unpack_kernel, parts, quarter, [chunk[:2] f...]
  transfers between devices with their start and end apart: 16 -> 16, of which waited for: 9 -> 9; matrix products, arithmetic and copies ran while one was open for 1% -> 1% of each run, Pallas kernels for 11% -> 13%
where the time goes in v5:
time: 69.9 us; the launch traced here: 69.5 us
  waiting for transfers between devices  28.7 us (41%)
  starting transfers between devices  27.2 us (39%)
  Pallas kernels  10.7 us (15%)
  local copies, waits for them, and re-layouts  1.43 us (2%)
  between operations  0.81 us (1%)
    ppermute x16, waiting for transfers between devices, swap(): lax.ppermute(value, axis, [(j, j ^ by) for j in range(lax.axis_size(axis))])  28.7 us
    ppermute x16, starting transfers between devices, swap(): lax.ppermute(value, axis, [(j, j ^ by) for j in range(lax.axis_size(axis))])  27.2 us
    pallas_call x1, Pallas kernels, update_matrices(): kernel_call(functools.partial(chain_kernel, places), 'chain', jax.ShapeDt...  3.51 us
    pallas_call x4, Pallas kernels, on_device(): kernel_call(functools.partial(unpack_kernel, parts, quarter, [chunk[:2] f...  3.13 us
    pallas_call x2, Pallas kernels, on_device(): kernel_call(functools.partial(apply_kernel, n_mem, parts, quarter, chunks...  3.03 us
    unnamed x14, local copies, waits for them, and re-layouts  1.43 us
  transfers between devices with their start and end apart: 16, of which 9 were waited for; matrix products, arithmetic and copies ran while one was open for 1% of the time, Pallas kernels for 13%

profile of v5, /device:TPU:0, one launch (start us, length us, event | category | flops | bytes accessed | tf_op | source)
XLA Modules:
  0.0 69.5 jit_solution(14101213156879639413)
XLA Ops:
  0.0 1.4 %copy-done = f32[20,16384]{1,0:T(8,128)S(1)} copy-done((f32[20,16384]{1,0:T(8,128)S(1)}, f32[20,16384]{1,0:T(8,128)}, u32[]{:S(2)}) %copy-start) | copy-done | bytes 1310744
  1.4 0.9 %seen.1.refs_0_ = f32[80,128]{1,0:T(8,128)S(1)} custom-call(s32[4]{0:T(128)} %tile_ref.1, s32[4]{0:T(128)} %order_ref.5, f32[20,16384]{1,0:T(8,128)S(1)} %copy-done), custom_call_target="tpu_custom_call" | custom-call | tf_op jit(solution)/shard_map/seen/pallas_call | solution.py:225
  2.3 5.1 %collective-permute-start.5 = (f32[80,128]{1,0:T(8,128)S(1)}, f32[80,128]{1,0:T(8,128)S(1)}, u32[]{:S(2)}, u32[]{:S(2)}) collective-permute-start(f32[80,128]{1,0:T(8,128)S(1)} %seen.1.refs_0_), channel_id=1, source_target_pairs={{0,24},{8,16},{16,8},{24,0},{1,25},{9,17},{17,9},{25,1},{2,26},{10... | collective-permute-start | bytes 122888 | tf_op jit(solution)/shard_map/ppermute | solution.py:192
  8.1 1.4 %collective-permute-done.5.refs_3_ = f32[80,128]{1,0:T(8,128)S(1)} collective-permute-done((f32[80,128]{1,0:T(8,128)S(1)}, f32[80,128]{1,0:T(8,128)S(1)}, u32[]{:S(2)}, u32[]{:S(2)}) %collective-permute-start.5) | collective-permute-done | bytes 40992 | tf_op jit(solution)/shard_map/ppermute | solution.py:192
  9.4 2.9 %collective-permute-done.4.refs_2_ = f32[80,128]{1,0:T(8,128)S(1)} collective-permute-done((f32[80,128]{1,0:T(8,128)S(1)}, f32[80,128]{1,0:T(8,128)S(1)}, u32[]{:S(2)}, u32[]{:S(2)}) %collective-permute-start.4) | collective-permute-done | bytes 40992 | tf_op jit(solution)/shard_map/ppermute | solution.py:192
  12.7 2.0 %collective-permute-start.7 = (f32[40,2048]{1,0:T(8,128)S(1)}, f32[40,2048]{1,0:T(8,128)S(1)}, u32[]{:S(2)}, u32[]{:S(2)}) collective-permute-start(f32[40,2048]{1,0:T(8,128)S(1)} %get-tuple-element.44), channel_id=1, source_target_pairs={{0,16},{8,24},{16,0},{24,8},{1,17},{9,25},{17,1},{25,9},{2,18},{10... | collective-permute-start | bytes 983048 | tf_op jit(solution)/shard_map/ppermute | solution.py:192
  14.7 2.2 %collective-permute-start.12 = (f32[40,1024]{1,0:T(8,128)S(1)}, f32[40,1024]{1,0:T(8,128)S(1)}, u32[]{:S(2)}, u32[]{:S(2)}) collective-permute-start(f32[40,1024]{1,0:T(8,128)S(1)} %get-tuple-element.50), channel_id=1, source_target_pairs={{0,24},{8,16},{16,8},{24,0},{1,25},{9,17},{17,9},{25,1},{2,26},{10... | collective-permute-start | bytes 491528 | tf_op jit(solution)/shard_map/ppermute | solution.py:192
  16.9 0.6 compare_reduce_fusion
  18.2 1.6 %collective-permute-start.8 = (f32[40,1024]{1,0:T(8,128)S(1)}, f32[40,1024]{1,0:T(8,128)S(1)}, u32[]{:S(2)}, u32[]{:S(2)}) collective-permute-start(f32[40,1024]{1,0:T(8,128)S(1)} %get-tuple-element.45), channel_id=1, source_target_pairs={{0,24},{8,16},{16,8},{24,0},{1,25},{9,17},{17,9},{25,1},{2,26},{10... | collective-permute-start | bytes 491528 | tf_op jit(solution)/shard_map/ppermute | solution.py:192
  19.9 16.8 %conditional.1 = (f32[80,2048]{1,0:T(8,128)S(1)}) conditional(s32[]{:T(128)} %convert_element_type.10, () %tuple.11, (f32[320,128]{1,0:T(8,128)S(1)}, s32[4]{0:T(128)S(1)}, s32[4]{0:T(128)S(1)}, s32[4,1024]{1,0:T(4,128)S(1)}, s32[4,256]{1,0:T(4,128)S(1)}, /*index=5*/f32[4,256]{1,0:T(4,128)S(1)}, f32[4,256]{1,0:T(4,128)S(1)}) %tuple.20), branch_computations={%region_1.0_spmd, %region_2.0_spmd} | conditional | flops 81920 | bytes 2949248 | solution.py:256
  20.0 1.4 %collective-permute-done = f32[320,128]{1,0:T(8,128)S(1)} collective-permute-done((f32[320,128]{1,0:T(8,128)S(1)}, f32[320,128]{1,0:T(8,128)S(1)}, u32[]{:S(2)}, u32[]{:S(2)}) %collective-permute-start) | collective-permute-done | bytes 163872 | tf_op jit(solution)/shard_map/cond/branch_1_fun/ppermute | solution.py:192
  21.4 1.6 %collective-permute-start.1 = (f32[320,128]{1,0:T(8,128)S(1)}, f32[320,128]{1,0:T(8,128)S(1)}, u32[]{:S(2)}, u32[]{:S(2)}) collective-permute-start(f32[320,128]{1,0:T(8,128)S(1)} %add.4), channel_id=1, source_target_pairs={{0,2},{1,3},{2,0},{3,1},{4,6},{5,7},{6,4},{7,5},{8,10},{9,11},{10,... | collective-permute-start | bytes 491528 | tf_op jit(solution)/shard_map/cond/branch_1_fun/ppermute | solution.py:192
  23.0 4.8 %collective-permute-done.1 = f32[320,128]{1,0:T(8,128)S(1)} collective-permute-done((f32[320,128]{1,0:T(8,128)S(1)}, f32[320,128]{1,0:T(8,128)S(1)}, u32[]{:S(2)}, u32[]{:S(2)}) %collective-permute-start.1) | collective-permute-done | bytes 163872 | tf_op jit(solution)/shard_map/cond/branch_1_fun/ppermute | solution.py:192
  27.7 1.6 %collective-permute-start.2 = (f32[320,128]{1,0:T(8,128)S(1)}, f32[320,128]{1,0:T(8,128)S(1)}, u32[]{:S(2)}, u32[]{:S(2)}) collective-permute-start(f32[320,128]{1,0:T(8,128)S(1)} %add.5.one_ref), channel_id=1, source_target_pairs={{0,4},{1,5},{2,6},{3,7},{4,0},{5,1},{6,2},{7,3},{8,12},{9,13},{10,... | collective-permute-start | bytes 491528 | tf_op jit(solution)/shard_map/cond/branch_1_fun/ppermute | solution.py:192
  29.3 3.9 %collective-permute-done.2.two_ref = f32[320,128]{1,0:T(8,128)S(1)} collective-permute-done((f32[320,128]{1,0:T(8,128)S(1)}, f32[320,128]{1,0:T(8,128)S(1)}, u32[]{:S(2)}, u32[]{:S(2)}) %collective-permute-start.2) | collective-permute-done | bytes 163872 | tf_op jit(solution)/shard_map/cond/branch_1_fun/ppermute | solution.py:192
  33.2 3.5 %chain.1 = f32[80,2048]{1,0:T(8,128)S(1)} custom-call(s32[4]{0:T(128)S(1)} %get-tuple-element.22.tile_ref, s32[4]{0:T(128)S(1)} %get-tuple-element.23.order_ref, s32[4,1024]{1,0:T(4,128)S(1)} %get-tuple-element.24.mask_ref, s32[4,256]{1,0:T(4,128)S(1)} %get-tuple-element.58.offset_ref, f32[4,256]{1,0:T(4,128)S(1)} %get-tuple-element.59.value_ref, ...), custom_call_target="tpu_custom_call" | custom-call | tf_op jit(solution)/shard_map/cond/branch_1_fun/chain/pallas_call | solution.py:213
  36.8 1.5 %collective-permute-done.7.refs_2_ = f32[40,2048]{1,0:T(8,128)S(1)} collective-permute-done((f32[40,2048]{1,0:T(8,128)S(1)}, f32[40,2048]{1,0:T(8,128)S(1)}, u32[]{:S(2)}, u32[]{:S(2)}) %collective-permute-start.7) | collective-permute-done | bytes 327712 | tf_op jit(solution)/shard_map/ppermute | solution.py:192
  38.3 1.5 %apply.3 = (f32[40,1024]{1,0:T(8,128)S(1)}, f32[40,1024]{1,0:T(8,128)S(1)}, f32[40,1024]{1,0:T(8,128)S(1)}, f32[40,1024]{1,0:T(8,128)S(1)}) custom-call(s32[4]{0:T(128)S(1)} %copy-done.2, s32[4,1024]{1,0:T(4,128)S(1)} %copy-done.1, f32[80,2048]{1,0:T(8,128)S(1)} %get-tuple-element.61.t_ref, f32[40,2048]{1,0:T(8,128)S(1)} %get-tuple-element.42.refs_0_, ...), custom_call_target="tpu_custom_call" | custom-call | tf_op jit(solution)/shard_map/apply/pallas_call | solution.py:268
  39.8 3.3 %collective-permute-start.15 = (f32[40,1024]{1,0:T(8,128)S(1)}, f32[40,1024]{1,0:T(8,128)S(1)}, u32[]{:S(2)}, u32[]{:S(2)}) collective-permute-start(f32[40,1024]{1,0:T(8,128)S(1)} %get-tuple-element.54), channel_id=1, source_target_pairs={{0,8},{8,0},{16,24},{24,16},{1,9},{9,1},{17,25},{25,17},{2,10},{10... | collective-permute-start | bytes 491528 | tf_op jit(solution)/shard_map/ppermute | solution.py:192
  43.1 1.7 %collective-permute-start.13 = (f32[40,1024]{1,0:T(8,128)S(1)}, f32[40,1024]{1,0:T(8,128)S(1)}, u32[]{:S(2)}, u32[]{:S(2)}) collective-permute-start(f32[40,1024]{1,0:T(8,128)S(1)} %get-tuple-element.51), channel_id=1, source_target_pairs={{0,16},{8,24},{16,0},{24,8},{1,17},{9,25},{17,1},{25,9},{2,18},{10... | collective-permute-start | bytes 491528 | tf_op jit(solution)/shard_map/ppermute | solution.py:192
  44.8 1.4 %collective-permute-start.14 = (f32[40,1024]{1,0:T(8,128)S(1)}, f32[40,1024]{1,0:T(8,128)S(1)}, u32[]{:S(2)}, u32[]{:S(2)}) collective-permute-start(f32[40,1024]{1,0:T(8,128)S(1)} %get-tuple-element.52), channel_id=1, source_target_pairs={{0,24},{8,16},{16,8},{24,0},{1,25},{9,17},{17,9},{25,1},{2,26},{10... | collective-permute-start | bytes 491528 | tf_op jit(solution)/shard_map/ppermute | solution.py:192
  46.2 1.5 %apply.2 = (f32[40,1024]{1,0:T(8,128)S(1)}, f32[40,1024]{1,0:T(8,128)S(1)}, f32[40,1024]{1,0:T(8,128)S(1)}, f32[40,1024]{1,0:T(8,128)S(1)}) custom-call(s32[4]{0:T(128)S(1)} %copy-done.2, s32[4,1024]{1,0:T(4,128)S(1)} %copy-done.1, f32[80,2048]{1,0:T(8,128)S(1)} %get-tuple-element.61.t_ref, f32[40,2048]{1,0:T(8,128)S(1)} %get-tuple-element.42.refs_0_, ...), custom_call_target="tpu_custom_call" | custom-call | tf_op jit(solution)/shard_map/apply/pallas_call | solution.py:268
  47.7 1.4 %collective-permute-start.11 = (f32[40,1024]{1,0:T(8,128)S(1)}, f32[40,1024]{1,0:T(8,128)S(1)}, u32[]{:S(2)}, u32[]{:S(2)}) collective-permute-start(f32[40,1024]{1,0:T(8,128)S(1)} %get-tuple-element.49), channel_id=1, source_target_pairs={{0,8},{8,0},{16,24},{24,16},{1,9},{9,1},{17,25},{25,17},{2,10},{10... | collective-permute-start | bytes 491528 | tf_op jit(solution)/shard_map/ppermute | solution.py:192
  49.1 2.0 %collective-permute-start.9 = (f32[40,1024]{1,0:T(8,128)S(1)}, f32[40,1024]{1,0:T(8,128)S(1)}, u32[]{:S(2)}, u32[]{:S(2)}) collective-permute-start(f32[40,1024]{1,0:T(8,128)S(1)} %get-tuple-element.46), channel_id=1, source_target_pairs={{0,16},{8,24},{16,0},{24,8},{1,17},{9,25},{17,1},{25,9},{2,18},{10... | collective-permute-start | bytes 491528 | tf_op jit(solution)/shard_map/ppermute | solution.py:192
  51.1 0.7 %collective-permute-done.15.refs_1_ = f32[40,1024]{1,0:T(8,128)S(1)} collective-permute-done((f32[40,1024]{1,0:T(8,128)S(1)}, f32[40,1024]{1,0:T(8,128)S(1)}, u32[]{:S(2)}, u32[]{:S(2)}) %collective-permute-start.15) | collective-permute-done | bytes 163872 | tf_op jit(solution)/shard_map/ppermute | solution.py:192
  51.8 2.3 %collective-permute-start.10 = (f32[40,1024]{1,0:T(8,128)S(1)}, f32[40,1024]{1,0:T(8,128)S(1)}, u32[]{:S(2)}, u32[]{:S(2)}) collective-permute-start(f32[40,1024]{1,0:T(8,128)S(1)} %get-tuple-element.47), channel_id=1, source_target_pairs={{0,24},{8,16},{16,8},{24,0},{1,25},{9,17},{17,9},{25,1},{2,26},{10... | collective-permute-start | bytes 491528 | tf_op jit(solution)/shard_map/ppermute | solution.py:192
  54.1 0.8 %unpack.4.refs_2_ = f32[20,16384]{1,0:T(8,128)} custom-call(f32[40,1024]{1,0:T(8,128)S(1)} %get-tuple-element.53.refs_0_, f32[40,1024]{1,0:T(8,128)S(1)} %collective-permute-done.15.refs_1_), custom_call_target="tpu_custom_call" | custom-call | tf_op jit(solution)/shard_map/unpack/pallas_call | solution.py:277
  54.9 3.2 %collective-permute-done.13.refs_0_ = f32[40,1024]{1,0:T(8,128)S(1)} collective-permute-done((f32[40,1024]{1,0:T(8,128)S(1)}, f32[40,1024]{1,0:T(8,128)S(1)}, u32[]{:S(2)}, u32[]{:S(2)}) %collective-permute-start.13) | collective-permute-done | bytes 163872 | tf_op jit(solution)/shard_map/ppermute | solution.py:192
  58.2 0.8 %unpack.5.refs_2_ = f32[20,16384]{1,0:T(8,128)} custom-call(f32[40,1024]{1,0:T(8,128)S(1)} %collective-permute-done.13.refs_0_, f32[40,1024]{1,0:T(8,128)S(1)} %collective-permute-done.14.refs_1_, f32[20,16384]{1,0:T(8,128)} %unpack.4.refs_2_), custom_call_target="tpu_custom_call", output_to_operand_aliasing={{}: (2, {})} | custom-call | tf_op jit(solution)/shard_map/unpack/pallas_call | solution.py:277
  59.0 0.8 %unpack.6.refs_2_ = f32[20,16384]{1,0:T(8,128)} custom-call(f32[40,1024]{1,0:T(8,128)S(1)} %get-tuple-element.48.refs_0_, f32[40,1024]{1,0:T(8,128)S(1)} %collective-permute-done.11.refs_1_, f32[20,16384]{1,0:T(8,128)} %unpack.5.refs_2_), custom_call_target="tpu_custom_call", output_to_operand_aliasing={{}: (2, {})} | custom-call | tf_op jit(solution)/shard_map/unpack/pallas_call | solution.py:277
  59.7 8.9 %collective-permute-done.9.refs_0_ = f32[40,1024]{1,0:T(8,128)S(1)} collective-permute-done((f32[40,1024]{1,0:T(8,128)S(1)}, f32[40,1024]{1,0:T(8,128)S(1)}, u32[]{:S(2)}, u32[]{:S(2)}) %collective-permute-start.9) | collective-permute-done | bytes 163872 | tf_op jit(solution)/shard_map/ppermute | solution.py:192
  68.7 0.8 %unpack.7 = f32[20,16384]{1,0:T(8,128)} custom-call(f32[40,1024]{1,0:T(8,128)S(1)} %collective-permute-done.9.refs_0_, f32[40,1024]{1,0:T(8,128)S(1)} %collective-permute-done.10.refs_1_, f32[20,16384]{1,0:T(8,128)} %unpack.6.refs_2_), custom_call_target="tpu_custom_call", output_to_operand_aliasing={{}: (2, {})} | custom-call | tf_op jit(solution)/shard_map/unpack/pallas_call | solution.py:277
  (28 shorter events, 1.1 us)
Async XLA Ops:
  0.0 1.4 %copy-start = (f32[20,16384]{1,0:T(8,128)S(1)}, f32[20,16384]{1,0:T(8,128)}, u32[]{:S(2)}) copy-start(f32[20,16384]{1,0:T(8,128)} %x_ref.3) | copy-start | bytes 3932164
  1.4 15.5 %copy-start.1 = (s32[4,1024]{1,0:T(4,128)S(1)}, s32[4,1024]{1,0:T(4,128)}, u32[]{:S(2)}) copy-start(s32[4,1024]{1,0:T(4,128)} %mask_ref.3) | copy-start | bytes 49156
  1.4 18.4 %copy-start.2 = (s32[4]{0:T(128)S(1)}, s32[4]{0:T(128)}, u32[]{:S(2)}) copy-start(s32[4]{0:T(128)} %order_ref.5) | copy-start | bytes 52
  1.4 18.5 %copy-start.3 = (s32[4,256]{1,0:T(4,128)S(1)}, s32[4,256]{1,0:T(4,128)}, u32[]{:S(2)}) copy-start(s32[4,256]{1,0:T(4,128)} %param.11) | copy-start | bytes 12292
  1.4 18.5 %copy-start.4 = (f32[4,256]{1,0:T(4,128)S(1)}, f32[4,256]{1,0:T(4,128)}, u32[]{:S(2)}) copy-start(f32[4,256]{1,0:T(4,128)} %param.12) | copy-start | bytes 12292
  1.4 18.5 %copy-start.5 = (f32[4,256]{1,0:T(4,128)S(1)}, f32[4,256]{1,0:T(4,128)}, u32[]{:S(2)}) copy-start(f32[4,256]{1,0:T(4,128)} %param.13) | copy-start | bytes 12292
  1.4 18.5 %copy-start.6 = (s32[4]{0:T(128)S(1)}, s32[4]{0:T(128)}, u32[]{:S(2)}) copy-start(s32[4]{0:T(128)} %tile_ref.1) | copy-start | bytes 52
  2.3 7.1 %collective-permute-start.5 = (f32[80,128]{1,0:T(8,128)S(1)}, f32[80,128]{1,0:T(8,128)S(1)}, u32[]{:S(2)}, u32[]{:S(2)}) collective-permute-start(f32[80,128]{1,0:T(8,128)S(1)} %seen.1.refs_0_), channel_id=1, source_target_pairs={{0,24},{8,16},{16,8},{24,0},{1,25},{9,17},{17,9},{25,1},{2,26},{10... | collective-permute-start | bytes 122888 | tf_op jit(solution)/shard_map/ppermute | solution.py:192
  7.4 4.9 %collective-permute-start.4 = (f32[80,128]{1,0:T(8,128)S(1)}, f32[80,128]{1,0:T(8,128)S(1)}, u32[]{:S(2)}, u32[]{:S(2)}) collective-permute-start(f32[80,128]{1,0:T(8,128)S(1)} %seen.1.refs_0_), channel_id=1, source_target_pairs={{0,16},{8,24},{16,0},{24,8},{1,17},{9,25},{17,1},{25,9},{2,18},{10... | collective-permute-start | bytes 122888 | tf_op jit(solution)/shard_map/ppermute | solution.py:192
  7.4 4.9 %collective-permute-start.3 = (f32[80,128]{1,0:T(8,128)S(1)}, f32[80,128]{1,0:T(8,128)S(1)}, u32[]{:S(2)}, u32[]{:S(2)}) collective-permute-start(f32[80,128]{1,0:T(8,128)S(1)} %seen.1.refs_0_), channel_id=1, source_target_pairs={{0,8},{8,0},{16,24},{24,16},{1,9},{9,1},{17,25},{25,17},{2,10},{10... | collective-permute-start | bytes 122888 | tf_op jit(solution)/shard_map/ppermute | solution.py:192
  12.4 24.3 %collective-permute-start.6 = (f32[40,2048]{1,0:T(8,128)S(1)}, f32[40,2048]{1,0:T(8,128)S(1)}, u32[]{:S(2)}, u32[]{:S(2)}) collective-permute-start(f32[40,2048]{1,0:T(8,128)S(1)} %get-tuple-element.43), channel_id=1, source_target_pairs={{0,8},{8,0},{16,24},{24,16},{1,9},{9,1},{17,25},{25,17},{2,10},{10... | collective-permute-start | bytes 983048 | tf_op jit(solution)/shard_map/ppermute | solution.py:192
  12.7 25.6 %collective-permute-start.7 = (f32[40,2048]{1,0:T(8,128)S(1)}, f32[40,2048]{1,0:T(8,128)S(1)}, u32[]{:S(2)}, u32[]{:S(2)}) collective-permute-start(f32[40,2048]{1,0:T(8,128)S(1)} %get-tuple-element.44), channel_id=1, source_target_pairs={{0,16},{8,24},{16,0},{24,8},{1,17},{9,25},{17,1},{25,9},{2,18},{10... | collective-permute-start | bytes 983048 | tf_op jit(solution)/shard_map/ppermute | solution.py:192
  14.7 22.1 %collective-permute-start.12 = (f32[40,1024]{1,0:T(8,128)S(1)}, f32[40,1024]{1,0:T(8,128)S(1)}, u32[]{:S(2)}, u32[]{:S(2)}) collective-permute-start(f32[40,1024]{1,0:T(8,128)S(1)} %get-tuple-element.50), channel_id=1, source_target_pairs={{0,24},{8,16},{16,8},{24,0},{1,25},{9,17},{17,9},{25,1},{2,26},{10... | collective-permute-start | bytes 491528 | tf_op jit(solution)/shard_map/ppermute | solution.py:192
  18.2 28.0 %collective-permute-start.8 = (f32[40,1024]{1,0:T(8,128)S(1)}, f32[40,1024]{1,0:T(8,128)S(1)}, u32[]{:S(2)}, u32[]{:S(2)}) collective-permute-start(f32[40,1024]{1,0:T(8,128)S(1)} %get-tuple-element.45), channel_id=1, source_target_pairs={{0,24},{8,16},{16,8},{24,0},{1,25},{9,17},{17,9},{25,1},{2,26},{10... | collective-permute-start | bytes 491528 | tf_op jit(solution)/shard_map/ppermute | solution.py:192
  19.9 1.5 %collective-permute-start = (f32[320,128]{1,0:T(8,128)S(1)}, f32[320,128]{1,0:T(8,128)S(1)}, u32[]{:S(2)}, u32[]{:S(2)}) collective-permute-start(f32[320,128]{1,0:T(8,128)S(1)} %get-tuple-element.28), channel_id=1, source_target_pairs={{0,1},{1,0},{2,3},{3,2},{4,5},{5,4},{6,7},{7,6},{8,9},{9,8},{10,11... | collective-permute-start | bytes 491528 | tf_op jit(solution)/shard_map/cond/branch_1_fun/ppermute | solution.py:192
  21.4 6.3 %collective-permute-start.1 = (f32[320,128]{1,0:T(8,128)S(1)}, f32[320,128]{1,0:T(8,128)S(1)}, u32[]{:S(2)}, u32[]{:S(2)}) collective-permute-start(f32[320,128]{1,0:T(8,128)S(1)} %add.4), channel_id=1, source_target_pairs={{0,2},{1,3},{2,0},{3,1},{4,6},{5,7},{6,4},{7,5},{8,10},{9,11},{10,... | collective-permute-start | bytes 491528 | tf_op jit(solution)/shard_map/cond/branch_1_fun/ppermute | solution.py:192
  27.7 5.5 %collective-permute-start.2 = (f32[320,128]{1,0:T(8,128)S(1)}, f32[320,128]{1,0:T(8,128)S(1)}, u32[]{:S(2)}, u32[]{:S(2)}) collective-permute-start(f32[320,128]{1,0:T(8,128)S(1)} %add.5.one_ref), channel_id=1, source_target_pairs={{0,4},{1,5},{2,6},{3,7},{4,0},{5,1},{6,2},{7,3},{8,12},{9,13},{10,... | collective-permute-start | bytes 491528 | tf_op jit(solution)/shard_map/cond/branch_1_fun/ppermute | solution.py:192
  39.8 12.0 %collective-permute-start.15 = (f32[40,1024]{1,0:T(8,128)S(1)}, f32[40,1024]{1,0:T(8,128)S(1)}, u32[]{:S(2)}, u32[]{:S(2)}) collective-permute-start(f32[40,1024]{1,0:T(8,128)S(1)} %get-tuple-element.54), channel_id=1, source_target_pairs={{0,8},{8,0},{16,24},{24,16},{1,9},{9,1},{17,25},{25,17},{2,10},{10... | collective-permute-start | bytes 491528 | tf_op jit(solution)/shard_map/ppermute | solution.py:192
  43.1 15.1 %collective-permute-start.13 = (f32[40,1024]{1,0:T(8,128)S(1)}, f32[40,1024]{1,0:T(8,128)S(1)}, u32[]{:S(2)}, u32[]{:S(2)}) collective-permute-start(f32[40,1024]{1,0:T(8,128)S(1)} %get-tuple-element.51), channel_id=1, source_target_pairs={{0,16},{8,24},{16,0},{24,8},{1,17},{9,25},{17,1},{25,9},{2,18},{10... | collective-permute-start | bytes 491528 | tf_op jit(solution)/shard_map/ppermute | solution.py:192
  44.8 13.3 %collective-permute-start.14 = (f32[40,1024]{1,0:T(8,128)S(1)}, f32[40,1024]{1,0:T(8,128)S(1)}, u32[]{:S(2)}, u32[]{:S(2)}) collective-permute-start(f32[40,1024]{1,0:T(8,128)S(1)} %get-tuple-element.52), channel_id=1, source_target_pairs={{0,24},{8,16},{16,8},{24,0},{1,25},{9,17},{17,9},{25,1},{2,26},{10... | collective-permute-start | bytes 491528 | tf_op jit(solution)/shard_map/ppermute | solution.py:192
  47.7 11.2 %collective-permute-start.11 = (f32[40,1024]{1,0:T(8,128)S(1)}, f32[40,1024]{1,0:T(8,128)S(1)}, u32[]{:S(2)}, u32[]{:S(2)}) collective-permute-start(f32[40,1024]{1,0:T(8,128)S(1)} %get-tuple-element.49), channel_id=1, source_target_pairs={{0,8},{8,0},{16,24},{24,16},{1,9},{9,1},{17,25},{25,17},{2,10},{10... | collective-permute-start | bytes 491528 | tf_op jit(solution)/shard_map/ppermute | solution.py:192
  49.1 19.6 %collective-permute-start.9 = (f32[40,1024]{1,0:T(8,128)S(1)}, f32[40,1024]{1,0:T(8,128)S(1)}, u32[]{:S(2)}, u32[]{:S(2)}) collective-permute-start(f32[40,1024]{1,0:T(8,128)S(1)} %get-tuple-element.46), channel_id=1, source_target_pairs={{0,16},{8,24},{16,0},{24,8},{1,17},{9,25},{17,1},{25,9},{2,18},{10... | collective-permute-start | bytes 491528 | tf_op jit(solution)/shard_map/ppermute | solution.py:192
  51.8 16.9 %collective-permute-start.10 = (f32[40,1024]{1,0:T(8,128)S(1)}, f32[40,1024]{1,0:T(8,128)S(1)}, u32[]{:S(2)}, u32[]{:S(2)}) collective-permute-start(f32[40,1024]{1,0:T(8,128)S(1)} %get-tuple-element.47), channel_id=1, source_target_pairs={{0,24},{8,16},{16,8},{24,0},{1,25},{9,17},{17,9},{25,1},{2,26},{10... | collective-permute-start | bytes 491528 | tf_op jit(solution)/shard_map/ppermute | solution.py:192

commit v6 on v5

--- a/solution.py
+++ b/solution.py
@@ -272,7 +272,7 @@
             [SMEM] * 2 + [VMEM] * (1 + len(jobs)),
             [VMEM] * n_mem,
         )(block_order, loc_mask, matrices, *[held[job] for job in jobs])
-        back = [updated[0]] + [swap(updated[d], "mem", d) for d in range(1, n_mem)]
+        back = [updated[0]] + [swap(updated[d], "mem", d) for d in range(n_mem - 1, 0, -1)][::-1]
         for shifts in (range(2), range(2, n_mem)):
             result = kernel_call(
                 functools.partial(unpack_kernel, parts, quarter, [chunk[:2] for chunk in chunks], shifts),

time: 69.9 us -> 69.9 us (level)
  no operation moved by 1% of the time
where the time goes in v6:
time: 69.9 us; the launch traced here: 69.5 us
  waiting for transfers between devices  28.7 us (41%)
  starting transfers between devices  27.2 us (39%)
  Pallas kernels  10.7 us (15%)
  local copies, waits for them, and re-layouts  1.43 us (2%)
  between operations  0.81 us (1%)
    ppermute x16, waiting for transfers between devices, swap(): lax.ppermute(value, axis, [(j, j ^ by) for j in range(lax.axis_size(axis))])  28.7 us
    ppermute x16, starting transfers between devices, swap(): lax.ppermute(value, axis, [(j, j ^ by) for j in range(lax.axis_size(axis))])  27.2 us
    pallas_call x1, Pallas kernels, update_matrices(): kernel_call(functools.partial(chain_kernel, places), 'chain', jax.ShapeDt...  3.51 us
    pallas_call x4, Pallas kernels, on_device(): kernel_call(functools.partial(unpack_kernel, parts, quarter, [chunk[:2] f...  3.13 us
    pallas_call x2, Pallas kernels, on_device(): kernel_call(functools.partial(apply_kernel, n_mem, parts, quarter, chunks...  3.02 us
    unnamed x14, local copies, waits for them, and re-layouts  1.43 us
  transfers between devices with their start and end apart: 16, of which 9 were waited for; matrix products, arithmetic and copies ran while one was open for 1% of the time, Pallas kernels for 13%

profile of v6, /device:TPU:0, one launch (start us, length us, event | category | flops | bytes accessed | tf_op | source)
XLA Modules:
  0.0 69.5 jit_solution(14101213156879639413)
XLA Ops:
  0.0 1.4 %copy-done = f32[20,16384]{1,0:T(8,128)S(1)} copy-done((f32[20,16384]{1,0:T(8,128)S(1)}, f32[20,16384]{1,0:T(8,128)}, u32[]{:S(2)}) %copy-start) | copy-done | bytes 1310744
  1.4 0.9 %seen.1.refs_0_ = f32[80,128]{1,0:T(8,128)S(1)} custom-call(s32[4]{0:T(128)} %tile_ref.1, s32[4]{0:T(128)} %order_ref.5, f32[20,16384]{1,0:T(8,128)S(1)} %copy-done), custom_call_target="tpu_custom_call" | custom-call | tf_op jit(solution)/shard_map/seen/pallas_call | solution.py:225
  2.3 5.1 %collective-permute-start.5 = (f32[80,128]{1,0:T(8,128)S(1)}, f32[80,128]{1,0:T(8,128)S(1)}, u32[]{:S(2)}, u32[]{:S(2)}) collective-permute-start(f32[80,128]{1,0:T(8,128)S(1)} %seen.1.refs_0_), channel_id=1, source_target_pairs={{0,24},{8,16},{16,8},{24,0},{1,25},{9,17},{17,9},{25,1},{2,26},{10... | collective-permute-start | bytes 122888 | tf_op jit(solution)/shard_map/ppermute | solution.py:192
  8.1 1.4 %collective-permute-done.5.refs_3_ = f32[80,128]{1,0:T(8,128)S(1)} collective-permute-done((f32[80,128]{1,0:T(8,128)S(1)}, f32[80,128]{1,0:T(8,128)S(1)}, u32[]{:S(2)}, u32[]{:S(2)}) %collective-permute-start.5) | collective-permute-done | bytes 40992 | tf_op jit(solution)/shard_map/ppermute | solution.py:192
  9.4 2.9 %collective-permute-done.4.refs_2_ = f32[80,128]{1,0:T(8,128)S(1)} collective-permute-done((f32[80,128]{1,0:T(8,128)S(1)}, f32[80,128]{1,0:T(8,128)S(1)}, u32[]{:S(2)}, u32[]{:S(2)}) %collective-permute-start.4) | collective-permute-done | bytes 40992 | tf_op jit(solution)/shard_map/ppermute | solution.py:192
  12.7 2.0 %collective-permute-start.7 = (f32[40,2048]{1,0:T(8,128)S(1)}, f32[40,2048]{1,0:T(8,128)S(1)}, u32[]{:S(2)}, u32[]{:S(2)}) collective-permute-start(f32[40,2048]{1,0:T(8,128)S(1)} %get-tuple-element.44), channel_id=1, source_target_pairs={{0,16},{8,24},{16,0},{24,8},{1,17},{9,25},{17,1},{25,9},{2,18},{10... | collective-permute-start | bytes 983048 | tf_op jit(solution)/shard_map/ppermute | solution.py:192
  14.7 2.2 %collective-permute-start.12 = (f32[40,1024]{1,0:T(8,128)S(1)}, f32[40,1024]{1,0:T(8,128)S(1)}, u32[]{:S(2)}, u32[]{:S(2)}) collective-permute-start(f32[40,1024]{1,0:T(8,128)S(1)} %get-tuple-element.50), channel_id=1, source_target_pairs={{0,24},{8,16},{16,8},{24,0},{1,25},{9,17},{17,9},{25,1},{2,26},{10... | collective-permute-start | bytes 491528 | tf_op jit(solution)/shard_map/ppermute | solution.py:192
  16.9 0.6 compare_reduce_fusion
  18.2 1.6 %collective-permute-start.8 = (f32[40,1024]{1,0:T(8,128)S(1)}, f32[40,1024]{1,0:T(8,128)S(1)}, u32[]{:S(2)}, u32[]{:S(2)}) collective-permute-start(f32[40,1024]{1,0:T(8,128)S(1)} %get-tuple-element.45), channel_id=1, source_target_pairs={{0,24},{8,16},{16,8},{24,0},{1,25},{9,17},{17,9},{25,1},{2,26},{10... | collective-permute-start | bytes 491528 | tf_op jit(solution)/shard_map/ppermute | solution.py:192
  19.9 16.8 %conditional.1 = (f32[80,2048]{1,0:T(8,128)S(1)}) conditional(s32[]{:T(128)} %convert_element_type.10, () %tuple.11, (f32[320,128]{1,0:T(8,128)S(1)}, s32[4]{0:T(128)S(1)}, s32[4]{0:T(128)S(1)}, s32[4,1024]{1,0:T(4,128)S(1)}, s32[4,256]{1,0:T(4,128)S(1)}, /*index=5*/f32[4,256]{1,0:T(4,128)S(1)}, f32[4,256]{1,0:T(4,128)S(1)}) %tuple.20), branch_computations={%region_1.0_spmd, %region_2.0_spmd} | conditional | flops 81920 | bytes 2949248 | solution.py:256
  20.0 1.4 %collective-permute-done = f32[320,128]{1,0:T(8,128)S(1)} collective-permute-done((f32[320,128]{1,0:T(8,128)S(1)}, f32[320,128]{1,0:T(8,128)S(1)}, u32[]{:S(2)}, u32[]{:S(2)}) %collective-permute-start) | collective-permute-done | bytes 163872 | tf_op jit(solution)/shard_map/cond/branch_1_fun/ppermute | solution.py:192
  21.4 1.6 %collective-permute-start.1 = (f32[320,128]{1,0:T(8,128)S(1)}, f32[320,128]{1,0:T(8,128)S(1)}, u32[]{:S(2)}, u32[]{:S(2)}) collective-permute-start(f32[320,128]{1,0:T(8,128)S(1)} %add.4), channel_id=1, source_target_pairs={{0,2},{1,3},{2,0},{3,1},{4,6},{5,7},{6,4},{7,5},{8,10},{9,11},{10,... | collective-permute-start | bytes 491528 | tf_op jit(solution)/shard_map/cond/branch_1_fun/ppermute | solution.py:192
  23.0 4.8 %collective-permute-done.1 = f32[320,128]{1,0:T(8,128)S(1)} collective-permute-done((f32[320,128]{1,0:T(8,128)S(1)}, f32[320,128]{1,0:T(8,128)S(1)}, u32[]{:S(2)}, u32[]{:S(2)}) %collective-permute-start.1) | collective-permute-done | bytes 163872 | tf_op jit(solution)/shard_map/cond/branch_1_fun/ppermute | solution.py:192
  27.7 1.6 %collective-permute-start.2 = (f32[320,128]{1,0:T(8,128)S(1)}, f32[320,128]{1,0:T(8,128)S(1)}, u32[]{:S(2)}, u32[]{:S(2)}) collective-permute-start(f32[320,128]{1,0:T(8,128)S(1)} %add.5.one_ref), channel_id=1, source_target_pairs={{0,4},{1,5},{2,6},{3,7},{4,0},{5,1},{6,2},{7,3},{8,12},{9,13},{10,... | collective-permute-start | bytes 491528 | tf_op jit(solution)/shard_map/cond/branch_1_fun/ppermute | solution.py:192
  29.3 3.9 %collective-permute-done.2.two_ref = f32[320,128]{1,0:T(8,128)S(1)} collective-permute-done((f32[320,128]{1,0:T(8,128)S(1)}, f32[320,128]{1,0:T(8,128)S(1)}, u32[]{:S(2)}, u32[]{:S(2)}) %collective-permute-start.2) | collective-permute-done | bytes 163872 | tf_op jit(solution)/shard_map/cond/branch_1_fun/ppermute | solution.py:192
  33.2 3.5 %chain.1 = f32[80,2048]{1,0:T(8,128)S(1)} custom-call(s32[4]{0:T(128)S(1)} %get-tuple-element.22.tile_ref, s32[4]{0:T(128)S(1)} %get-tuple-element.23.order_ref, s32[4,1024]{1,0:T(4,128)S(1)} %get-tuple-element.24.mask_ref, s32[4,256]{1,0:T(4,128)S(1)} %get-tuple-element.58.offset_ref, f32[4,256]{1,0:T(4,128)S(1)} %get-tuple-element.59.value_ref, ...), custom_call_target="tpu_custom_call" | custom-call | tf_op jit(solution)/shard_map/cond/branch_1_fun/chain/pallas_call | solution.py:213
  36.8 1.5 %collective-permute-done.7.refs_2_ = f32[40,2048]{1,0:T(8,128)S(1)} collective-permute-done((f32[40,2048]{1,0:T(8,128)S(1)}, f32[40,2048]{1,0:T(8,128)S(1)}, u32[]{:S(2)}, u32[]{:S(2)}) %collective-permute-start.7) | collective-permute-done | bytes 327712 | tf_op jit(solution)/shard_map/ppermute | solution.py:192
  38.3 1.5 %apply.3 = (f32[40,1024]{1,0:T(8,128)S(1)}, f32[40,1024]{1,0:T(8,128)S(1)}, f32[40,1024]{1,0:T(8,128)S(1)}, f32[40,1024]{1,0:T(8,128)S(1)}) custom-call(s32[4]{0:T(128)S(1)} %copy-done.2, s32[4,1024]{1,0:T(4,128)S(1)} %copy-done.1, f32[80,2048]{1,0:T(8,128)S(1)} %get-tuple-element.61.t_ref, f32[40,2048]{1,0:T(8,128)S(1)} %get-tuple-element.42.refs_0_, ...), custom_call_target="tpu_custom_call" | custom-call | tf_op jit(solution)/shard_map/apply/pallas_call | solution.py:268
  39.8 3.3 %collective-permute-start.15 = (f32[40,1024]{1,0:T(8,128)S(1)}, f32[40,1024]{1,0:T(8,128)S(1)}, u32[]{:S(2)}, u32[]{:S(2)}) collective-permute-start(f32[40,1024]{1,0:T(8,128)S(1)} %get-tuple-element.54), channel_id=1, source_target_pairs={{0,8},{8,0},{16,24},{24,16},{1,9},{9,1},{17,25},{25,17},{2,10},{10... | collective-permute-start | bytes 491528 | tf_op jit(solution)/shard_map/ppermute | solution.py:192
  43.1 1.7 %collective-permute-start.13 = (f32[40,1024]{1,0:T(8,128)S(1)}, f32[40,1024]{1,0:T(8,128)S(1)}, u32[]{:S(2)}, u32[]{:S(2)}) collective-permute-start(f32[40,1024]{1,0:T(8,128)S(1)} %get-tuple-element.51), channel_id=1, source_target_pairs={{0,16},{8,24},{16,0},{24,8},{1,17},{9,25},{17,1},{25,9},{2,18},{10... | collective-permute-start | bytes 491528 | tf_op jit(solution)/shard_map/ppermute | solution.py:192
  44.8 1.4 %collective-permute-start.14 = (f32[40,1024]{1,0:T(8,128)S(1)}, f32[40,1024]{1,0:T(8,128)S(1)}, u32[]{:S(2)}, u32[]{:S(2)}) collective-permute-start(f32[40,1024]{1,0:T(8,128)S(1)} %get-tuple-element.52), channel_id=1, source_target_pairs={{0,24},{8,16},{16,8},{24,0},{1,25},{9,17},{17,9},{25,1},{2,26},{10... | collective-permute-start | bytes 491528 | tf_op jit(solution)/shard_map/ppermute | solution.py:192
  46.2 1.5 %apply.2 = (f32[40,1024]{1,0:T(8,128)S(1)}, f32[40,1024]{1,0:T(8,128)S(1)}, f32[40,1024]{1,0:T(8,128)S(1)}, f32[40,1024]{1,0:T(8,128)S(1)}) custom-call(s32[4]{0:T(128)S(1)} %copy-done.2, s32[4,1024]{1,0:T(4,128)S(1)} %copy-done.1, f32[80,2048]{1,0:T(8,128)S(1)} %get-tuple-element.61.t_ref, f32[40,2048]{1,0:T(8,128)S(1)} %get-tuple-element.42.refs_0_, ...), custom_call_target="tpu_custom_call" | custom-call | tf_op jit(solution)/shard_map/apply/pallas_call | solution.py:268
  47.7 1.4 %collective-permute-start.11 = (f32[40,1024]{1,0:T(8,128)S(1)}, f32[40,1024]{1,0:T(8,128)S(1)}, u32[]{:S(2)}, u32[]{:S(2)}) collective-permute-start(f32[40,1024]{1,0:T(8,128)S(1)} %get-tuple-element.49), channel_id=1, source_target_pairs={{0,8},{8,0},{16,24},{24,16},{1,9},{9,1},{17,25},{25,17},{2,10},{10... | collective-permute-start | bytes 491528 | tf_op jit(solution)/shard_map/ppermute | solution.py:192
  49.1 2.0 %collective-permute-start.9 = (f32[40,1024]{1,0:T(8,128)S(1)}, f32[40,1024]{1,0:T(8,128)S(1)}, u32[]{:S(2)}, u32[]{:S(2)}) collective-permute-start(f32[40,1024]{1,0:T(8,128)S(1)} %get-tuple-element.46), channel_id=1, source_target_pairs={{0,16},{8,24},{16,0},{24,8},{1,17},{9,25},{17,1},{25,9},{2,18},{10... | collective-permute-start | bytes 491528 | tf_op jit(solution)/shard_map/ppermute | solution.py:192
  51.1 0.7 %collective-permute-done.15.refs_1_ = f32[40,1024]{1,0:T(8,128)S(1)} collective-permute-done((f32[40,1024]{1,0:T(8,128)S(1)}, f32[40,1024]{1,0:T(8,128)S(1)}, u32[]{:S(2)}, u32[]{:S(2)}) %collective-permute-start.15) | collective-permute-done | bytes 163872 | tf_op jit(solution)/shard_map/ppermute | solution.py:192
  51.8 2.3 %collective-permute-start.10 = (f32[40,1024]{1,0:T(8,128)S(1)}, f32[40,1024]{1,0:T(8,128)S(1)}, u32[]{:S(2)}, u32[]{:S(2)}) collective-permute-start(f32[40,1024]{1,0:T(8,128)S(1)} %get-tuple-element.47), channel_id=1, source_target_pairs={{0,24},{8,16},{16,8},{24,0},{1,25},{9,17},{17,9},{25,1},{2,26},{10... | collective-permute-start | bytes 491528 | tf_op jit(solution)/shard_map/ppermute | solution.py:192
  54.1 0.8 %unpack.4.refs_2_ = f32[20,16384]{1,0:T(8,128)} custom-call(f32[40,1024]{1,0:T(8,128)S(1)} %get-tuple-element.53.refs_0_, f32[40,1024]{1,0:T(8,128)S(1)} %collective-permute-done.15.refs_1_), custom_call_target="tpu_custom_call" | custom-call | tf_op jit(solution)/shard_map/unpack/pallas_call | solution.py:277
  54.9 3.2 %collective-permute-done.13.refs_0_ = f32[40,1024]{1,0:T(8,128)S(1)} collective-permute-done((f32[40,1024]{1,0:T(8,128)S(1)}, f32[40,1024]{1,0:T(8,128)S(1)}, u32[]{:S(2)}, u32[]{:S(2)}) %collective-permute-start.13) | collective-permute-done | bytes 163872 | tf_op jit(solution)/shard_map/ppermute | solution.py:192
  58.2 0.8 %unpack.5.refs_2_ = f32[20,16384]{1,0:T(8,128)} custom-call(f32[40,1024]{1,0:T(8,128)S(1)} %collective-permute-done.13.refs_0_, f32[40,1024]{1,0:T(8,128)S(1)} %collective-permute-done.14.refs_1_, f32[20,16384]{1,0:T(8,128)} %unpack.4.refs_2_), custom_call_target="tpu_custom_call", output_to_operand_aliasing={{}: (2, {})} | custom-call | tf_op jit(solution)/shard_map/unpack/pallas_call | solution.py:277
  59.0 0.8 %unpack.6.refs_2_ = f32[20,16384]{1,0:T(8,128)} custom-call(f32[40,1024]{1,0:T(8,128)S(1)} %get-tuple-element.48.refs_0_, f32[40,1024]{1,0:T(8,128)S(1)} %collective-permute-done.11.refs_1_, f32[20,16384]{1,0:T(8,128)} %unpack.5.refs_2_), custom_call_target="tpu_custom_call", output_to_operand_aliasing={{}: (2, {})} | custom-call | tf_op jit(solution)/shard_map/unpack/pallas_call | solution.py:277
  59.7 8.9 %collective-permute-done.9.refs_0_ = f32[40,1024]{1,0:T(8,128)S(1)} collective-permute-done((f32[40,1024]{1,0:T(8,128)S(1)}, f32[40,1024]{1,0:T(8,128)S(1)}, u32[]{:S(2)}, u32[]{:S(2)}) %collective-permute-start.9) | collective-permute-done | bytes 163872 | tf_op jit(solution)/shard_map/ppermute | solution.py:192
  68.7 0.8 %unpack.7 = f32[20,16384]{1,0:T(8,128)} custom-call(f32[40,1024]{1,0:T(8,128)S(1)} %collective-permute-done.9.refs_0_, f32[40,1024]{1,0:T(8,128)S(1)} %collective-permute-done.10.refs_1_, f32[20,16384]{1,0:T(8,128)} %unpack.6.refs_2_), custom_call_target="tpu_custom_call", output_to_operand_aliasing={{}: (2, {})} | custom-call | tf_op jit(solution)/shard_map/unpack/pallas_call | solution.py:277
  (28 shorter events, 1.1 us)
Async XLA Ops:
  0.0 1.4 %copy-start = (f32[20,16384]{1,0:T(8,128)S(1)}, f32[20,16384]{1,0:T(8,128)}, u32[]{:S(2)}) copy-start(f32[20,16384]{1,0:T(8,128)} %x_ref.3) | copy-start | bytes 3932164
  1.4 15.5 %copy-start.1 = (s32[4,1024]{1,0:T(4,128)S(1)}, s32[4,1024]{1,0:T(4,128)}, u32[]{:S(2)}) copy-start(s32[4,1024]{1,0:T(4,128)} %mask_ref.3) | copy-start | bytes 49156
  1.4 18.4 %copy-start.2 = (s32[4]{0:T(128)S(1)}, s32[4]{0:T(128)}, u32[]{:S(2)}) copy-start(s32[4]{0:T(128)} %order_ref.5) | copy-start | bytes 52
  1.4 18.5 %copy-start.3 = (s32[4,256]{1,0:T(4,128)S(1)}, s32[4,256]{1,0:T(4,128)}, u32[]{:S(2)}) copy-start(s32[4,256]{1,0:T(4,128)} %param.11) | copy-start | bytes 12292
  1.4 18.5 %copy-start.4 = (f32[4,256]{1,0:T(4,128)S(1)}, f32[4,256]{1,0:T(4,128)}, u32[]{:S(2)}) copy-start(f32[4,256]{1,0:T(4,128)} %param.12) | copy-start | bytes 12292
  1.4 18.5 %copy-start.5 = (f32[4,256]{1,0:T(4,128)S(1)}, f32[4,256]{1,0:T(4,128)}, u32[]{:S(2)}) copy-start(f32[4,256]{1,0:T(4,128)} %param.13) | copy-start | bytes 12292
  1.4 18.5 %copy-start.6 = (s32[4]{0:T(128)S(1)}, s32[4]{0:T(128)}, u32[]{:S(2)}) copy-start(s32[4]{0:T(128)} %tile_ref.1) | copy-start | bytes 52
  2.3 7.1 %collective-permute-start.5 = (f32[80,128]{1,0:T(8,128)S(1)}, f32[80,128]{1,0:T(8,128)S(1)}, u32[]{:S(2)}, u32[]{:S(2)}) collective-permute-start(f32[80,128]{1,0:T(8,128)S(1)} %seen.1.refs_0_), channel_id=1, source_target_pairs={{0,24},{8,16},{16,8},{24,0},{1,25},{9,17},{17,9},{25,1},{2,26},{10... | collective-permute-start | bytes 122888 | tf_op jit(solution)/shard_map/ppermute | solution.py:192
  7.4 4.9 %collective-permute-start.4 = (f32[80,128]{1,0:T(8,128)S(1)}, f32[80,128]{1,0:T(8,128)S(1)}, u32[]{:S(2)}, u32[]{:S(2)}) collective-permute-start(f32[80,128]{1,0:T(8,128)S(1)} %seen.1.refs_0_), channel_id=1, source_target_pairs={{0,16},{8,24},{16,0},{24,8},{1,17},{9,25},{17,1},{25,9},{2,18},{10... | collective-permute-start | bytes 122888 | tf_op jit(solution)/shard_map/ppermute | solution.py:192
  7.4 4.9 %collective-permute-start.3 = (f32[80,128]{1,0:T(8,128)S(1)}, f32[80,128]{1,0:T(8,128)S(1)}, u32[]{:S(2)}, u32[]{:S(2)}) collective-permute-start(f32[80,128]{1,0:T(8,128)S(1)} %seen.1.refs_0_), channel_id=1, source_target_pairs={{0,8},{8,0},{16,24},{24,16},{1,9},{9,1},{17,25},{25,17},{2,10},{10... | collective-permute-start | bytes 122888 | tf_op jit(solution)/shard_map/ppermute | solution.py:192
  12.4 24.3 %collective-permute-start.6 = (f32[40,2048]{1,0:T(8,128)S(1)}, f32[40,2048]{1,0:T(8,128)S(1)}, u32[]{:S(2)}, u32[]{:S(2)}) collective-permute-start(f32[40,2048]{1,0:T(8,128)S(1)} %get-tuple-element.43), channel_id=1, source_target_pairs={{0,8},{8,0},{16,24},{24,16},{1,9},{9,1},{17,25},{25,17},{2,10},{10... | collective-permute-start | bytes 983048 | tf_op jit(solution)/shard_map/ppermute | solution.py:192
  12.7 25.6 %collective-permute-start.7 = (f32[40,2048]{1,0:T(8,128)S(1)}, f32[40,2048]{1,0:T(8,128)S(1)}, u32[]{:S(2)}, u32[]{:S(2)}) collective-permute-start(f32[40,2048]{1,0:T(8,128)S(1)} %get-tuple-element.44), channel_id=1, source_target_pairs={{0,16},{8,24},{16,0},{24,8},{1,17},{9,25},{17,1},{25,9},{2,18},{10... | collective-permute-start | bytes 983048 | tf_op jit(solution)/shard_map/ppermute | solution.py:192
  14.7 22.1 %collective-permute-start.12 = (f32[40,1024]{1,0:T(8,128)S(1)}, f32[40,1024]{1,0:T(8,128)S(1)}, u32[]{:S(2)}, u32[]{:S(2)}) collective-permute-start(f32[40,1024]{1,0:T(8,128)S(1)} %get-tuple-element.50), channel_id=1, source_target_pairs={{0,24},{8,16},{16,8},{24,0},{1,25},{9,17},{17,9},{25,1},{2,26},{10... | collective-permute-start | bytes 491528 | tf_op jit(solution)/shard_map/ppermute | solution.py:192
  18.2 28.0 %collective-permute-start.8 = (f32[40,1024]{1,0:T(8,128)S(1)}, f32[40,1024]{1,0:T(8,128)S(1)}, u32[]{:S(2)}, u32[]{:S(2)}) collective-permute-start(f32[40,1024]{1,0:T(8,128)S(1)} %get-tuple-element.45), channel_id=1, source_target_pairs={{0,24},{8,16},{16,8},{24,0},{1,25},{9,17},{17,9},{25,1},{2,26},{10... | collective-permute-start | bytes 491528 | tf_op jit(solution)/shard_map/ppermute | solution.py:192
  19.9 1.5 %collective-permute-start = (f32[320,128]{1,0:T(8,128)S(1)}, f32[320,128]{1,0:T(8,128)S(1)}, u32[]{:S(2)}, u32[]{:S(2)}) collective-permute-start(f32[320,128]{1,0:T(8,128)S(1)} %get-tuple-element.28), channel_id=1, source_target_pairs={{0,1},{1,0},{2,3},{3,2},{4,5},{5,4},{6,7},{7,6},{8,9},{9,8},{10,11... | collective-permute-start | bytes 491528 | tf_op jit(solution)/shard_map/cond/branch_1_fun/ppermute | solution.py:192
  21.4 6.3 %collective-permute-start.1 = (f32[320,128]{1,0:T(8,128)S(1)}, f32[320,128]{1,0:T(8,128)S(1)}, u32[]{:S(2)}, u32[]{:S(2)}) collective-permute-start(f32[320,128]{1,0:T(8,128)S(1)} %add.4), channel_id=1, source_target_pairs={{0,2},{1,3},{2,0},{3,1},{4,6},{5,7},{6,4},{7,5},{8,10},{9,11},{10,... | collective-permute-start | bytes 491528 | tf_op jit(solution)/shard_map/cond/branch_1_fun/ppermute | solution.py:192
  27.7 5.5 %collective-permute-start.2 = (f32[320,128]{1,0:T(8,128)S(1)}, f32[320,128]{1,0:T(8,128)S(1)}, u32[]{:S(2)}, u32[]{:S(2)}) collective-permute-start(f32[320,128]{1,0:T(8,128)S(1)} %add.5.one_ref), channel_id=1, source_target_pairs={{0,4},{1,5},{2,6},{3,7},{4,0},{5,1},{6,2},{7,3},{8,12},{9,13},{10,... | collective-permute-start | bytes 491528 | tf_op jit(solution)/shard_map/cond/branch_1_fun/ppermute | solution.py:192
  39.8 12.0 %collective-permute-start.15 = (f32[40,1024]{1,0:T(8,128)S(1)}, f32[40,1024]{1,0:T(8,128)S(1)}, u32[]{:S(2)}, u32[]{:S(2)}) collective-permute-start(f32[40,1024]{1,0:T(8,128)S(1)} %get-tuple-element.54), channel_id=1, source_target_pairs={{0,8},{8,0},{16,24},{24,16},{1,9},{9,1},{17,25},{25,17},{2,10},{10... | collective-permute-start | bytes 491528 | tf_op jit(solution)/shard_map/ppermute | solution.py:192
  43.1 15.1 %collective-permute-start.13 = (f32[40,1024]{1,0:T(8,128)S(1)}, f32[40,1024]{1,0:T(8,128)S(1)}, u32[]{:S(2)}, u32[]{:S(2)}) collective-permute-start(f32[40,1024]{1,0:T(8,128)S(1)} %get-tuple-element.51), channel_id=1, source_target_pairs={{0,16},{8,24},{16,0},{24,8},{1,17},{9,25},{17,1},{25,9},{2,18},{10... | collective-permute-start | bytes 491528 | tf_op jit(solution)/shard_map/ppermute | solution.py:192
  44.8 13.3 %collective-permute-start.14 = (f32[40,1024]{1,0:T(8,128)S(1)}, f32[40,1024]{1,0:T(8,128)S(1)}, u32[]{:S(2)}, u32[]{:S(2)}) collective-permute-start(f32[40,1024]{1,0:T(8,128)S(1)} %get-tuple-element.52), channel_id=1, source_target_pairs={{0,24},{8,16},{16,8},{24,0},{1,25},{9,17},{17,9},{25,1},{2,26},{10... | collective-permute-start | bytes 491528 | tf_op jit(solution)/shard_map/ppermute | solution.py:192
  47.7 11.3 %collective-permute-start.11 = (f32[40,1024]{1,0:T(8,128)S(1)}, f32[40,1024]{1,0:T(8,128)S(1)}, u32[]{:S(2)}, u32[]{:S(2)}) collective-permute-start(f32[40,1024]{1,0:T(8,128)S(1)} %get-tuple-element.49), channel_id=1, source_target_pairs={{0,8},{8,0},{16,24},{24,16},{1,9},{9,1},{17,25},{25,17},{2,10},{10... | collective-permute-start | bytes 491528 | tf_op jit(solution)/shard_map/ppermute | solution.py:192
  49.1 19.6 %collective-permute-start.9 = (f32[40,1024]{1,0:T(8,128)S(1)}, f32[40,1024]{1,0:T(8,128)S(1)}, u32[]{:S(2)}, u32[]{:S(2)}) collective-permute-start(f32[40,1024]{1,0:T(8,128)S(1)} %get-tuple-element.46), channel_id=1, source_target_pairs={{0,16},{8,24},{16,0},{24,8},{1,17},{9,25},{17,1},{25,9},{2,18},{10... | collective-permute-start | bytes 491528 | tf_op jit(solution)/shard_map/ppermute | solution.py:192
  51.8 16.9 %collective-permute-start.10 = (f32[40,1024]{1,0:T(8,128)S(1)}, f32[40,1024]{1,0:T(8,128)S(1)}, u32[]{:S(2)}, u32[]{:S(2)}) collective-permute-start(f32[40,1024]{1,0:T(8,128)S(1)} %get-tuple-element.47), channel_id=1, source_target_pairs={{0,24},{8,16},{16,8},{24,0},{1,25},{9,17},{17,9},{25,1},{2,26},{10... | collective-permute-start | bytes 491528 | tf_op jit(solution)/shard_map/ppermute | solution.py:192

commit v7 on v6

--- a/solution.py
+++ b/solution.py
@@ -203,7 +203,7 @@
         )(state, *after)
 
     def update_matrices(slab):
-        hop = 1
+        hop = 2
         while True:
             other = swap(slab, "grid", hop)
             hop *= 2
@@ -253,6 +253,7 @@
         [VMEM] * n_mem,
         VMEM,
     )(*seen)
+    slab = slab + swap(slab, "grid", 1)
     matrices = lax.cond(jnp.any(loc_mask > 0), update_matrices, no_updates, slab)
     result = []
     for group in ((0,), (1,)):

time: 69.9 us -> 69.9 us (level)
  transfers between devices with their start and end apart: 16 -> 16, of which waited for: 9 -> 8; matrix products, arithmetic and copies ran while one was open for 1% -> 1% of each run, Pallas kernels for 13% -> 13%
where the time goes in v7:
time: 69.9 us; the launch traced here: 69.5 us
  waiting for transfers between devices  28.2 us (40%)
  starting transfers between devices  27.7 us (40%)
  Pallas kernels  10.7 us (15%)
  local copies, waits for them, and re-layouts  1.43 us (2%)
  between operations  0.81 us (1%)
    ppermute x16, waiting for transfers between devices, swap(): lax.ppermute(value, axis, [(j, j ^ by) for j in range(lax.axis_size(axis))])  28.2 us
    ppermute x16, starting transfers between devices, swap(): lax.ppermute(value, axis, [(j, j ^ by) for j in range(lax.axis_size(axis))])  27.7 us
    pallas_call x1, Pallas kernels, update_matrices(): kernel_call(functools.partial(chain_kernel, places), 'chain', jax.ShapeDt...  3.51 us
    pallas_call x4, Pallas kernels, on_device(): kernel_call(functools.partial(unpack_kernel, parts, quarter, [chunk[:2] f...  3.13 us
    pallas_call x2, Pallas kernels, on_device(): kernel_call(functools.partial(apply_kernel, n_mem, parts, quarter, chunks...  3.03 us
    unnamed x14, local copies, waits for them, and re-layouts  1.43 us
  transfers between devices with their start and end apart: 16, of which 8 were waited for; matrix products, arithmetic and copies ran while one was open for 1% of the time, Pallas kernels for 13%

profile of v7, /device:TPU:0, one launch (start us, length us, event | category | flops | bytes accessed | tf_op | source)
XLA Modules:
  0.0 69.5 jit_solution(13378304574616266016)
XLA Ops:
  0.0 1.4 %copy-done = f32[20,16384]{1,0:T(8,128)S(1)} copy-done((f32[20,16384]{1,0:T(8,128)S(1)}, f32[20,16384]{1,0:T(8,128)}, u32[]{:S(2)}) %copy-start) | copy-done | bytes 1310744
  1.4 0.9 %seen.1.refs_0_ = f32[80,128]{1,0:T(8,128)S(1)} custom-call(s32[4]{0:T(128)} %tile_ref.1, s32[4]{0:T(128)} %order_ref.5, f32[20,16384]{1,0:T(8,128)S(1)} %copy-done), custom_call_target="tpu_custom_call" | custom-call | tf_op jit(solution)/shard_map/seen/pallas_call | solution.py:225
  2.3 5.1 %collective-permute-start.4 = (f32[80,128]{1,0:T(8,128)S(1)}, f32[80,128]{1,0:T(8,128)S(1)}, u32[]{:S(2)}, u32[]{:S(2)}) collective-permute-start(f32[80,128]{1,0:T(8,128)S(1)} %seen.1.refs_0_), channel_id=1, source_target_pairs={{0,24},{8,16},{16,8},{24,0},{1,25},{9,17},{17,9},{25,1},{2,26},{10... | collective-permute-start | bytes 122888 | tf_op jit(solution)/shard_map/ppermute | solution.py:192
  7.4 0.6 collective-permute-start.2
  8.1 1.4 %collective-permute-done.4.refs_3_ = f32[80,128]{1,0:T(8,128)S(1)} collective-permute-done((f32[80,128]{1,0:T(8,128)S(1)}, f32[80,128]{1,0:T(8,128)S(1)}, u32[]{:S(2)}, u32[]{:S(2)}) %collective-permute-start.4) | collective-permute-done | bytes 40992 | tf_op jit(solution)/shard_map/ppermute | solution.py:192
  9.4 2.9 %collective-permute-done.3.refs_2_ = f32[80,128]{1,0:T(8,128)S(1)} collective-permute-done((f32[80,128]{1,0:T(8,128)S(1)}, f32[80,128]{1,0:T(8,128)S(1)}, u32[]{:S(2)}, u32[]{:S(2)}) %collective-permute-start.3) | collective-permute-done | bytes 40992 | tf_op jit(solution)/shard_map/ppermute | solution.py:192
  12.7 2.0 %collective-permute-start.7 = (f32[40,2048]{1,0:T(8,128)S(1)}, f32[40,2048]{1,0:T(8,128)S(1)}, u32[]{:S(2)}, u32[]{:S(2)}) collective-permute-start(f32[40,2048]{1,0:T(8,128)S(1)} %get-tuple-element.48), channel_id=1, source_target_pairs={{0,16},{8,24},{16,0},{24,8},{1,17},{9,25},{17,1},{25,9},{2,18},{10... | collective-permute-start | bytes 983048 | tf_op jit(solution)/shard_map/ppermute | solution.py:192
  14.7 2.3 %collective-permute-start.12 = (f32[40,1024]{1,0:T(8,128)S(1)}, f32[40,1024]{1,0:T(8,128)S(1)}, u32[]{:S(2)}, u32[]{:S(2)}) collective-permute-start(f32[40,1024]{1,0:T(8,128)S(1)} %get-tuple-element.54), channel_id=1, source_target_pairs={{0,24},{8,16},{16,8},{24,0},{1,25},{9,17},{17,9},{25,1},{2,26},{10... | collective-permute-start | bytes 491528 | tf_op jit(solution)/shard_map/ppermute | solution.py:192
  17.1 0.6 compare_reduce_fusion
  18.4 1.6 %collective-permute-start.8 = (f32[40,1024]{1,0:T(8,128)S(1)}, f32[40,1024]{1,0:T(8,128)S(1)}, u32[]{:S(2)}, u32[]{:S(2)}) collective-permute-start(f32[40,1024]{1,0:T(8,128)S(1)} %get-tuple-element.49), channel_id=1, source_target_pairs={{0,24},{8,16},{16,8},{24,0},{1,25},{9,17},{17,9},{25,1},{2,26},{10... | collective-permute-start | bytes 491528 | tf_op jit(solution)/shard_map/ppermute | solution.py:192
  20.0 15.0 %conditional.1 = (f32[80,2048]{1,0:T(8,128)S(1)}) conditional(s32[]{:T(128)} %convert_element_type.10, () %tuple.11, (f32[320,128]{1,0:T(8,128)S(1)}, f32[320,128]{1,0:T(8,128)S(1)}, s32[4]{0:T(128)S(1)}, s32[4]{0:T(128)S(1)}, s32[4,1024]{1,0:T(4,128)S(1)}, /*index=5*/s32[4,256]{1,0:T(4,128)S(1)}, f32[4,256]{1,0:T(4,128)S(1)}, ...), branch_computations={%region_1.0_spmd, %region_2.0_spmd} | conditional | flops 81920 | bytes 2293848 | solution.py:257
  20.1 1.6 %collective-permute-start = (f32[320,128]{1,0:T(8,128)S(1)}, f32[320,128]{1,0:T(8,128)S(1)}, u32[]{:S(2)}, u32[]{:S(2)}) collective-permute-start(f32[320,128]{1,0:T(8,128)S(1)} %add.5), channel_id=1, source_target_pairs={{0,2},{1,3},{2,0},{3,1},{4,6},{5,7},{6,4},{7,5},{8,10},{9,11},{10,... | collective-permute-start | bytes 491528 | tf_op jit(solution)/shard_map/cond/branch_1_fun/ppermute | solution.py:192
  21.6 4.5 %collective-permute-done = f32[320,128]{1,0:T(8,128)S(1)} collective-permute-done((f32[320,128]{1,0:T(8,128)S(1)}, f32[320,128]{1,0:T(8,128)S(1)}, u32[]{:S(2)}, u32[]{:S(2)}) %collective-permute-start) | collective-permute-done | bytes 163872 | tf_op jit(solution)/shard_map/cond/branch_1_fun/ppermute | solution.py:192
  26.2 1.6 %collective-permute-start.1 = (f32[320,128]{1,0:T(8,128)S(1)}, f32[320,128]{1,0:T(8,128)S(1)}, u32[]{:S(2)}, u32[]{:S(2)}) collective-permute-start(f32[320,128]{1,0:T(8,128)S(1)} %add.6.one_ref), channel_id=1, source_target_pairs={{0,4},{1,5},{2,6},{3,7},{4,0},{5,1},{6,2},{7,3},{8,12},{9,13},{10,... | collective-permute-start | bytes 491528 | tf_op jit(solution)/shard_map/cond/branch_1_fun/ppermute | solution.py:192
  27.8 3.8 %collective-permute-done.1.two_ref = f32[320,128]{1,0:T(8,128)S(1)} collective-permute-done((f32[320,128]{1,0:T(8,128)S(1)}, f32[320,128]{1,0:T(8,128)S(1)}, u32[]{:S(2)}, u32[]{:S(2)}) %collective-permute-start.1) | collective-permute-done | bytes 163872 | tf_op jit(solution)/shard_map/cond/branch_1_fun/ppermute | solution.py:192
  31.6 3.5 %chain.1 = f32[80,2048]{1,0:T(8,128)S(1)} custom-call(s32[4]{0:T(128)S(1)} %get-tuple-element.25.tile_ref, s32[4]{0:T(128)S(1)} %get-tuple-element.26.order_ref, s32[4,1024]{1,0:T(4,128)S(1)} %get-tuple-element.27.mask_ref, s32[4,256]{1,0:T(4,128)S(1)} %get-tuple-element.62.offset_ref, f32[4,256]{1,0:T(4,128)S(1)} %get-tuple-element.63.value_ref, ...), custom_call_target="tpu_custom_call" | custom-call | tf_op jit(solution)/shard_map/cond/branch_1_fun/chain/pallas_call | solution.py:213
  35.1 2.9 %collective-permute-done.7.refs_2_ = f32[40,2048]{1,0:T(8,128)S(1)} collective-permute-done((f32[40,2048]{1,0:T(8,128)S(1)}, f32[40,2048]{1,0:T(8,128)S(1)}, u32[]{:S(2)}, u32[]{:S(2)}) %collective-permute-start.7) | collective-permute-done | bytes 327712 | tf_op jit(solution)/shard_map/ppermute | solution.py:192
  38.0 1.5 %apply.3 = (f32[40,1024]{1,0:T(8,128)S(1)}, f32[40,1024]{1,0:T(8,128)S(1)}, f32[40,1024]{1,0:T(8,128)S(1)}, f32[40,1024]{1,0:T(8,128)S(1)}) custom-call(s32[4]{0:T(128)S(1)} %copy-done.2, s32[4,1024]{1,0:T(4,128)S(1)} %copy-done.1, f32[80,2048]{1,0:T(8,128)S(1)} %get-tuple-element.65.t_ref, f32[40,2048]{1,0:T(8,128)S(1)} %get-tuple-element.46.refs_0_, ...), custom_call_target="tpu_custom_call" | custom-call | tf_op jit(solution)/shard_map/apply/pallas_call | solution.py:269
  39.5 3.5 %collective-permute-start.15 = (f32[40,1024]{1,0:T(8,128)S(1)}, f32[40,1024]{1,0:T(8,128)S(1)}, u32[]{:S(2)}, u32[]{:S(2)}) collective-permute-start(f32[40,1024]{1,0:T(8,128)S(1)} %get-tuple-element.58), channel_id=1, source_target_pairs={{0,8},{8,0},{16,24},{24,16},{1,9},{9,1},{17,25},{25,17},{2,10},{10... | collective-permute-start | bytes 491528 | tf_op jit(solution)/shard_map/ppermute | solution.py:192
  43.1 1.7 %collective-permute-start.13 = (f32[40,1024]{1,0:T(8,128)S(1)}, f32[40,1024]{1,0:T(8,128)S(1)}, u32[]{:S(2)}, u32[]{:S(2)}) collective-permute-start(f32[40,1024]{1,0:T(8,128)S(1)} %get-tuple-element.55), channel_id=1, source_target_pairs={{0,16},{8,24},{16,0},{24,8},{1,17},{9,25},{17,1},{25,9},{2,18},{10... | collective-permute-start | bytes 491528 | tf_op jit(solution)/shard_map/ppermute | solution.py:192
  44.8 1.4 %collective-permute-start.14 = (f32[40,1024]{1,0:T(8,128)S(1)}, f32[40,1024]{1,0:T(8,128)S(1)}, u32[]{:S(2)}, u32[]{:S(2)}) collective-permute-start(f32[40,1024]{1,0:T(8,128)S(1)} %get-tuple-element.56), channel_id=1, source_target_pairs={{0,24},{8,16},{16,8},{24,0},{1,25},{9,17},{17,9},{25,1},{2,26},{10... | collective-permute-start | bytes 491528 | tf_op jit(solution)/shard_map/ppermute | solution.py:192
  46.2 1.5 %apply.2 = (f32[40,1024]{1,0:T(8,128)S(1)}, f32[40,1024]{1,0:T(8,128)S(1)}, f32[40,1024]{1,0:T(8,128)S(1)}, f32[40,1024]{1,0:T(8,128)S(1)}) custom-call(s32[4]{0:T(128)S(1)} %copy-done.2, s32[4,1024]{1,0:T(4,128)S(1)} %copy-done.1, f32[80,2048]{1,0:T(8,128)S(1)} %get-tuple-element.65.t_ref, f32[40,2048]{1,0:T(8,128)S(1)} %get-tuple-element.46.refs_0_, ...), custom_call_target="tpu_custom_call" | custom-call | tf_op jit(solution)/shard_map/apply/pallas_call | solution.py:269
  47.7 1.4 %collective-permute-start.11 = (f32[40,1024]{1,0:T(8,128)S(1)}, f32[40,1024]{1,0:T(8,128)S(1)}, u32[]{:S(2)}, u32[]{:S(2)}) collective-permute-start(f32[40,1024]{1,0:T(8,128)S(1)} %get-tuple-element.53), channel_id=1, source_target_pairs={{0,8},{8,0},{16,24},{24,16},{1,9},{9,1},{17,25},{25,17},{2,10},{10... | collective-permute-start | bytes 491528 | tf_op jit(solution)/shard_map/ppermute | solution.py:192
  49.1 2.0 %collective-permute-start.9 = (f32[40,1024]{1,0:T(8,128)S(1)}, f32[40,1024]{1,0:T(8,128)S(1)}, u32[]{:S(2)}, u32[]{:S(2)}) collective-permute-start(f32[40,1024]{1,0:T(8,128)S(1)} %get-tuple-element.50), channel_id=1, source_target_pairs={{0,16},{8,24},{16,0},{24,8},{1,17},{9,25},{17,1},{25,9},{2,18},{10... | collective-permute-start | bytes 491528 | tf_op jit(solution)/shard_map/ppermute | solution.py:192
  51.1 0.7 %collective-permute-done.15.refs_1_ = f32[40,1024]{1,0:T(8,128)S(1)} collective-permute-done((f32[40,1024]{1,0:T(8,128)S(1)}, f32[40,1024]{1,0:T(8,128)S(1)}, u32[]{:S(2)}, u32[]{:S(2)}) %collective-permute-start.15) | collective-permute-done | bytes 163872 | tf_op jit(solution)/shard_map/ppermute | solution.py:192
  51.8 2.5 %collective-permute-start.10 = (f32[40,1024]{1,0:T(8,128)S(1)}, f32[40,1024]{1,0:T(8,128)S(1)}, u32[]{:S(2)}, u32[]{:S(2)}) collective-permute-start(f32[40,1024]{1,0:T(8,128)S(1)} %get-tuple-element.51), channel_id=1, source_target_pairs={{0,24},{8,16},{16,8},{24,0},{1,25},{9,17},{17,9},{25,1},{2,26},{10... | collective-permute-start | bytes 491528 | tf_op jit(solution)/shard_map/ppermute | solution.py:192
  54.4 0.8 %unpack.4.refs_2_ = f32[20,16384]{1,0:T(8,128)} custom-call(f32[40,1024]{1,0:T(8,128)S(1)} %get-tuple-element.57.refs_0_, f32[40,1024]{1,0:T(8,128)S(1)} %collective-permute-done.15.refs_1_), custom_call_target="tpu_custom_call" | custom-call | tf_op jit(solution)/shard_map/unpack/pallas_call | solution.py:278
  55.1 3.0 %collective-permute-done.13.refs_0_ = f32[40,1024]{1,0:T(8,128)S(1)} collective-permute-done((f32[40,1024]{1,0:T(8,128)S(1)}, f32[40,1024]{1,0:T(8,128)S(1)}, u32[]{:S(2)}, u32[]{:S(2)}) %collective-permute-start.13) | collective-permute-done | bytes 163872 | tf_op jit(solution)/shard_map/ppermute | solution.py:192
  58.2 0.8 %unpack.5.refs_2_ = f32[20,16384]{1,0:T(8,128)} custom-call(f32[40,1024]{1,0:T(8,128)S(1)} %collective-permute-done.13.refs_0_, f32[40,1024]{1,0:T(8,128)S(1)} %collective-permute-done.14.refs_1_, f32[20,16384]{1,0:T(8,128)} %unpack.4.refs_2_), custom_call_target="tpu_custom_call", output_to_operand_aliasing={{}: (2, {})} | custom-call | tf_op jit(solution)/shard_map/unpack/pallas_call | solution.py:278
  59.0 0.8 %unpack.6.refs_2_ = f32[20,16384]{1,0:T(8,128)} custom-call(f32[40,1024]{1,0:T(8,128)S(1)} %get-tuple-element.52.refs_0_, f32[40,1024]{1,0:T(8,128)S(1)} %collective-permute-done.11.refs_1_, f32[20,16384]{1,0:T(8,128)} %unpack.5.refs_2_), custom_call_target="tpu_custom_call", output_to_operand_aliasing={{}: (2, {})} | custom-call | tf_op jit(solution)/shard_map/unpack/pallas_call | solution.py:278
  59.7 8.9 %collective-permute-done.9.refs_0_ = f32[40,1024]{1,0:T(8,128)S(1)} collective-permute-done((f32[40,1024]{1,0:T(8,128)S(1)}, f32[40,1024]{1,0:T(8,128)S(1)}, u32[]{:S(2)}, u32[]{:S(2)}) %collective-permute-start.9) | collective-permute-done | bytes 163872 | tf_op jit(solution)/shard_map/ppermute | solution.py:192
  68.7 0.8 %unpack.7 = f32[20,16384]{1,0:T(8,128)} custom-call(f32[40,1024]{1,0:T(8,128)S(1)} %collective-permute-done.9.refs_0_, f32[40,1024]{1,0:T(8,128)S(1)} %collective-permute-done.10.refs_1_, f32[20,16384]{1,0:T(8,128)} %unpack.6.refs_2_), custom_call_target="tpu_custom_call", output_to_operand_aliasing={{}: (2, {})} | custom-call | tf_op jit(solution)/shard_map/unpack/pallas_call | solution.py:278
  (28 shorter events, 0.5 us)
Async XLA Ops:
  0.0 1.4 %copy-start = (f32[20,16384]{1,0:T(8,128)S(1)}, f32[20,16384]{1,0:T(8,128)}, u32[]{:S(2)}) copy-start(f32[20,16384]{1,0:T(8,128)} %x_ref.3) | copy-start | bytes 3932164
  1.4 15.7 %copy-start.1 = (s32[4,1024]{1,0:T(4,128)S(1)}, s32[4,1024]{1,0:T(4,128)}, u32[]{:S(2)}) copy-start(s32[4,1024]{1,0:T(4,128)} %mask_ref.3) | copy-start | bytes 49156
  1.4 18.6 %copy-start.2 = (s32[4]{0:T(128)S(1)}, s32[4]{0:T(128)}, u32[]{:S(2)}) copy-start(s32[4]{0:T(128)} %order_ref.5) | copy-start | bytes 52
  1.4 18.6 %copy-start.3 = (s32[4,256]{1,0:T(4,128)S(1)}, s32[4,256]{1,0:T(4,128)}, u32[]{:S(2)}) copy-start(s32[4,256]{1,0:T(4,128)} %param.11) | copy-start | bytes 12292
  1.4 18.6 %copy-start.4 = (f32[4,256]{1,0:T(4,128)S(1)}, f32[4,256]{1,0:T(4,128)}, u32[]{:S(2)}) copy-start(f32[4,256]{1,0:T(4,128)} %param.12) | copy-start | bytes 12292
  1.4 18.6 %copy-start.5 = (f32[4,256]{1,0:T(4,128)S(1)}, f32[4,256]{1,0:T(4,128)}, u32[]{:S(2)}) copy-start(f32[4,256]{1,0:T(4,128)} %param.13) | copy-start | bytes 12292
  1.4 18.6 %copy-start.6 = (s32[4]{0:T(128)S(1)}, s32[4]{0:T(128)}, u32[]{:S(2)}) copy-start(s32[4]{0:T(128)} %tile_ref.1) | copy-start | bytes 52
  2.3 7.1 %collective-permute-start.4 = (f32[80,128]{1,0:T(8,128)S(1)}, f32[80,128]{1,0:T(8,128)S(1)}, u32[]{:S(2)}, u32[]{:S(2)}) collective-permute-start(f32[80,128]{1,0:T(8,128)S(1)} %seen.1.refs_0_), channel_id=1, source_target_pairs={{0,24},{8,16},{16,8},{24,0},{1,25},{9,17},{17,9},{25,1},{2,26},{10... | collective-permute-start | bytes 122888 | tf_op jit(solution)/shard_map/ppermute | solution.py:192
  7.4 4.9 %collective-permute-start.3 = (f32[80,128]{1,0:T(8,128)S(1)}, f32[80,128]{1,0:T(8,128)S(1)}, u32[]{:S(2)}, u32[]{:S(2)}) collective-permute-start(f32[80,128]{1,0:T(8,128)S(1)} %seen.1.refs_0_), channel_id=1, source_target_pairs={{0,16},{8,24},{16,0},{24,8},{1,17},{9,25},{17,1},{25,9},{2,18},{10... | collective-permute-start | bytes 122888 | tf_op jit(solution)/shard_map/ppermute | solution.py:192
  7.4 4.9 %collective-permute-start.2 = (f32[80,128]{1,0:T(8,128)S(1)}, f32[80,128]{1,0:T(8,128)S(1)}, u32[]{:S(2)}, u32[]{:S(2)}) collective-permute-start(f32[80,128]{1,0:T(8,128)S(1)} %seen.1.refs_0_), channel_id=1, source_target_pairs={{0,8},{8,0},{16,24},{24,16},{1,9},{9,1},{17,25},{25,17},{2,10},{10... | collective-permute-start | bytes 122888 | tf_op jit(solution)/shard_map/ppermute | solution.py:192
  12.4 22.6 %collective-permute-start.6 = (f32[40,2048]{1,0:T(8,128)S(1)}, f32[40,2048]{1,0:T(8,128)S(1)}, u32[]{:S(2)}, u32[]{:S(2)}) collective-permute-start(f32[40,2048]{1,0:T(8,128)S(1)} %get-tuple-element.47), channel_id=1, source_target_pairs={{0,8},{8,0},{16,24},{24,16},{1,9},{9,1},{17,25},{25,17},{2,10},{10... | collective-permute-start | bytes 983048 | tf_op jit(solution)/shard_map/ppermute | solution.py:192
  12.7 25.3 %collective-permute-start.7 = (f32[40,2048]{1,0:T(8,128)S(1)}, f32[40,2048]{1,0:T(8,128)S(1)}, u32[]{:S(2)}, u32[]{:S(2)}) collective-permute-start(f32[40,2048]{1,0:T(8,128)S(1)} %get-tuple-element.48), channel_id=1, source_target_pairs={{0,16},{8,24},{16,0},{24,8},{1,17},{9,25},{17,1},{25,9},{2,18},{10... | collective-permute-start | bytes 983048 | tf_op jit(solution)/shard_map/ppermute | solution.py:192
  14.7 5.3 %collective-permute-start.5 = (f32[320,128]{1,0:T(8,128)S(1)}, f32[320,128]{1,0:T(8,128)S(1)}, u32[]{:S(2)}, u32[]{:S(2)}) collective-permute-start(f32[320,128]{1,0:T(8,128)S(1)} %join.1), channel_id=1, source_target_pairs={{0,1},{1,0},{2,3},{3,2},{4,5},{5,4},{6,7},{7,6},{8,9},{9,8},{10,11... | collective-permute-start | bytes 491528 | tf_op jit(solution)/shard_map/ppermute | solution.py:192
  14.7 20.3 %collective-permute-start.12 = (f32[40,1024]{1,0:T(8,128)S(1)}, f32[40,1024]{1,0:T(8,128)S(1)}, u32[]{:S(2)}, u32[]{:S(2)}) collective-permute-start(f32[40,1024]{1,0:T(8,128)S(1)} %get-tuple-element.54), channel_id=1, source_target_pairs={{0,24},{8,16},{16,8},{24,0},{1,25},{9,17},{17,9},{25,1},{2,26},{10... | collective-permute-start | bytes 491528 | tf_op jit(solution)/shard_map/ppermute | solution.py:192
  18.4 27.8 %collective-permute-start.8 = (f32[40,1024]{1,0:T(8,128)S(1)}, f32[40,1024]{1,0:T(8,128)S(1)}, u32[]{:S(2)}, u32[]{:S(2)}) collective-permute-start(f32[40,1024]{1,0:T(8,128)S(1)} %get-tuple-element.49), channel_id=1, source_target_pairs={{0,24},{8,16},{16,8},{24,0},{1,25},{9,17},{17,9},{25,1},{2,26},{10... | collective-permute-start | bytes 491528 | tf_op jit(solution)/shard_map/ppermute | solution.py:192
  20.1 6.1 %collective-permute-start = (f32[320,128]{1,0:T(8,128)S(1)}, f32[320,128]{1,0:T(8,128)S(1)}, u32[]{:S(2)}, u32[]{:S(2)}) collective-permute-start(f32[320,128]{1,0:T(8,128)S(1)} %add.5), channel_id=1, source_target_pairs={{0,2},{1,3},{2,0},{3,1},{4,6},{5,7},{6,4},{7,5},{8,10},{9,11},{10,... | collective-permute-start | bytes 491528 | tf_op jit(solution)/shard_map/cond/branch_1_fun/ppermute | solution.py:192
  26.2 5.4 %collective-permute-start.1 = (f32[320,128]{1,0:T(8,128)S(1)}, f32[320,128]{1,0:T(8,128)S(1)}, u32[]{:S(2)}, u32[]{:S(2)}) collective-permute-start(f32[320,128]{1,0:T(8,128)S(1)} %add.6.one_ref), channel_id=1, source_target_pairs={{0,4},{1,5},{2,6},{3,7},{4,0},{5,1},{6,2},{7,3},{8,12},{9,13},{10,... | collective-permute-start | bytes 491528 | tf_op jit(solution)/shard_map/cond/branch_1_fun/ppermute | solution.py:192
  39.5 12.3 %collective-permute-start.15 = (f32[40,1024]{1,0:T(8,128)S(1)}, f32[40,1024]{1,0:T(8,128)S(1)}, u32[]{:S(2)}, u32[]{:S(2)}) collective-permute-start(f32[40,1024]{1,0:T(8,128)S(1)} %get-tuple-element.58), channel_id=1, source_target_pairs={{0,8},{8,0},{16,24},{24,16},{1,9},{9,1},{17,25},{25,17},{2,10},{10... | collective-permute-start | bytes 491528 | tf_op jit(solution)/shard_map/ppermute | solution.py:192
  43.1 15.1 %collective-permute-start.13 = (f32[40,1024]{1,0:T(8,128)S(1)}, f32[40,1024]{1,0:T(8,128)S(1)}, u32[]{:S(2)}, u32[]{:S(2)}) collective-permute-start(f32[40,1024]{1,0:T(8,128)S(1)} %get-tuple-element.55), channel_id=1, source_target_pairs={{0,16},{8,24},{16,0},{24,8},{1,17},{9,25},{17,1},{25,9},{2,18},{10... | collective-permute-start | bytes 491528 | tf_op jit(solution)/shard_map/ppermute | solution.py:192
  44.8 13.3 %collective-permute-start.14 = (f32[40,1024]{1,0:T(8,128)S(1)}, f32[40,1024]{1,0:T(8,128)S(1)}, u32[]{:S(2)}, u32[]{:S(2)}) collective-permute-start(f32[40,1024]{1,0:T(8,128)S(1)} %get-tuple-element.56), channel_id=1, source_target_pairs={{0,24},{8,16},{16,8},{24,0},{1,25},{9,17},{17,9},{25,1},{2,26},{10... | collective-permute-start | bytes 491528 | tf_op jit(solution)/shard_map/ppermute | solution.py:192
  47.7 11.2 %collective-permute-start.11 = (f32[40,1024]{1,0:T(8,128)S(1)}, f32[40,1024]{1,0:T(8,128)S(1)}, u32[]{:S(2)}, u32[]{:S(2)}) collective-permute-start(f32[40,1024]{1,0:T(8,128)S(1)} %get-tuple-element.53), channel_id=1, source_target_pairs={{0,8},{8,0},{16,24},{24,16},{1,9},{9,1},{17,25},{25,17},{2,10},{10... | collective-permute-start | bytes 491528 | tf_op jit(solution)/shard_map/ppermute | solution.py:192
  49.1 19.6 %collective-permute-start.9 = (f32[40,1024]{1,0:T(8,128)S(1)}, f32[40,1024]{1,0:T(8,128)S(1)}, u32[]{:S(2)}, u32[]{:S(2)}) collective-permute-start(f32[40,1024]{1,0:T(8,128)S(1)} %get-tuple-element.50), channel_id=1, source_target_pairs={{0,16},{8,24},{16,0},{24,8},{1,17},{9,25},{17,1},{25,9},{2,18},{10... | collective-permute-start | bytes 491528 | tf_op jit(solution)/shard_map/ppermute | solution.py:192
  51.8 16.9 %collective-permute-start.10 = (f32[40,1024]{1,0:T(8,128)S(1)}, f32[40,1024]{1,0:T(8,128)S(1)}, u32[]{:S(2)}, u32[]{:S(2)}) collective-permute-start(f32[40,1024]{1,0:T(8,128)S(1)} %get-tuple-element.51), channel_id=1, source_target_pairs={{0,24},{8,16},{16,8},{24,0},{1,25},{9,17},{17,9},{25,1},{2,26},{10... | collective-permute-start | bytes 491528 | tf_op jit(solution)/shard_map/ppermute | solution.py:192
